TPU v7x, 256 devices: a whole 4x4x8 slice. The times are simulated.
256 devices in a mesh: rows: 64 (over z, x, core), sub: 4 (over y).
Axes of the slice: x: 4, y: 4, z: 8, core: 2. Of those that a mesh axis runs over, the one named last changes fastest.
Arguments:
- points: bfloat16 [262144, 256], P(('rows', 'sub')), may hold values from -1.5 to 1.5
- init_dist: float32 [262144], P(('rows', 'sub')), may hold values from 0.5 to 6
- picks: int32 [3, 4096], P(None, ('rows', 'sub')), may hold values from 0 to 1023, as said below
- pick_counts: int32 [3, 256], P(None, ('rows', 'sub')), may hold values from 1 to 16, as said below
Outputs:
- min_dist: float32 [262144], P(('rows', 'sub'))
- normalized: float32 [262144], P(('rows', 'sub'))
- round_costs: float32 [3], replicated
Inputs may be any that keep to these rules, and one draw needn't show every extreme that they name: `picks`: local row numbers of the picking device; slots past that device's count hold arbitrary row numbers. `pick_counts`: in every round some device has exactly 16 live slots.
All inputs are finite; a program needn't handle non-finite values.
Results may differ from a plain program's by a relative error of at most 0.0003.
Values may be sent and summed in bfloat16 or wider, within the bound.
No kernel may reach another device: no remote copies, remote signals or barrier semaphores. Data moves between devices by JAX's collectives and lax.ppermute only.
A program may use at most 64 MiB of HBM per device.

v0:
```python
import jax
import jax.numpy as jnp
from jax import lax
from jax.sharding import PartitionSpec as P


def piece_minimum(points, row_sq, piece, live_rows):
    inner = jnp.dot(points, piece.T, preferred_element_type=jnp.float32)
    cand_sq = jnp.sum(jnp.square(piece.astype(jnp.float32)), axis=1)
    cand_sq = jnp.where(live_rows, cand_sq, jnp.inf)
    dist = jnp.maximum(row_sq[:, None] + cand_sq[None, :] - 2.0 * inner, 0.0)
    return jnp.min(dist, axis=1)


def live_slots(count_row, length, most):
    limits = jnp.repeat(count_row, most, total_repeat_length=length)
    slot_no = jnp.arange(length, dtype=jnp.int32) % most
    return slot_no < limits


def shards(points, init_dist, picks, pick_counts):
    most = picks.shape[1]
    rounds = picks.shape[0]
    row_sq = jnp.sum(jnp.square(points.astype(jnp.float32)), axis=1)
    count_table = lax.all_gather(pick_counts, ("rows", "sub"), axis=1, tiled=True)
    current = init_dist
    partials = []
    for step in range(rounds):
        cand = points[picks[step]]

        def fold_round(carry, piece, start, step=step):
            live_rows = live_slots(count_table[step], piece.shape[0], most)
            return jnp.minimum(carry, piece_minimum(points, row_sq, piece, live_rows))

        current = fold_round(
            current, lax.all_gather(cand, ("rows", "sub"), axis=0, tiled=True), jnp.int32(0)
        )
        partials.append(jnp.sum(current))
    round_costs = jnp.stack(
        [lax.psum(partial_value, ("rows", "sub")) for partial_value in partials]
    )
    total_rows = float(points.shape[0] * lax.axis_size(("rows", "sub")))
    normalized = current * total_rows / round_costs[rounds - 1]
    return (current, normalized, round_costs)


def solution(mesh):
    placed = (
        P(("rows", "sub"), None),
        P(("rows", "sub")),
        P(None, ("rows", "sub")),
        P(None, ("rows", "sub")),
    )
    return jax.shard_map(
        shards,
        mesh=mesh,
        in_specs=placed,
        out_specs=(P(("rows", "sub")), P(("rows", "sub")), P()),
        check_vma=False,
    )
```

profile of v0, /device:TPU:1, one launch (start us, length us, event | category | flops | bytes accessed | tf_op | source)
XLA Modules:
  0.0 433.3 jit_solution(7852477465553086536)
XLA Ops:
  7.2 0.8 fusion.16
  8.0 2.3 gather_fusion
  10.3 0.0 all-gather.10.cloned.1.call-start
  10.4 2.3 gather_fusion.1
  12.7 0.0 all-gather.12.cloned.1.call-start
  12.8 2.3 gather_fusion.2
  15.1 0.8 broadcast_add_fusion
  15.8 2.3 scatter_custom_fusion
  18.2 0.3 reduce-window.14
  18.5 0.1 slice.75
  18.5 0.1 reduce-window.15
  18.6 58.7 %all-gather.3 = s32[256,1,3]{2,1,0:T(1,128)S(1)} all-gather(s32[1,1,3]{2,1,0:T(1,128)} %bitcast.57), channel_id=1, replica_groups=mesh['rows'=64,'sub'=4] {'rows','sub'}, dimensions={0}, use_global_device_ids=true | all-gather | bytes 3084 | tf_op jit(solution)/shard_map/all_gather | solution.py:25
  77.2 0.1 slice_reduce_fusion.3
  77.4 0.3 slice_reduce_fusion.2
  77.6 0.1 fusion.12
  77.7 25.7 %gather_fusion.3 = s32[4096]{0:T(1024)S(1)} fusion(s32[256]{0:T(256)S(1)} %get-tuple-element.32, s32[4096]{0:T(1024)S(1)} %fusion.12), kind=kCustom, calls=%fused_computation.clone | custom fusion | bytes 49152 | tf_op jit(solution)/shard_map/jit(_take)/gather | solution.py:16
  103.5 25.7 %gather_fusion.4 = s32[4096]{0:T(1024)S(1)} fusion(s32[256]{0:T(256)S(1)} %get-tuple-element.34, s32[4096]{0:T(1024)S(1)} %fusion.12), kind=kCustom, calls=%fused_computation.1.clone | custom fusion | bytes 49152 | tf_op jit(solution)/shard_map/jit(_take)/gather | solution.py:16
  129.2 25.7 %gather_fusion.5 = s32[4096]{0:T(1024)S(1)} fusion(s32[256]{0:T(256)S(1)} %get-tuple-element.33, s32[4096]{0:T(1024)S(1)} %fusion.12), kind=kCustom, calls=%fused_computation.2.clone | custom fusion | bytes 49152 | tf_op jit(solution)/shard_map/jit(_take)/gather | solution.py:16
  155.0 0.2 multiply_reduce_fusion.3
  155.2 2.2 multiply_reduce_fusion.2
  157.5 0.1 fusion.9
  157.6 69.3 %all-gather.10.cloned.1.call-done = bf16[4096,256]{1,0:T(8,128)(2,1)} async-done(((bf16[16,256]{1,0:T(8,128)(2,1)}), bf16[4096,256]{1,0:T(8,128)(2,1)}) %all-gather.10.cloned.1.call-update) | async-done | bytes 2097168 | tf_op jit(solution)/shard_map/all_gather | solution.py:36
  226.8 2.2 multiply_reduce_fusion.1
  229.1 104.5 %all-gather.12.cloned.1.call-done = bf16[4096,256]{1,0:T(8,128)(2,1)} async-done(((bf16[16,256]{1,0:T(8,128)(2,1)}), bf16[4096,256]{1,0:T(8,128)(2,1)}) %all-gather.12.cloned.1.call-update) | async-done | bytes 2097168 | tf_op jit(solution)/shard_map/all_gather | solution.py:36
  333.6 2.2 multiply_reduce_fusion
  335.9 3.2 fusion.5
  339.1 3.2 fusion.3
  342.3 3.2 fusion.1
  345.6 0.7 minimum_reduce_fusion.1
  346.3 76.9 %all-reduce = (f32[]{:T(128)}, f32[1]{0:T(128)}, f32[1]{0:T(128)}) all-reduce(f32[]{:T(128)} %get-tuple-element.44, f32[1]{0:T(128)} %bitcast.18, f32[1]{0:T(128)} %bitcast.17), channel_id=1, replica_groups=mesh['rows'=64,'sub'=4] {'rows','sub'}, use_global_device_ids=true, to_apply=%region_11.13 | all-reduce | flops 3 | bytes 24 | tf_op jit(solution)/shard_map/psum | solution.py:40
  423.2 1.2 multiply_divide_fusion
  424.3 2.4 pad_maximum_fusion
  (24 shorter events, 0.2 us)
Async XLA Ops:
  7.2 148.1 %all-gather.8.cloned.1.call-start = ((), (), s32[]{:S(2)}) async-start(), calls=%async_computation | async-start | bytes 2105344 | tf_op jit(solution)/shard_map/all_gather | solution.py:36
  10.3 216.5 %all-gather.10.cloned.1.call-start = ((), (), s32[]{:S(2)}) async-start(), calls=%async_computation.1 | async-start | bytes 2105344 | tf_op jit(solution)/shard_map/all_gather | solution.py:36
  12.7 320.9 %all-gather.12.cloned.1.call-start = ((), (), s32[]{:S(2)}) async-start(), calls=%async_computation.2 | async-start | bytes 2105344 | tf_op jit(solution)/shard_map/all_gather | solution.py:36
  129.2 25.8 %copy-start.3 = (bf16[1024,256]{1,0:T(8,128)(2,1)S(1)}, bf16[1024,256]{1,0:T(8,128)(2,1)}, u32[]{:S(2)}) copy-start(bf16[1024,256]{1,0:T(8,128)(2,1)} %param.12) | copy-start | bytes 1572868
  157.5 178.3 %copy-start = (bf16[4096,256]{1,0:T(8,128)(2,1)S(1)}, bf16[4096,256]{1,0:T(8,128)(2,1)}, u32[]{:S(2)}) copy-start(bf16[4096,256]{1,0:T(8,128)(2,1)} %all-gather.8.cloned.1.call-done) | copy-start | bytes 6291460
  335.8 3.2 copy-start.1
  339.0 3.3 copy-start.2
  342.3 3.3 copy-start.5
  346.3 80.5 %copy-start.4 = (f32[1024]{0:T(1024)}, f32[1024]{0:T(1024)S(1)}, u32[]{:S(2)}) copy-start(f32[1024]{0:T(1024)S(1)} %get-tuple-element.45) | copy-start | bytes 12292
Sparse Core Ops, SparseCore 0:
  11.7 108.2 all-gather.7
  123.8 103.0 all-gather.9
  230.6 102.9 all-gather.11
where the time goes:
time: 434 us; the launch traced here: 433 us
  waiting for transfers between devices  174 us (40%)
  blocking collectives  136 us (31%)
  local copies, waits for them, and re-layouts  84.6 us (19%)
  other arithmetic  15.5 us (4%)
  between operations  14 us (3%)
  matrix products  9.67 us (2%)
    all_gather x3, waiting for transfers between devices, shards(): lax.all_gather(cand, ('rows', 'sub'), axis=0, tiled=True)  174 us
    gather x3, local copies, waits for them, and re-layouts, live_slots(): limits = jnp.repeat(count_row, most, total_repeat_length=length)  77.2 us
    psum x1, blocking collectives, shards(): lax.psum(partial_value, ('rows', 'sub'))  76.9 us
    all_gather x1, blocking collectives, shards(): lax.all_gather(pick_counts, ('rows', 'sub'), axis=1, tiled=True)  58.7 us
    dot_general x3, matrix products, piece_minimum(): inner = jnp.dot(points, piece.T, preferred_element_type=jnp.float32)  9.67 us
  transfers between devices with their start and end apart: 3, of which 2 were waited for; matrix products, arithmetic and copies ran while one was open for 21% of the time, Pallas kernels for 0%

commit v1 on v0

v1 whole, which is shorter than its diff:
```python
import jax
import jax.numpy as jnp
from jax import lax
from jax.experimental import pallas as pl
from jax.experimental.pallas import tpu as pltpu
from jax.sharding import Mesh, PartitionSpec as P

CHIPS_Z, CHIPS_X, CORES = 8, 4, 2
TILE = 256


def nearest_kernel(first_ref, *refs):
    blocks, (mine_ref, other_ref, out_ref, sq_ref) = refs[:-4], refs[-4:]
    rounds = out_ref.shape[1]
    sources, slots, width = mine_ref.shape
    most = slots // rounds
    halves = (mine_ref, other_ref)
    rows = sources * most

    def half_round(half, step):
        return halves[half][:, step * most : (step + 1) * most, :].reshape(rows, width)

    for half in range(2):
        for step in range(rounds):
            values = half_round(half, step).astype(jnp.float32)
            squares = jnp.sum(values * values, axis=1, keepdims=True)
            sq_ref[half, step] = jnp.broadcast_to(squares, (rows, 128))

    count = len(blocks)
    for shift, block_ref in enumerate(blocks):
        place = lax.rem(first_ref[0] - shift + count, count)

        def one_tile(tile, _, block_ref=block_ref, place=place):
            start = pl.multiple_of(tile * TILE, TILE)
            weights = block_ref[pl.ds(start, TILE), :] * jnp.bfloat16(-2.0)
            for step in range(rounds):
                best = None
                for half in range(2):
                    values = half_round(half, step)
                    for part in range(0, rows, TILE):
                        inner = lax.dot_general(
                            values[part : part + TILE],
                            weights,
                            (((1,), (1,)), ((), ())),
                            preferred_element_type=jnp.float32,
                        )
                        squares = sq_ref[half, step, part : part + TILE, :]
                        dist = inner + jnp.concatenate([squares] * (TILE // 128), axis=1)
                        low = jnp.min(dist.reshape(TILE // 8, 8, TILE), axis=0)
                        best = low if best is None else jnp.minimum(best, low)
                out_ref[place, step : step + 1, pl.ds(start, TILE)] = jnp.min(
                    best, axis=0, keepdims=True
                )
            return 0

        lax.fori_loop(0, block_ref.shape[0] // TILE, one_tile, 0)


def nearest(first, blocks, mine, other, rounds):
    sources, slots, _ = mine.shape
    vmem = pl.BlockSpec(memory_space=pltpu.VMEM)
    return pl.pallas_call(
        nearest_kernel,
        out_shape=jax.ShapeDtypeStruct((len(blocks), rounds, blocks[0].shape[0]), jnp.float32),
        in_specs=[pl.BlockSpec(memory_space=pltpu.SMEM)] + [vmem] * (len(blocks) + 2),
        out_specs=vmem,
        scratch_shapes=[pltpu.VMEM((2, rounds, sources * (slots // rounds), 128), jnp.float32)],
        compiler_params=pltpu.CompilerParams(vmem_limit_bytes=32 * 1024 * 1024),
    )(first, *blocks, mine, other)


def shards(points, init_dist, picks, pick_counts):
    rounds, most = picks.shape
    rows, width = points.shape
    subs = lax.axis_size("y")
    groups = lax.axis_size(("z", "x"))
    blocks = [points] + [
        lax.ppermute(points, "y", [(i, (i + shift) % subs) for i in range(subs)])
        for shift in range(1, subs)
    ]
    slot_no = jnp.arange(most, dtype=jnp.int32)[None, :]
    named = jnp.where(slot_no < pick_counts, picks, picks[:, :1]).reshape(-1)
    select = (named[:, None] == jnp.arange(rows, dtype=jnp.int32)[None, :]).astype(jnp.bfloat16)
    cand = jnp.dot(select, points, preferred_element_type=jnp.float32).astype(jnp.bfloat16)
    mine = lax.all_to_all(
        jnp.broadcast_to(cand[None], (groups,) + cand.shape), ("z", "x"), 0, 0, tiled=True
    )
    other = lax.ppermute(mine, "c", [(0, 1), (1, 0)])
    first = lax.axis_index("y").astype(jnp.int32)[None]
    partial_low = nearest(first, blocks, mine, other, rounds)
    low = jnp.min(lax.all_to_all(partial_low, "y", 0, 0, tiled=True), axis=0)
    row_sq = jnp.sum(jnp.square(points.astype(jnp.float32)), axis=1)
    dist = jnp.maximum(row_sq[None] + low, 0.0)
    current = init_dist
    partials = []
    for step in range(rounds):
        current = jnp.minimum(current, dist[step])
        partials.append(jnp.sum(current))
    everyone = ("z", "x", "c", "y")
    devices = lax.axis_size(everyone)
    shares = jnp.broadcast_to(jnp.stack(partials)[None], (devices, rounds))
    round_costs = jnp.sum(lax.all_to_all(shares, everyone, 0, 0, tiled=True), axis=0)
    normalized = current * float(rows * devices) / round_costs[rounds - 1]
    return (current, normalized, round_costs)


def solution(mesh):
    fine = Mesh(
        mesh.devices.reshape(CHIPS_Z, CHIPS_X, CORES, mesh.shape["sub"]), ("z", "x", "c", "y")
    )
    rows = ("z", "x", "c", "y")
    return jax.shard_map(
        shards,
        mesh=fine,
        in_specs=(P(rows, None), P(rows), P(None, rows), P(None, rows)),
        out_specs=(P(rows), P(rows), P()),
        check_vma=False,
    )
```

time: 434 us -> 114 us (0.26)
  waiting for transfers between devices: 174 us -> 26.5 us
  blocking collectives: 136 us -> 53.7 us
  local copies, waits for them, and re-layouts: 84.6 us -> 3.09 us
  between operations: 14 us -> 0.72 us
  Pallas kernels: 0 us -> 12.1 us
  starting transfers between devices: 0.12 us -> 11.3 us
  other arithmetic: 15.5 us -> 4.63 us
  matrix products: 9.67 us -> 1.28 us
    all_gather x3 -> x0, waiting for transfers between devices: 174 us -> none  [shards(): lax.all_gather(cand, ('rows', 'sub'), axis=0, tiled=True)]
    gather x6 -> x0, local copies, waits for them, and re-layouts: 84.1 us -> none  [the longest x3 77.2 us: live_slots(): limits = jnp.repeat(count_row, most, total_repeat_length=length)]
    psum x1 -> x0, blocking collectives: 76.9 us -> none  [shards(): lax.psum(partial_value, ('rows', 'sub'))]
    all_gather x1 -> x0, blocking collectives: 58.7 us -> none  [shards(): lax.all_gather(pick_counts, ('rows', 'sub'), axis=1, tiled=True)]
    all_to_all x0 -> x2, blocking collectives: none -> 53.7 us  [the longest x1 32.9 us: shards(): lax.all_to_all(jnp.broadcast_to(cand[None], (groups,) + cand.shape), ('z'...]
    ppermute x0 -> x4, waiting for transfers between devices: none -> 22.3 us  [the longest x3 22.3 us: shards(): lax.ppermute(points, 'y', [(i, (i + shift) % subs) for i in range(subs)])]
    pallas_call x0 -> x1, Pallas kernels: none -> 12.1 us  [nearest(): pl.pallas_call(nearest_kernel, out_shape=jax.ShapeDtypeStruct((len(blocks...]
    dot_general x3 -> x1, matrix products: 9.67 us -> 1.28 us  [shards(): jnp.dot(select, points, preferred_element_type=jnp.float32)]
  transfers between devices with their start and end apart: 3 -> 5, of which waited for: 2 -> 3; matrix products, arithmetic and copies ran while one was open for 21% -> 0% of each run, Pallas kernels for 0% -> 0%
where the time goes in v1:
time: 114 us; the launch traced here: 113 us
  blocking collectives  53.7 us (47%)
  waiting for transfers between devices  26.5 us (23%)
  Pallas kernels  12.1 us (11%)
  starting transfers between devices  11.3 us (10%)
  other arithmetic  4.63 us (4%)
  local copies, waits for them, and re-layouts  3.09 us (3%)
  matrix products  1.28 us (1%)
    all_to_all x1, blocking collectives, shards(): lax.all_to_all(jnp.broadcast_to(cand[None], (groups,) + cand.shape), ('z'...  32.9 us
    ppermute x3, waiting for transfers between devices, shards(): lax.ppermute(points, 'y', [(i, (i + shift) % subs) for i in range(subs)])  22.3 us
    all_to_all x1, blocking collectives, shards(): lax.all_to_all(shares, everyone, 0, 0, tiled=True)  20.9 us
    pallas_call x1, Pallas kernels, nearest(): pl.pallas_call(nearest_kernel, out_shape=jax.ShapeDtypeStruct((len(blocks...  12.1 us
    ppermute x3, starting transfers between devices, shards(): lax.ppermute(points, 'y', [(i, (i + shift) % subs) for i in range(subs)])  4.98 us
    all_to_all x1, waiting for transfers between devices, shards(): low = jnp.min(lax.all_to_all(partial_low, 'y', 0, 0, tiled=True), axis=0)  4.26 us
    all_to_all x1, starting transfers between devices, shards(): low = jnp.min(lax.all_to_all(partial_low, 'y', 0, 0, tiled=True), axis=0)  3.45 us
    ppermute x1, starting transfers between devices, shards(): other = lax.ppermute(mine, 'c', [(0, 1), (1, 0)])  2.82 us
  transfers between devices with their start and end apart: 5, of which 3 were waited for; matrix products, arithmetic and copies ran while one was open for 0% of the time, Pallas kernels for 0%

profile of v1, /device:TPU:1, one launch (start us, length us, event | category | flops | bytes accessed | tf_op | source)
XLA Modules:
  0.0 113.3 jit_solution(2647332089364823117)
XLA Ops:
  0.6 0.0 copy-start.2
  0.6 0.9 slice_reduce_fusion
  1.5 0.0 copy-done.2
  1.5 0.6 copy-done.5
  2.2 0.1 fusion.1
  2.2 0.1 eq.15
  2.3 1.3 %convolution_convert_fusion = bf16[48,256]{1,0:T(8,128)(2,1)S(1)} fusion(bf16[1024,256]{1,0:T(8,128)(2,1)} %refs_0_.1, s32[48]{0:T(128)S(1)} %eq.15), kind=kOutput, calls=%fused_computation | convolution fusion | flops 25227264 | bytes 549056 | tf_op jit(solution)/shard_map/dot_general | solution.py:84
  3.6 0.1 broadcast_in_dim.31
  3.7 0.0 copy-start
  3.7 32.9 %all_to_all.16.refs_4_ = bf16[32,48,256]{2,1,0:T(8,128)(2,1)S(1)} all-to-all(bf16[32,48,256]{2,1,0:T(8,128)(2,1)S(1)} %broadcast_in_dim.31), channel_id=1, replica_groups=mesh['z'=8,'x'=4,'c'=2,'y'=4] {'z','x'}, dimensions={0} | all-to-all | bytes 1572864 | tf_op jit(solution)/shard_map/all_to_all | solution.py:85
  36.5 2.8 %collective-permute-start.3 = (bf16[32,48,256]{2,1,0:T(8,128)(2,1)S(1)}, bf16[32,48,256]{2,1,0:T(8,128)(2,1)S(1)}, u32[]{:S(2)}, u32[]{:S(2)}) collective-permute-start(bf16[32,48,256]{2,1,0:T(8,128)(2,1)S(1)} %all_to_all.16.refs_4_), channel_id=1, source_target_pairs={{0,4},{4,0},{1,5},{5,1},{2,6},{6,2},{3,7},{7,3},{8,12},{12,8},{9,1... | collective-permute-start | bytes 2359304 | tf_op jit(solution)/shard_map/ppermute | solution.py:88
  39.4 0.0 copy-done
  39.4 1.3 %collective-permute-start = (bf16[1024,256]{1,0:T(8,128)(2,1)S(1)}, bf16[1024,256]{1,0:T(8,128)(2,1)S(1)}, u32[]{:S(2)}, u32[]{:S(2)}) collective-permute-start(bf16[1024,256]{1,0:T(8,128)(2,1)S(1)} %copy-done), channel_id=1, source_target_pairs={{0,1},{1,2},{2,3},{3,0},{4,5},{5,6},{6,7},{7,4},{8,9},{9,10},{10,1... | collective-permute-start | bytes 1572872 | tf_op jit(solution)/shard_map/ppermute | solution.py:78
  40.7 2.6 %collective-permute-start.1 = (bf16[1024,256]{1,0:T(8,128)(2,1)S(1)}, bf16[1024,256]{1,0:T(8,128)(2,1)S(1)}, u32[]{:S(2)}, u32[]{:S(2)}) collective-permute-start(bf16[1024,256]{1,0:T(8,128)(2,1)S(1)} %copy-done), channel_id=1, source_target_pairs={{0,2},{1,3},{2,0},{3,1},{4,6},{5,7},{6,4},{7,5},{8,10},{9,11},{10,... | collective-permute-start | bytes 1572872 | tf_op jit(solution)/shard_map/ppermute | solution.py:78
  43.3 1.1 collective-permute-start.2
  44.3 9.9 %collective-permute-done.refs_1_ = bf16[1024,256]{1,0:T(8,128)(2,1)S(1)} collective-permute-done((bf16[1024,256]{1,0:T(8,128)(2,1)S(1)}, bf16[1024,256]{1,0:T(8,128)(2,1)S(1)}, u32[]{:S(2)}, u32[]{:S(2)}) %collective-permute-start) | collective-permute-done | bytes 524320 | tf_op jit(solution)/shard_map/ppermute | solution.py:78
  54.3 12.3 %collective-permute-done.1.refs_2_ = bf16[1024,256]{1,0:T(8,128)(2,1)S(1)} collective-permute-done((bf16[1024,256]{1,0:T(8,128)(2,1)S(1)}, bf16[1024,256]{1,0:T(8,128)(2,1)S(1)}, u32[]{:S(2)}, u32[]{:S(2)}) %collective-permute-start.1) | collective-permute-done | bytes 524320 | tf_op jit(solution)/shard_map/ppermute | solution.py:78
  66.6 0.0 collective-permute-done.2.refs_3_
  66.6 0.0 collective-permute-done.3.refs_5_
  66.6 12.1 %shard_map.67 = f32[4,3,1024]{2,1,0:T(4,128)} custom-call(s32[1]{0:T(128)} %bitcast.first_ref, bf16[1024,256]{1,0:T(8,128)(2,1)S(1)} %copy-done, bf16[1024,256]{1,0:T(8,128)(2,1)S(1)} %collective-permute-done.refs_1_, bf16[1024,256]{1,0:T(8,128)(2,1)S(1)} %collective-permute-done.1.refs_2_, bf16[1024,256]{1,0:T(8,128)(2,1)} %collective-permute-done.2.refs_3_, ...), custom_call_target="tpu_custom_call" | custom-call | tf_op jit(solution)/shard_map/pallas_call | solution.py:62
  78.7 3.5 %all-to-all-start.1 = ((f32[4,3,1024]{2,1,0:T(4,128)}), f32[4,3,1024]{2,1,0:T(4,128)S(1)}, u32[]{:S(2)}, u32[]{:S(2)}) async-start(f32[4,3,1024]{2,1,0:T(4,128)} %shard_map.67), calls=%async_computation.1 | async-start | bytes 131072 | tf_op jit(solution)/shard_map/all_to_all | solution.py:91
  82.2 0.2 multiply_reduce_fusion
  82.4 4.3 %all-to-all-done.1 = f32[4,3,1024]{2,1,0:T(4,128)S(1)} async-done(((f32[4,3,1024]{2,1,0:T(4,128)}), f32[4,3,1024]{2,1,0:T(4,128)S(1)}, u32[]{:S(2)}, u32[]{:S(2)}) %all-to-all-start.1) | async-done | bytes 49184 | tf_op jit(solution)/shard_map/all_to_all | solution.py:91
  86.7 0.0 copy-start.3
  86.7 0.7 copy-done.3
  87.4 0.7 minimum_reduce_fusion.1
  88.1 2.1 %pad_maximum_fusion = f32[3]{0:T(128)S(1)} fusion(f32[1]{0:T(128)} %bitcast.7, f32[1]{0:T(128)} %bitcast.6, f32[1]{0:T(128)} %bitcast.5), kind=kLoop, calls=%fused_computation.11 | loop fusion | flops 6 | bytes 24 | tf_op jit(solution)/shard_map/stack | solution.py:101
  90.2 0.1 broadcast_in_dim.32
  90.2 20.9 %all_to_all.17 = f32[256,1,3]{2,1,0:T(1,128)S(1)} all-to-all(f32[256,1,3]{2,1,0:T(1,128)S(1)} %broadcast_in_dim.32), channel_id=1, replica_groups=mesh['z'=8,'x'=4,'c'=2,'y'=4] {'z','x','c','y'}, dimensions={0} | all-to-all | bytes 6144 | tf_op jit(solution)/shard_map/all_to_all | solution.py:102
  111.1 0.3 reduce_sum.49
  111.4 0.7 slice.19
  112.1 1.3 %multiply_divide_fusion = f32[1024]{0:T(1024)} fusion(f32[1024]{0:T(1024)S(1)} %get-tuple-element.11, f32[]{:T(128)} %bitcast.8), kind=kLoop, calls=%fused_computation.5 | loop fusion | flops 2048 | bytes 8196 | tf_op jit(solution)/shard_map/div | solution.py:103
  (8 shorter events, 0.0 us)
Async XLA Ops:
  0.6 0.9 copy-start.2
  1.5 0.7 copy-start.5
  3.7 35.7 %copy-start = (bf16[1024,256]{1,0:T(8,128)(2,1)S(1)}, bf16[1024,256]{1,0:T(8,128)(2,1)}, u32[]{:S(2)}) copy-start(bf16[1024,256]{1,0:T(8,128)(2,1)} %refs_0_.1) | copy-start | bytes 1572868
  36.5 30.1 %collective-permute-start.3 = (bf16[32,48,256]{2,1,0:T(8,128)(2,1)S(1)}, bf16[32,48,256]{2,1,0:T(8,128)(2,1)S(1)}, u32[]{:S(2)}, u32[]{:S(2)}) collective-permute-start(bf16[32,48,256]{2,1,0:T(8,128)(2,1)S(1)} %all_to_all.16.refs_4_), channel_id=1, source_target_pairs={{0,4},{4,0},{1,5},{5,1},{2,6},{6,2},{3,7},{7,3},{8,12},{12,8},{9,1... | collective-permute-start | bytes 2359304 | tf_op jit(solution)/shard_map/ppermute | solution.py:88
  39.4 14.9 %collective-permute-start = (bf16[1024,256]{1,0:T(8,128)(2,1)S(1)}, bf16[1024,256]{1,0:T(8,128)(2,1)S(1)}, u32[]{:S(2)}, u32[]{:S(2)}) collective-permute-start(bf16[1024,256]{1,0:T(8,128)(2,1)S(1)} %copy-done), channel_id=1, source_target_pairs={{0,1},{1,2},{2,3},{3,0},{4,5},{5,6},{6,7},{7,4},{8,9},{9,10},{10,1... | collective-permute-start | bytes 1572872 | tf_op jit(solution)/shard_map/ppermute | solution.py:78
  40.7 25.9 %collective-permute-start.1 = (bf16[1024,256]{1,0:T(8,128)(2,1)S(1)}, bf16[1024,256]{1,0:T(8,128)(2,1)S(1)}, u32[]{:S(2)}, u32[]{:S(2)}) collective-permute-start(bf16[1024,256]{1,0:T(8,128)(2,1)S(1)} %copy-done), channel_id=1, source_target_pairs={{0,2},{1,3},{2,0},{3,1},{4,6},{5,7},{6,4},{7,5},{8,10},{9,11},{10,... | collective-permute-start | bytes 1572872 | tf_op jit(solution)/shard_map/ppermute | solution.py:78
  43.3 23.3 %collective-permute-start.2 = (bf16[1024,256]{1,0:T(8,128)(2,1)S(1)}, bf16[1024,256]{1,0:T(8,128)(2,1)}, u32[]{:S(2)}, u32[]{:S(2)}) collective-permute-start(bf16[1024,256]{1,0:T(8,128)(2,1)S(1)} %copy-done), channel_id=1, source_target_pairs={{0,3},{1,0},{2,1},{3,2},{4,7},{5,4},{6,5},{7,6},{8,11},{9,8},{10,9... | collective-permute-start | bytes 1572872 | tf_op jit(solution)/shard_map/ppermute | solution.py:78
  78.7 7.9 %all-to-all-start.1 = ((f32[4,3,1024]{2,1,0:T(4,128)}), f32[4,3,1024]{2,1,0:T(4,128)S(1)}, u32[]{:S(2)}, u32[]{:S(2)}) async-start(f32[4,3,1024]{2,1,0:T(4,128)} %shard_map.67), calls=%async_computation.1 | async-start | bytes 131072 | tf_op jit(solution)/shard_map/all_to_all | solution.py:91
  86.7 0.7 copy-start.3
  88.1 24.0 %copy-start.1 = (f32[1024]{0:T(1024)}, f32[1024]{0:T(1024)S(1)}, u32[]{:S(2)}) copy-start(f32[1024]{0:T(1024)S(1)} %get-tuple-element.11) | copy-start | bytes 12292
  111.4 0.7 copy-start.4

commit v2 on v0

v2 whole, which is shorter than its diff:
```python
import jax
import jax.numpy as jnp
from jax import lax
from jax.experimental import pallas as pl
from jax.experimental.pallas import tpu as pltpu
from jax.sharding import Mesh, PartitionSpec as P

CHIPS_Z, CHIPS_X, CORES = 8, 4, 2
PART = 256
LANES = 128
TURN_FLOPS = 3_000_000
F32, BF16 = jnp.float32, jnp.bfloat16
VMEM = pl.BlockSpec(memory_space=pltpu.VMEM)
SMEM = pl.BlockSpec(memory_space=pltpu.SMEM)
PARAMS = pltpu.CompilerParams(vmem_limit_bytes=40 * 1024 * 1024)


def pick_kernel(picks_ref, counts_ref, points_ref, out_ref, select_ref):
    rounds, most = picks_ref.shape
    column = lax.broadcasted_iota(jnp.int32, (1, points_ref.shape[0]), 1)
    for step in range(rounds):
        for slot in range(most):
            named = jnp.where(slot < counts_ref[step], picks_ref[step, slot], picks_ref[step, 0])
            row = step * most + slot
            select_ref[row : row + 1, :] = jnp.where(column == named, 1.0, 0.0).astype(F32)
    cand = jnp.dot(
        select_ref[...].astype(BF16), points_ref[...], preferred_element_type=F32
    ).astype(BF16)
    for copy in range(out_ref.shape[0]):
        out_ref[copy] = cand


def pick_rows(picks, counts, points, copies):
    slots = picks.shape[0] * picks.shape[1]
    rows, width = points.shape
    return pl.pallas_call(
        pick_kernel,
        out_shape=jax.ShapeDtypeStruct((copies, slots, width), BF16),
        in_specs=[SMEM, SMEM, VMEM],
        out_specs=VMEM,
        scratch_shapes=[pltpu.VMEM((slots, rows), F32)],
        compiler_params=PARAMS,
        cost_estimate=pl.CostEstimate(
            flops=2 * slots * rows * width, bytes_accessed=rows * width * 2, transcendentals=0
        ),
    )(picks, counts, points)


def turn_kernel(place_ref, *refs):
    blocks, (turned_ref, length_ref) = refs[:-2], refs[-2:]
    for number, block_ref in enumerate(blocks):
        turned = (block_ref[...] * BF16(-2.0)).T
        place = place_ref[number]
        turned_ref[place] = turned
        wide = turned.astype(F32)
        length_ref[place] = jnp.sum(wide * wide, axis=0, keepdims=True) * 0.25


def turn(places, blocks):
    count, (rows, width) = len(blocks), blocks[0].shape
    return pl.pallas_call(
        turn_kernel,
        out_shape=(
            jax.ShapeDtypeStruct((count, width, rows), BF16),
            jax.ShapeDtypeStruct((count, 1, rows), F32),
        ),
        in_specs=[SMEM] + [VMEM] * count,
        out_specs=(VMEM, VMEM),
        compiler_params=PARAMS,
        cost_estimate=pl.CostEstimate(
            flops=TURN_FLOPS, bytes_accessed=count * rows * width * 4, transcendentals=0
        ),
    )(places, *blocks)


def near_body(turned_ref, cand_ref, sq_ref, number, step, rounds):
    sources, slots, width = cand_ref.shape
    most = slots // rounds
    rows = sources * most
    count = turned_ref.shape[2]
    values = cand_ref[:, step * most : (step + 1) * most, :].reshape(rows, width)
    weights = turned_ref[number]
    best = None
    for part in range(0, rows, PART):
        inner = jnp.dot(values[part : part + PART], weights, preferred_element_type=F32)
        squares = sq_ref[step, part : part + PART, :]
        dist = inner + jnp.concatenate([squares] * (count // LANES), axis=1)
        low = jnp.min(dist.reshape(PART // 8, 8, count), axis=0)
        best = low if best is None else jnp.minimum(best, low)
    return jnp.min(best, axis=0, keepdims=True)


def squares_of(cand_ref, sq_ref, rounds):
    sources, slots, width = cand_ref.shape
    most = slots // rounds
    rows = sources * most
    for step in range(rounds):
        values = cand_ref[:, step * most : (step + 1) * most, :].reshape(rows, width).astype(F32)
        squares = jnp.sum(values * values, axis=1, keepdims=True)
        sq_ref[step] = jnp.broadcast_to(squares, (rows, LANES))


def first_kernel(turned_ref, cand_ref, out_ref, sq_ref):
    rounds = out_ref.shape[1]
    squares_of(cand_ref, sq_ref, rounds)
    for number in range(turned_ref.shape[0]):
        for step in range(rounds):
            out_ref[number, step : step + 1, :] = near_body(
                turned_ref, cand_ref, sq_ref, number, step, rounds
            )


def second_kernel(place_ref, turned_ref, cand_ref, low_ref, length_ref, init_ref, out_ref, sq_ref):
    copies, count, rounds, _ = out_ref.shape
    squares_of(cand_ref, sq_ref, rounds)
    mine = place_ref[0]
    for number in range(count):
        limit = jnp.where(mine == number, init_ref[...], jnp.inf)
        for step in range(rounds):
            low = near_body(turned_ref, cand_ref, sq_ref, number, step, rounds)
            low = jnp.minimum(low, low_ref[number, step : step + 1, :])
            dist = jnp.minimum(jnp.maximum(low + length_ref[number], 0.0), limit)
            for copy in range(copies):
                out_ref[copy, number, step : step + 1, :] = dist


def cost_of(turned, cand):
    count, width, rows = turned.shape
    return pl.CostEstimate(
        flops=2 * count * rows * width * cand.shape[0] * cand.shape[1],
        bytes_accessed=2 * (turned.size + cand.size),
        transcendentals=0,
    )


def first_half(turned, cand, rounds):
    count, width, rows = turned.shape
    return pl.pallas_call(
        first_kernel,
        out_shape=jax.ShapeDtypeStruct((count, rounds, rows), F32),
        in_specs=[VMEM] * 2,
        out_specs=VMEM,
        scratch_shapes=[pltpu.VMEM((rounds, cand.shape[0] * cand.shape[1] // rounds, LANES), F32)],
        compiler_params=PARAMS,
        cost_estimate=cost_of(turned, cand),
    )(turned, cand)


def second_half(places, turned, cand, low, lengths, init_row, rounds):
    count, width, rows = turned.shape
    return pl.pallas_call(
        second_kernel,
        out_shape=jax.ShapeDtypeStruct((count, count, rounds, rows), F32),
        in_specs=[SMEM] + [VMEM] * 5,
        out_specs=VMEM,
        scratch_shapes=[pltpu.VMEM((rounds, cand.shape[0] * cand.shape[1] // rounds, LANES), F32)],
        compiler_params=PARAMS,
        cost_estimate=cost_of(turned, cand),
    )(places, turned, cand, low, lengths, init_row)


def total_kernel(place_ref, dist_ref, own_ref, total_ref):
    rounds = dist_ref.shape[2]
    dist = jnp.min(dist_ref[...], axis=0)
    lane = lax.broadcasted_iota(jnp.int32, total_ref.shape, 1)
    total = jnp.zeros(total_ref.shape, F32)
    current = None
    for step in range(rounds):
        current = dist[:, step, :] if step == 0 else jnp.minimum(current, dist[:, step, :])
        total = jnp.where(lane == step, jnp.sum(current), total)
    total_ref[...] = total
    mine = place_ref[0]
    own = current[0:1]
    for number in range(1, current.shape[0]):
        own = jnp.where(mine == number, current[number : number + 1], own)
    own_ref[...] = own


def totals(places, dist, peers):
    return pl.pallas_call(
        total_kernel,
        out_shape=(
            jax.ShapeDtypeStruct((1, dist.shape[3]), F32),
            jax.ShapeDtypeStruct((peers, LANES), F32),
        ),
        in_specs=[SMEM, VMEM],
        out_specs=(VMEM, VMEM),
        compiler_params=PARAMS,
    )(places, dist)


def finish_kernel(all_rows, own_ref, share_ref, normal_ref, cost_ref):
    rounds = cost_ref.shape[1]
    total = jnp.sum(share_ref[...], axis=0, keepdims=True)
    cost_ref[...] = total[:, :rounds]
    normal_ref[...] = own_ref[...] * all_rows / total[:, rounds - 1 : rounds]


def finish(own, shares, rounds, all_rows):
    def body(*refs):
        finish_kernel(all_rows, *refs)

    return pl.pallas_call(
        body,
        out_shape=(
            jax.ShapeDtypeStruct(own.shape, F32),
            jax.ShapeDtypeStruct((1, rounds), F32),
        ),
        in_specs=[VMEM, VMEM],
        out_specs=(VMEM, VMEM),
        compiler_params=PARAMS,
    )(own, shares)


def shards(points, init_dist, picks, pick_counts):
    rounds, most = picks.shape
    rows, width = points.shape
    subs = lax.axis_size("y")
    sub = lax.axis_index("y").astype(jnp.int32)
    blocks = [points] + [
        lax.ppermute(points, "y", [(i, (i + shift) % subs) for i in range(subs)])
        for shift in range(1, subs)
    ]
    places = (sub - jnp.arange(subs, dtype=jnp.int32)) % subs
    cand = pick_rows(picks, pick_counts.reshape(-1), points, CHIPS_Z)
    along_z = lax.all_to_all(cand, "z", 0, 0, tiled=True)
    along_z, blocks[1], blocks[3] = lax.optimization_barrier((along_z, blocks[1], blocks[3]))
    mine = lax.all_to_all(
        jnp.broadcast_to(along_z[None], (CHIPS_X,) + along_z.shape), "x", 0, 0
    ).reshape((CHIPS_Z * CHIPS_X,) + cand.shape[1:])
    other = lax.ppermute(mine, "c", [(0, 1), (1, 0)])
    turned, lengths = turn(places, blocks)
    low = first_half(turned, mine, rounds)
    dist = second_half(places, turned, other, low, lengths, init_dist[None], rounds)
    shared = lax.all_to_all(dist, "y", 0, 0, tiled=True)
    peers = ("z", "x", "c")
    own, total = totals(places, shared, lax.axis_size(("z", "x")))
    total = total + lax.ppermute(total, "c", [(0, 1), (1, 0)])
    shares = lax.all_to_all(total, ("z", "x"), 0, 0, tiled=True)
    all_rows = float(rows * subs * lax.axis_size(peers))
    normalized, round_costs = finish(own, shares, rounds, all_rows)
    return (own[0], normalized[0], round_costs[0])


def solution(mesh):
    fine = Mesh(
        mesh.devices.reshape(CHIPS_Z, CHIPS_X, CORES, mesh.shape["sub"]), ("z", "x", "c", "y")
    )
    rows = ("z", "x", "c", "y")
    return jax.shard_map(
        shards,
        mesh=fine,
        in_specs=(P(rows, None), P(rows), P(None, rows), P(None, rows)),
        out_specs=(P(rows), P(rows), P()),
        check_vma=False,
    )
```

time: 434 us -> 82.4 us (0.19)
  waiting for transfers between devices: 174 us -> 8.43 us
  blocking collectives: 136 us -> 38.8 us
  local copies, waits for them, and re-layouts: 84.6 us -> 4.37 us
  starting transfers between devices: 0.12 us -> 17.3 us
  other arithmetic: 15.5 us -> 0.01 us
  between operations: 14 us -> 0.7 us
  Pallas kernels: 0 us -> 12.3 us
  matrix products: 9.67 us -> 0 us
    all_gather x3 -> x0, waiting for transfers between devices: 174 us -> none  [shards(): lax.all_gather(cand, ('rows', 'sub'), axis=0, tiled=True)]
    gather x6 -> x0, local copies, waits for them, and re-layouts: 84.1 us -> none  [the longest x3 77.2 us: live_slots(): limits = jnp.repeat(count_row, most, total_repeat_length=length)]
    psum x1 -> x0, blocking collectives: 76.9 us -> none  [shards(): lax.psum(partial_value, ('rows', 'sub'))]
    all_gather x1 -> x0, blocking collectives: 58.7 us -> none  [shards(): lax.all_gather(pick_counts, ('rows', 'sub'), axis=1, tiled=True)]
    all_to_all x0 -> x3, blocking collectives: none -> 38.8 us  [the longest x1 16.5 us: shards(): along_z = lax.all_to_all(cand, 'z', 0, 0, tiled=True)]
    ppermute x0 -> x5, starting transfers between devices: none -> 13.3 us  [the longest x3 5.18 us: shards(): lax.ppermute(points, 'y', [(i, (i + shift) % subs) for i in range(subs)])]
    pallas_call x0 -> x6, Pallas kernels: none -> 12.3 us  [the longest x1 4.72 us: second_half(): pl.pallas_call(second_kernel, out_shape=jax.ShapeDtypeStruct((count, coun...]
    dot_general x3 -> x0, matrix products: 9.67 us -> none  [piece_minimum(): inner = jnp.dot(points, piece.T, preferred_element_type=jnp.float32)]
  transfers between devices with their start and end apart: 3 -> 6, of which waited for: 2 -> 2; matrix products, arithmetic and copies ran while one was open for 21% -> 0% of each run, Pallas kernels for 0% -> 7%
where the time goes in v2:
time: 82.4 us; the launch traced here: 82 us
  blocking collectives  38.8 us (47%)
  starting transfers between devices  17.3 us (21%)
  Pallas kernels  12.3 us (15%)
  waiting for transfers between devices  8.43 us (10%)
  local copies, waits for them, and re-layouts  4.37 us (5%)
    all_to_all x1, blocking collectives, shards(): along_z = lax.all_to_all(cand, 'z', 0, 0, tiled=True)  16.5 us
    all_to_all x1, blocking collectives, shards(): shares = lax.all_to_all(total, ('z', 'x'), 0, 0, tiled=True)  13.5 us
    all_to_all x1, blocking collectives, shards(): shared = lax.all_to_all(dist, 'y', 0, 0, tiled=True)  8.81 us
    all_to_all x1, waiting for transfers between devices, shards(): lax.all_to_all(jnp.broadcast_to(along_z[None], (CHIPS_X,) + along_z.shape...  7.58 us
    ppermute x3, starting transfers between devices, shards(): lax.ppermute(points, 'y', [(i, (i + shift) % subs) for i in range(subs)])  5.18 us
    pallas_call x1, Pallas kernels, second_half(): pl.pallas_call(second_kernel, out_shape=jax.ShapeDtypeStruct((count, coun...  4.72 us
    ppermute x1, starting transfers between devices, shards(): other = lax.ppermute(mine, 'c', [(0, 1), (1, 0)])  4.13 us
    ppermute x1, starting transfers between devices, shards(): total = total + lax.ppermute(total, 'c', [(0, 1), (1, 0)])  4.02 us
  transfers between devices with their start and end apart: 6, of which 2 were waited for; matrix products, arithmetic and copies ran while one was open for 0% of the time, Pallas kernels for 7%

profile of v2, /device:TPU:1, one launch (start us, length us, event | category | flops | bytes accessed | tf_op | source)
XLA Modules:
  0.0 82.0 jit_solution(9692409654127807458)
XLA Ops:
  0.6 3.6 %collective-permute-start.1 = (bf16[1024,256]{1,0:T(8,128)(2,1)}, bf16[1024,256]{1,0:T(8,128)(2,1)S(1)}, u32[]{:S(2)}, u32[]{:S(2)}) collective-permute-start(bf16[1024,256]{1,0:T(8,128)(2,1)} %refs_0_.1), channel_id=1, source_target_pairs={{0,3},{1,0},{2,1},{3,2},{4,7},{5,4},{6,5},{7,6},{8,11},{9,8},{10,9... | collective-permute-start | bytes 1572872 | tf_op jit(solution)/shard_map/ppermute | solution.py:221
  4.3 0.0 collective-permute-start
  4.3 0.0 copy-start
  4.3 1.1 %copy-done = bf16[1024,256]{1,0:T(8,128)(2,1)S(1)} copy-done((bf16[1024,256]{1,0:T(8,128)(2,1)S(1)}, bf16[1024,256]{1,0:T(8,128)(2,1)}, u32[]{:S(2)}) %copy-start) | copy-done | bytes 524312
  5.4 0.7 copy-done.3
  6.1 0.7 copy-done.4
  6.7 0.9 %shard_map.67 = bf16[8,48,256]{2,1,0:T(8,128)(2,1)S(1)} custom-call(s32[3,16]{1,0:T(4,128)S(1)} %copy-done.3, s32[3]{0:T(128)S(1)} %bitcast.14, bf16[1024,256]{1,0:T(8,128)(2,1)S(1)} %copy-done), custom_call_target="tpu_custom_call" | custom-call | flops 25165824 | bytes 524288 | tf_op jit(solution)/shard_map/pallas_call | solution.py:36
  7.6 16.5 %all_to_all.26 = bf16[8,48,256]{2,1,0:T(8,128)(2,1)S(1)} all-to-all(bf16[8,48,256]{2,1,0:T(8,128)(2,1)S(1)} %shard_map.67), channel_id=1, replica_groups=mesh['z'=8,'x'=4,'c'=2,'y'=4] {'z'}, dimensions={0} | all-to-all | bytes 393216 | tf_op jit(solution)/shard_map/all_to_all | solution.py:226
  24.1 0.0 collective-permute-done.1.refs_3_
  24.1 0.0 collective-permute-done.refs_1_
  24.1 1.0 %broadcast_in_dim.4 = bf16[4,8,48,256]{3,2,1,0:T(8,128)(2,1)} broadcast(bf16[8,48,256]{2,1,0:T(8,128)(2,1)S(1)} %all_to_all.26), dimensions={1,2,3} | broadcast | bytes 983040 | tf_op jit(solution)/shard_map/broadcast_in_dim | solution.py:229
  25.1 4.0 %all-to-all-start.1 = ((bf16[4,8,48,256]{3,2,1,0:T(8,128)(2,1)}), bf16[4,8,48,256]{3,2,1,0:T(8,128)(2,1)S(1)}, u32[]{:S(2)}, u32[]{:S(2)}) async-start(bf16[4,8,48,256]{3,2,1,0:T(8,128)(2,1)} %broadcast_in_dim.4), calls=%async_computation.1 | async-start | bytes 1572864 | tf_op jit(solution)/shard_map/all_to_all | solution.py:228
  29.1 0.0 copy-done.1
  29.1 1.5 %collective-permute-start.2 = (bf16[1024,256]{1,0:T(8,128)(2,1)S(1)}, bf16[1024,256]{1,0:T(8,128)(2,1)S(1)}, u32[]{:S(2)}, u32[]{:S(2)}) collective-permute-start(bf16[1024,256]{1,0:T(8,128)(2,1)S(1)} %copy-done.1), channel_id=1, source_target_pairs={{0,2},{1,3},{2,0},{3,1},{4,6},{5,7},{6,4},{7,5},{8,10},{9,11},{10,... | collective-permute-start | bytes 1572872 | tf_op jit(solution)/shard_map/ppermute | solution.py:221
  30.6 7.6 %all-to-all-done.1 = bf16[4,8,48,256]{3,2,1,0:T(8,128)(2,1)S(1)} async-done(((bf16[4,8,48,256]{3,2,1,0:T(8,128)(2,1)}), bf16[4,8,48,256]{3,2,1,0:T(8,128)(2,1)S(1)}, u32[]{:S(2)}, u32[]{:S(2)}) %all-to-all-start.1) | async-done | bytes 786464 | tf_op jit(solution)/shard_map/all_to_all | solution.py:228
  38.2 4.1 %collective-permute-start.3 = (bf16[32,48,256]{2,1,0:T(8,128)(2,1)S(1)}, bf16[32,48,256]{2,1,0:T(8,128)(2,1)}, u32[]{:S(2)}, u32[]{:S(2)}) collective-permute-start(bf16[32,48,256]{2,1,0:T(8,128)(2,1)S(1)} %bitcast.10), channel_id=1, source_target_pairs={{0,4},{4,0},{1,5},{5,1},{2,6},{6,2},{3,7},{7,3},{8,12},{12,8},{9,1... | collective-permute-start | bytes 2359304 | tf_op jit(solution)/shard_map/ppermute | solution.py:231
  42.4 0.0 collective-permute-done.2.refs_2_
  42.4 1.3 %shard_map.68 = (bf16[4,256,1024]{2,1,0:T(8,128)(2,1)S(1)}, f32[4,1,1024]{2,1,0:T(1,128)S(1)}) custom-call(s32[4]{0:T(128)S(1)} %and_select_fusion.place_ref, bf16[1024,256]{1,0:T(8,128)(2,1)S(1)} %copy-done.1, bf16[1024,256]{1,0:T(8,128)(2,1)S(1)} %collective-permute-done.refs_1_, bf16[1024,256]{1,0:T(8,128)(2,1)S(1)} %collective-permute-done.2.refs_2_, ...), custom_call_target="tpu_custom_call" | custom-call | flops 3000000 | bytes 4194304 | tf_op jit(solution)/shard_map/pallas_call | solution.py:61
  43.7 0.0 copy-start.5
  43.7 3.6 %shard_map.69.low_ref = f32[4,3,1024]{2,1,0:T(4,128)S(1)} custom-call(bf16[4,256,1024]{2,1,0:T(8,128)(2,1)S(1)} %get-tuple-element.14.turned_ref, bf16[32,48,256]{2,1,0:T(8,128)(2,1)S(1)} %bitcast.11), custom_call_target="tpu_custom_call" | custom-call | flops 3221225472 | bytes 2883584 | tf_op jit(solution)/shard_map/pallas_call | solution.py:138
  47.2 0.0 collective-permute-done.3.cand_ref
  47.3 0.0 copy-done.5
  47.3 4.7 %shard_map.70 = f32[4,4,3,1024]{3,2,1,0:T(4,128)S(1)} custom-call(s32[4]{0:T(128)S(1)} %and_select_fusion.place_ref, bf16[4,256,1024]{2,1,0:T(8,128)(2,1)S(1)} %get-tuple-element.14.turned_ref, bf16[32,48,256]{2,1,0:T(8,128)(2,1)} %collective-permute-done.3.cand_ref, f32[4,3,1024]{2,1,0:T(4,128)S(1)} %shard_map.69.low_ref, ...), custom_call_target="tpu_custom_call" | custom-call | flops 3221225472 | bytes 2883584 | tf_op jit(solution)/shard_map/pallas_call | solution.py:151
  52.0 0.1 copy.7
  52.1 8.8 %all_to_all.27 = f32[4,4,3,1024]{3,1,2,0:T(4,128)S(1)} all-to-all(f32[4,4,3,1024]{3,1,2,0:T(4,128)S(1)} %copy.7), channel_id=1, replica_groups=mesh['z'=8,'x'=4,'c'=2,'y'=4] {'y'}, dimensions={0} | all-to-all | bytes 393216 | tf_op jit(solution)/shard_map/all_to_all | solution.py:235
  60.9 0.1 copy.8.dist_ref
  61.1 1.2 %shard_map.71 = (f32[1,1024]{1,0:T(1,128)}, f32[32,128]{1,0:T(8,128)S(1)}) custom-call(s32[4]{0:T(128)S(1)} %and_select_fusion.place_ref, f32[4,4,3,1024]{3,2,1,0:T(4,128)S(1)} %copy.8.dist_ref), custom_call_target="tpu_custom_call" | custom-call | tf_op jit(solution)/shard_map/pallas_call | solution.py:180
  62.3 4.0 %collective-permute-start.4 = (f32[32,128]{1,0:T(8,128)S(1)}, f32[32,128]{1,0:T(8,128)S(1)}, u32[]{:S(2)}, u32[]{:S(2)}) collective-permute-start(f32[32,128]{1,0:T(8,128)S(1)} %get-tuple-element.18), channel_id=1, source_target_pairs={{0,4},{4,0},{1,5},{5,1},{2,6},{6,2},{3,7},{7,3},{8,12},{12,8},{9,1... | collective-permute-start | bytes 49160 | tf_op jit(solution)/shard_map/ppermute | solution.py:238
  66.3 0.8 %collective-permute-done.4 = f32[32,128]{1,0:T(8,128)S(1)} collective-permute-done((f32[32,128]{1,0:T(8,128)S(1)}, f32[32,128]{1,0:T(8,128)S(1)}, u32[]{:S(2)}, u32[]{:S(2)}) %collective-permute-start.4) | collective-permute-done | bytes 16416 | tf_op jit(solution)/shard_map/ppermute | solution.py:238
  67.1 13.5 %all_to_all.28 = f32[32,1,128]{2,1,0:T(1,128)S(1)} all-to-all(f32[32,1,128]{2,1,0:T(1,128)S(1)} %bitcast.16), channel_id=1, replica_groups=mesh['z'=8,'x'=4,'c'=2,'y'=4] {'z','x'}, dimensions={0} | all-to-all | bytes 32768 | tf_op jit(solution)/shard_map/all_to_all | solution.py:239
  80.7 0.7 copy-done.2
  81.3 0.7 shard_map.72
  (6 shorter events, 0.0 us)
Async XLA Ops:
  0.6 23.5 %collective-permute-start.1 = (bf16[1024,256]{1,0:T(8,128)(2,1)}, bf16[1024,256]{1,0:T(8,128)(2,1)S(1)}, u32[]{:S(2)}, u32[]{:S(2)}) collective-permute-start(bf16[1024,256]{1,0:T(8,128)(2,1)} %refs_0_.1), channel_id=1, source_target_pairs={{0,3},{1,0},{2,1},{3,2},{4,7},{5,4},{6,5},{7,6},{8,11},{9,8},{10,9... | collective-permute-start | bytes 1572872 | tf_op jit(solution)/shard_map/ppermute | solution.py:221
  4.3 19.9 %collective-permute-start = (bf16[1024,256]{1,0:T(8,128)(2,1)}, bf16[1024,256]{1,0:T(8,128)(2,1)S(1)}, u32[]{:S(2)}, u32[]{:S(2)}) collective-permute-start(bf16[1024,256]{1,0:T(8,128)(2,1)} %refs_0_.1), channel_id=1, source_target_pairs={{0,1},{1,2},{2,3},{3,0},{4,5},{5,6},{6,7},{7,4},{8,9},{9,10},{10,1... | collective-permute-start | bytes 1572872 | tf_op jit(solution)/shard_map/ppermute | solution.py:221
  4.3 1.1 %copy-start = (bf16[1024,256]{1,0:T(8,128)(2,1)S(1)}, bf16[1024,256]{1,0:T(8,128)(2,1)}, u32[]{:S(2)}) copy-start(bf16[1024,256]{1,0:T(8,128)(2,1)} %refs_0_.1) | copy-start | bytes 1572868
  5.4 0.7 copy-start.3
  6.1 0.7 copy-start.4
  6.7 22.4 %copy-start.1 = (bf16[1024,256]{1,0:T(8,128)(2,1)S(1)}, bf16[1024,256]{1,0:T(8,128)(2,1)}, u32[]{:S(2)}) copy-start(bf16[1024,256]{1,0:T(8,128)(2,1)} %refs_0_.1) | copy-start | bytes 1572868
  25.1 13.1 %all-to-all-start.1 = ((bf16[4,8,48,256]{3,2,1,0:T(8,128)(2,1)}), bf16[4,8,48,256]{3,2,1,0:T(8,128)(2,1)S(1)}, u32[]{:S(2)}, u32[]{:S(2)}) async-start(bf16[4,8,48,256]{3,2,1,0:T(8,128)(2,1)} %broadcast_in_dim.4), calls=%async_computation.1 | async-start | bytes 1572864 | tf_op jit(solution)/shard_map/all_to_all | solution.py:228
  29.1 13.3 %collective-permute-start.2 = (bf16[1024,256]{1,0:T(8,128)(2,1)S(1)}, bf16[1024,256]{1,0:T(8,128)(2,1)S(1)}, u32[]{:S(2)}, u32[]{:S(2)}) collective-permute-start(bf16[1024,256]{1,0:T(8,128)(2,1)S(1)} %copy-done.1), channel_id=1, source_target_pairs={{0,2},{1,3},{2,0},{3,1},{4,6},{5,7},{6,4},{7,5},{8,10},{9,11},{10,... | collective-permute-start | bytes 1572872 | tf_op jit(solution)/shard_map/ppermute | solution.py:221
  38.2 9.0 %collective-permute-start.3 = (bf16[32,48,256]{2,1,0:T(8,128)(2,1)S(1)}, bf16[32,48,256]{2,1,0:T(8,128)(2,1)}, u32[]{:S(2)}, u32[]{:S(2)}) collective-permute-start(bf16[32,48,256]{2,1,0:T(8,128)(2,1)S(1)} %bitcast.10), channel_id=1, source_target_pairs={{0,4},{4,0},{1,5},{5,1},{2,6},{6,2},{3,7},{7,3},{8,12},{12,8},{9,1... | collective-permute-start | bytes 2359304 | tf_op jit(solution)/shard_map/ppermute | solution.py:231
  43.7 3.6 %copy-start.5 = (f32[1024]{0:T(1024)S(1)}, f32[1024]{0:T(1024)}, u32[]{:S(2)}) copy-start(f32[1024]{0:T(1024)} %param.5) | copy-start | bytes 12292
  62.3 4.9 %collective-permute-start.4 = (f32[32,128]{1,0:T(8,128)S(1)}, f32[32,128]{1,0:T(8,128)S(1)}, u32[]{:S(2)}, u32[]{:S(2)}) collective-permute-start(f32[32,128]{1,0:T(8,128)S(1)} %get-tuple-element.18), channel_id=1, source_target_pairs={{0,4},{4,0},{1,5},{5,1},{2,6},{6,2},{3,7},{7,3},{8,12},{12,8},{9,1... | collective-permute-start | bytes 49160 | tf_op jit(solution)/shard_map/ppermute | solution.py:238
  80.7 0.7 copy-start.2

commit v3 on v2

v3 whole, which is shorter than its diff:
```python
import jax
import jax.numpy as jnp
from jax import lax
from jax.experimental import pallas as pl
from jax.experimental.pallas import tpu as pltpu
from jax.sharding import Mesh, PartitionSpec as P

CHIPS_Z, CHIPS_X, CORES = 8, 4, 2
PART = 256
LANES = 128
F32, BF16 = jnp.float32, jnp.bfloat16
VMEM = pl.BlockSpec(memory_space=pltpu.VMEM)
ANY = pl.BlockSpec(memory_space=pl.ANY)
SMEM = pl.BlockSpec(memory_space=pltpu.SMEM)
PARAMS = pltpu.CompilerParams(vmem_limit_bytes=40 * 1024 * 1024)


def pick_kernel(picks_hbm, counts_hbm, points_hbm, out_ref, picks_ref, counts_ref, points_ref, select_ref, sems):
    copies = [
        pltpu.make_async_copy(points_hbm, points_ref, sems.at[0]),
        pltpu.make_async_copy(picks_hbm, picks_ref, sems.at[1]),
        pltpu.make_async_copy(counts_hbm, counts_ref, sems.at[2]),
    ]
    for copy in copies:
        copy.start()
    copies[1].wait()
    copies[2].wait()
    rounds, most = picks_ref.shape
    column = lax.broadcasted_iota(jnp.int32, (1, points_ref.shape[0]), 1)
    for step in range(rounds):
        for slot in range(most):
            named = jnp.where(slot < counts_ref[step], picks_ref[step, slot], picks_ref[step, 0])
            row = step * most + slot
            select_ref[row : row + 1, :] = jnp.where(column == named, 1.0, 0.0).astype(F32)
    select = select_ref[...].astype(BF16)
    copies[0].wait()
    cand = jnp.dot(select, points_ref[...], preferred_element_type=F32).astype(BF16)
    for place in range(out_ref.shape[0]):
        out_ref[place] = cand


def pick_rows(picks, counts, points, copies):
    slots = picks.shape[0] * picks.shape[1]
    rows, width = points.shape
    return pl.pallas_call(
        pick_kernel,
        out_shape=jax.ShapeDtypeStruct((copies, slots, width), BF16),
        in_specs=[ANY, ANY, ANY],
        out_specs=VMEM,
        scratch_shapes=[
            pltpu.SMEM(picks.shape, jnp.int32),
            pltpu.SMEM(counts.shape, jnp.int32),
            pltpu.VMEM(points.shape, BF16),
            pltpu.VMEM((slots, rows), F32),
            pltpu.SemaphoreType.DMA((3,)),
        ],
        compiler_params=pltpu.CompilerParams(vmem_limit_bytes=60 * 1024 * 1024),
        cost_estimate=pl.CostEstimate(
            flops=2 * slots * rows * width, bytes_accessed=rows * width * 2, transcendentals=0
        ),
    )(picks, counts, points)


def turn_kernel(*refs):
    blocks, (turned_ref, length_ref) = refs[:-2], refs[-2:]
    width = turned_ref.shape[1]
    place = 0
    for block_ref in blocks:
        rows = block_ref.shape[0]
        number, start = divmod(place, turned_ref.shape[2])
        turned = (block_ref[...] * BF16(-2.0)).T
        turned_ref[number, :, start : start + rows] = turned
        wide = turned.astype(F32)
        length_ref[number, :, start : start + rows] = jnp.sum(wide * wide, axis=0, keepdims=True) * 0.25
        place += rows


def turn(blocks, rows):
    width = blocks[0].shape[1]
    count = sum(block.shape[0] for block in blocks) // rows
    return pl.pallas_call(
        turn_kernel,
        out_shape=(
            jax.ShapeDtypeStruct((count, width, rows), BF16),
            jax.ShapeDtypeStruct((count, 1, rows), F32),
        ),
        in_specs=[VMEM] * len(blocks),
        out_specs=(VMEM, VMEM),
        compiler_params=PARAMS,
        cost_estimate=pl.CostEstimate(
            flops=count * rows * width * 3, bytes_accessed=count * rows * width * 4, transcendentals=0
        ),
    )(*blocks)


def half_round(cand_ref, step, rounds):
    sources, slots, width = cand_ref.shape
    most = slots // rounds
    return cand_ref[:, step * most : (step + 1) * most, :].reshape(sources * most, width)


def squares_of(cands, sq_ref, rounds):
    for step in range(rounds):
        base = 0
        for cand_ref in cands:
            values = half_round(cand_ref, step, rounds).astype(F32)
            squares = jnp.sum(values * values, axis=1, keepdims=True)
            rows = values.shape[0]
            sq_ref[step, base : base + rows] = jnp.broadcast_to(squares, (rows, LANES))
            base += rows


def lowest(weights, cands, sq_ref, step, rounds):
    count = weights.shape[1]
    best = None
    base = 0
    for cand_ref in cands:
        values = half_round(cand_ref, step, rounds)
        for part in range(0, values.shape[0], PART):
            piece = values[part : part + PART]
            size = piece.shape[0]
            inner = jnp.dot(piece, weights, preferred_element_type=F32)
            squares = sq_ref[step, base : base + size, :]
            dist = inner + jnp.concatenate([squares] * (count // LANES), axis=1)
            low = jnp.min(dist.reshape(size // 8, 8, count), axis=0)
            best = low if best is None else jnp.minimum(best, low)
            base += size
    return jnp.min(best, axis=0, keepdims=True)


def blocks_of(turned):
    return [(ref, number) for ref in turned for number in range(ref.shape[0])]


def near_cost(turned, cands):
    columns = sum(block.shape[0] * block.shape[2] for block in turned)
    return pl.CostEstimate(
        flops=2 * columns * sum(cand.size for cand in cands),
        bytes_accessed=2 * sum(x.size for x in turned + cands),
        transcendentals=0,
    )


def near(turned, cands, low, rounds):
    count, rows = sum(block.shape[0] for block in turned), turned[0].shape[2]

    def body(*refs):
        turned_refs, refs = refs[: len(turned)], refs[len(turned) :]
        cand_refs, refs = refs[: len(cands)], refs[len(cands) :]
        out_ref, sq_ref = refs[-2:]
        squares_of(cand_refs, sq_ref, rounds)
        for place, (ref, number) in enumerate(blocks_of(turned_refs)):
            for step in range(rounds):
                value = lowest(ref[number], cand_refs, sq_ref, step, rounds)
                if low is not None:
                    value = jnp.minimum(value, refs[0][place, step : step + 1, :])
                out_ref[place, step : step + 1, :] = value

    extra = [] if low is None else [low]
    slots = sum(cand.shape[0] * cand.shape[1] for cand in cands)
    return pl.pallas_call(
        body,
        out_shape=jax.ShapeDtypeStruct((count, rounds, rows), F32),
        in_specs=[VMEM] * (len(turned) + len(cands) + len(extra)),
        out_specs=VMEM,
        scratch_shapes=[pltpu.VMEM((rounds, slots // rounds, LANES), F32)],
        compiler_params=PARAMS,
        cost_estimate=near_cost(turned, cands),
    )(*turned, *cands, *extra)


def last_near(places, turned, cands, low, lengths, init_row, rounds):
    count, rows = sum(block.shape[0] for block in turned), turned[0].shape[2]

    def body(place_ref, *refs):
        turned_refs, refs = refs[: len(turned)], refs[len(turned) :]
        length_refs, refs = refs[: len(turned)], refs[len(turned) :]
        cand_refs, refs = refs[: len(cands)], refs[len(cands) :]
        low_ref, init_ref, out_ref, sq_ref = refs
        squares_of(cand_refs, sq_ref, rounds)
        blocks = zip(blocks_of(turned_refs), blocks_of(length_refs))
        for number, ((ref, inner), (length_ref, _)) in enumerate(blocks):
            place = place_ref[number]
            for step in range(rounds):
                value = lowest(ref[inner], cand_refs, sq_ref, step, rounds)
                value = jnp.minimum(value, low_ref[number, step : step + 1, :])
                dist = jnp.maximum(value + length_ref[inner], 0.0)
                if number == 0:
                    dist = jnp.minimum(dist, init_ref[...])
                for copy in range(out_ref.shape[0]):
                    out_ref[copy, step, pl.ds(place, 1), :] = dist

    slots = sum(cand.shape[0] * cand.shape[1] for cand in cands)
    return pl.pallas_call(
        body,
        out_shape=jax.ShapeDtypeStruct((count, rounds, count, rows), F32),
        in_specs=[SMEM] + [VMEM] * (len(turned) + len(lengths) + len(cands) + 2),
        out_specs=VMEM,
        scratch_shapes=[pltpu.VMEM((rounds, slots // rounds, LANES), F32)],
        compiler_params=PARAMS,
        cost_estimate=near_cost(turned, cands),
    )(places, *turned, *lengths, *cands, low, init_row)


def total_kernel(place_ref, dist_ref, own_ref, total_ref):
    rounds = dist_ref.shape[1]
    lane = lax.broadcasted_iota(jnp.int32, total_ref.shape, 1)
    total = jnp.zeros(total_ref.shape, F32)
    current = None
    for step in range(rounds):
        dist = jnp.min(dist_ref[:, step], axis=0)
        current = dist if step == 0 else jnp.minimum(current, dist)
        total = jnp.where(lane == step, jnp.sum(current), total)
    total_ref[...] = total
    mine = place_ref[0]
    own = current[0:1]
    for number in range(1, current.shape[0]):
        own = jnp.where(mine == number, current[number : number + 1], own)
    own_ref[...] = own


def totals(places, dist, peers):
    return pl.pallas_call(
        total_kernel,
        out_shape=(
            jax.ShapeDtypeStruct((1, dist.shape[3]), F32),
            jax.ShapeDtypeStruct((peers, LANES), F32),
        ),
        in_specs=[SMEM, VMEM],
        out_specs=(VMEM, VMEM),
        compiler_params=PARAMS,
    )(places, dist)


def finish(own, shares, rounds, all_rows):
    def body(own_ref, share_ref, min_ref, normal_ref, cost_ref):
        total = jnp.sum(share_ref[...], axis=0, keepdims=True)
        cost_ref[...] = total[:, :rounds]
        min_ref[...] = own_ref[...]
        normal_ref[...] = own_ref[...] * all_rows / total[:, rounds - 1 : rounds]

    row = jax.ShapeDtypeStruct(own.shape, F32)
    return pl.pallas_call(
        body,
        out_shape=(row, row, jax.ShapeDtypeStruct((1, rounds), F32)),
        in_specs=[VMEM, VMEM],
        out_specs=(VMEM, VMEM, VMEM),
        compiler_params=PARAMS,
    )(own, shares)


def shift(block, axis, size, by):
    return lax.ppermute(block, axis, [(i, (i + by) % size) for i in range(size)])


def shards(points, init_dist, picks, pick_counts):
    rounds, most = picks.shape
    rows, width = points.shape
    subs = lax.axis_size("y")
    sub = lax.axis_index("y").astype(jnp.int32)
    half = rows // 2
    behind, ahead = (shift(points, "y", subs, by) for by in (1, 3))
    across = [shift(behind[:half], "y", subs, 1), shift(ahead[half:], "y", subs, 3)]
    places = (sub + jnp.array([0, 3, 1, 2], jnp.int32)) % subs
    cand = pick_rows(picks, pick_counts.reshape(-1), points, CHIPS_Z)
    along_z = lax.all_to_all(cand, "z", 0, 0, tiled=True)
    from_x = [shift(along_z, "x", CHIPS_X, by) for by in (2, 1, 3)]
    opposite, after, before = from_x
    swapped = shift(along_z, "c", CORES, 1)
    near_turned, near_lengths = turn([points, behind, ahead], rows)
    far_turned, far_lengths = turn(across, rows)
    turned, lengths = [near_turned, far_turned], [near_lengths, far_lengths]
    low = near(turned, [along_z, swapped], None, rounds)
    beside = [shift(piece, "c", CORES, 1) for piece in (after, before)]
    low = near(turned, [after, before], low, rounds)
    low = near(turned, beside, low, rounds)
    opposite, low = lax.optimization_barrier((opposite, low))
    last = shift(opposite, "c", CORES, 1)
    low = near(turned, [opposite], low, rounds)
    last = [last]
    dist = last_near(places, turned, last, low, lengths, init_dist[None], rounds)
    shared = lax.all_to_all(dist, "y", 0, 0, tiled=True)
    own, total = totals(places, shared, lax.axis_size(("z", "x")))
    total = total + shift(total, "c", CORES, 1)
    shares = lax.all_to_all(total, ("z", "x"), 0, 0, tiled=True)
    all_rows = float(rows * lax.axis_size(("z", "x", "c", "y")))
    min_dist, normalized, round_costs = finish(own, shares, rounds, all_rows)
    return (min_dist[0], normalized[0], round_costs[0])


def solution(mesh):
    fine = Mesh(
        mesh.devices.reshape(CHIPS_Z, CHIPS_X, CORES, mesh.shape["sub"]), ("z", "x", "c", "y")
    )
    rows = ("z", "x", "c", "y")
    return jax.shard_map(
        shards,
        mesh=fine,
        in_specs=(P(rows, None), P(rows), P(None, rows), P(None, rows)),
        out_specs=(P(rows), P(rows), P()),
        check_vma=False,
    )
```

time: 82.4 us -> 69 us (0.84)
  blocking collectives: 38.8 us -> 20.6 us
  starting transfers between devices: 17.3 us -> 28.4 us
  local copies, waits for them, and re-layouts: 4.37 us -> 0.05 us
  waiting for transfers between devices: 8.43 us -> 6.4 us
    all_to_all x1 -> x0, blocking collectives: 16.5 us -> none  [shards(): along_z = lax.all_to_all(cand, 'z', 0, 0, tiled=True)]
    ppermute x5 -> x12, starting transfers between devices: 13.3 us -> 20.2 us  [shift(): lax.ppermute(block, axis, [(i, (i + by) % size) for i in range(size)])]
    all_to_all x1, starting transfers between devices: 4.01 us -> 8.2 us  [shards(): along_z = lax.all_to_all(cand, 'z', 0, 0, tiled=True)]
    unnamed x12 -> x6, local copies, waits for them, and re-layouts: 3.14 us -> 0.02 us
    all_to_all x1, waiting for transfers between devices: 7.58 us -> 5.41 us  [shards(): along_z = lax.all_to_all(cand, 'z', 0, 0, tiled=True)]
    pallas_call x1, Pallas kernels: 0.91 us -> 1.97 us  [pick_rows(): pl.pallas_call(pick_kernel, out_shape=jax.ShapeDtypeStruct((copies, slots...]
    broadcast_in_dim x1 -> x0, local copies, waits for them, and re-layouts: 0.97 us -> none  [shards(): jnp.broadcast_to(along_z[None], (CHIPS_X,) + along_z.shape)]
    all_to_all x1, blocking collectives: 8.81 us -> 7.87 us  [shards(): shared = lax.all_to_all(dist, 'y', 0, 0, tiled=True)]
  transfers between devices with their start and end apart: 6 -> 13, of which waited for: 2 -> 3; matrix products, arithmetic and copies ran while one was open for 0% -> 0% of each run, Pallas kernels for 7% -> 14%
where the time goes in v3:
time: 69 us; the launch traced here: 68.7 us
  starting transfers between devices  28.4 us (41%)
  blocking collectives  20.6 us (30%)
  Pallas kernels  12.5 us (18%)
  waiting for transfers between devices  6.4 us (9%)
  between operations  0.77 us (1%)
    ppermute x12, starting transfers between devices, shift(): lax.ppermute(block, axis, [(i, (i + by) % size) for i in range(size)])  20.2 us
    all_to_all x1, blocking collectives, shards(): shares = lax.all_to_all(total, ('z', 'x'), 0, 0, tiled=True)  12.7 us
    all_to_all x1, starting transfers between devices, shards(): along_z = lax.all_to_all(cand, 'z', 0, 0, tiled=True)  8.2 us
    all_to_all x1, blocking collectives, shards(): shared = lax.all_to_all(dist, 'y', 0, 0, tiled=True)  7.87 us
    pallas_call x4, Pallas kernels, near(): pl.pallas_call(body, out_shape=jax.ShapeDtypeStruct((count, rounds, rows)...  6.77 us
    all_to_all x1, waiting for transfers between devices, shards(): along_z = lax.all_to_all(cand, 'z', 0, 0, tiled=True)  5.41 us
    pallas_call x1, Pallas kernels, pick_rows(): pl.pallas_call(pick_kernel, out_shape=jax.ShapeDtypeStruct((copies, slots...  1.97 us
    pallas_call x1, Pallas kernels, last_near(): pl.pallas_call(body, out_shape=jax.ShapeDtypeStruct((count, rounds, count...  1.65 us
  transfers between devices with their start and end apart: 13, of which 3 were waited for; matrix products, arithmetic and copies ran while one was open for 0% of the time, Pallas kernels for 14%

profile of v3, /device:TPU:1, one launch (start us, length us, event | category | flops | bytes accessed | tf_op | source)
XLA Modules:
  0.0 68.7 jit_solution(18336138576799659555)
XLA Ops:
  0.6 2.2 %collective-permute-start = (bf16[1024,256]{1,0:T(8,128)(2,1)}, bf16[1024,256]{1,0:T(8,128)(2,1)S(1)}, u32[]{:S(2)}, u32[]{:S(2)}) collective-permute-start(bf16[1024,256]{1,0:T(8,128)(2,1)} %points_hbm.1), channel_id=1, source_target_pairs={{0,1},{1,2},{2,3},{3,0},{4,5},{5,6},{6,7},{7,4},{8,9},{9,10},{10,1... | collective-permute-start | bytes 1572872 | tf_op jit(solution)/shard_map/ppermute | solution.py:253
  2.8 1.5 %collective-permute-start.1 = (bf16[1024,256]{1,0:T(8,128)(2,1)}, bf16[1024,256]{1,0:T(8,128)(2,1)S(1)}, u32[]{:S(2)}, u32[]{:S(2)}) collective-permute-start(bf16[1024,256]{1,0:T(8,128)(2,1)} %points_hbm.1), channel_id=1, source_target_pairs={{0,3},{1,0},{2,1},{3,2},{4,7},{5,4},{6,5},{7,6},{8,11},{9,8},{10,9... | collective-permute-start | bytes 1572872 | tf_op jit(solution)/shard_map/ppermute | solution.py:253
  4.4 2.0 %shard_map.78 = bf16[8,48,256]{2,1,0:T(8,128)(2,1)} custom-call(s32[3,16]{1,0:T(4,128)} %picks_hbm.1, s32[3]{0:T(128)} %bitcast.12, bf16[1024,256]{1,0:T(8,128)(2,1)} %points_hbm.1), custom_call_target="tpu_custom_call" | custom-call | flops 25165824 | bytes 524288 | tf_op jit(solution)/shard_map/pallas_call | solution.py:45
  6.4 8.2 %all-to-all-start = ((bf16[8,48,256]{2,1,0:T(8,128)(2,1)}), bf16[8,48,256]{2,1,0:T(8,128)(2,1)S(1)}, u32[]{:S(2)}, u32[]{:S(2)}) async-start(bf16[8,48,256]{2,1,0:T(8,128)(2,1)} %shard_map.78), calls=%async_computation | async-start | bytes 393216 | tf_op jit(solution)/shard_map/all_to_all | solution.py:266
  14.6 1.2 %collective-permute-start.2 = (bf16[512,256]{1,0:T(8,128)(2,1)S(1)}, bf16[512,256]{1,0:T(8,128)(2,1)S(1)}, u32[]{:S(2)}, u32[]{:S(2)}) collective-permute-start(bf16[512,256]{1,0:T(8,128)(2,1)S(1)} %slice.8), channel_id=1, source_target_pairs={{0,1},{1,2},{2,3},{3,0},{4,5},{5,6},{6,7},{7,4},{8,9},{9,10},{10,1... | collective-permute-start | bytes 786440 | tf_op jit(solution)/shard_map/ppermute | solution.py:253
  15.8 1.7 %collective-permute-start.3 = (bf16[512,256]{1,0:T(8,128)(2,1)S(1)}, bf16[512,256]{1,0:T(8,128)(2,1)S(1)}, u32[]{:S(2)}, u32[]{:S(2)}) collective-permute-start(bf16[512,256]{1,0:T(8,128)(2,1)S(1)} %slice.9), channel_id=1, source_target_pairs={{0,3},{1,0},{2,1},{3,2},{4,7},{5,4},{6,5},{7,6},{8,11},{9,8},{10,9... | collective-permute-start | bytes 786440 | tf_op jit(solution)/shard_map/ppermute | solution.py:253
  17.5 5.4 %all-to-all-done.refs_2_ = bf16[8,48,256]{2,1,0:T(8,128)(2,1)S(1)} async-done(((bf16[8,48,256]{2,1,0:T(8,128)(2,1)}), bf16[8,48,256]{2,1,0:T(8,128)(2,1)S(1)}, u32[]{:S(2)}, u32[]{:S(2)}) %all-to-all-start) | async-done | bytes 196640 | tf_op jit(solution)/shard_map/all_to_all | solution.py:266
  22.9 1.2 %collective-permute-start.5 = (bf16[8,48,256]{2,1,0:T(8,128)(2,1)S(1)}, bf16[8,48,256]{2,1,0:T(8,128)(2,1)S(1)}, u32[]{:S(2)}, u32[]{:S(2)}) collective-permute-start(bf16[8,48,256]{2,1,0:T(8,128)(2,1)S(1)} %all-to-all-done.refs_2_), channel_id=1, source_target_pairs={{0,8},{8,16},{16,24},{24,0},{1,9},{9,17},{17,25},{25,1},{2,10},{10... | collective-permute-start | bytes 589832 | tf_op jit(solution)/shard_map/ppermute | solution.py:253
  24.1 1.5 %collective-permute-start.7 = (bf16[8,48,256]{2,1,0:T(8,128)(2,1)S(1)}, bf16[8,48,256]{2,1,0:T(8,128)(2,1)S(1)}, u32[]{:S(2)}, u32[]{:S(2)}) collective-permute-start(bf16[8,48,256]{2,1,0:T(8,128)(2,1)S(1)} %all-to-all-done.refs_2_), channel_id=1, source_target_pairs={{0,24},{8,0},{16,8},{24,16},{1,25},{9,1},{17,9},{25,17},{2,26},{10... | collective-permute-start | bytes 589832 | tf_op jit(solution)/shard_map/ppermute | solution.py:253
  25.6 3.6 %collective-permute-start.9 = (bf16[8,48,256]{2,1,0:T(8,128)(2,1)S(1)}, bf16[8,48,256]{2,1,0:T(8,128)(2,1)S(1)}, u32[]{:S(2)}, u32[]{:S(2)}) collective-permute-start(bf16[8,48,256]{2,1,0:T(8,128)(2,1)S(1)} %all-to-all-done.refs_2_), channel_id=1, source_target_pairs={{0,4},{4,0},{1,5},{5,1},{2,6},{6,2},{3,7},{7,3},{8,12},{12,8},{9,1... | collective-permute-start | bytes 589832 | tf_op jit(solution)/shard_map/ppermute | solution.py:253
  29.2 0.5 shard_map.76
  29.8 1.6 %collective-permute-start.4 = (bf16[8,48,256]{2,1,0:T(8,128)(2,1)S(1)}, bf16[8,48,256]{2,1,0:T(8,128)(2,1)S(1)}, u32[]{:S(2)}, u32[]{:S(2)}) collective-permute-start(bf16[8,48,256]{2,1,0:T(8,128)(2,1)S(1)} %all-to-all-done.refs_2_), channel_id=1, source_target_pairs={{0,16},{8,24},{16,0},{24,8},{1,17},{9,25},{17,1},{25,9},{2,18},{10... | collective-permute-start | bytes 589832 | tf_op jit(solution)/shard_map/ppermute | solution.py:253
  31.4 3.3 %collective-permute-start.6 = (bf16[8,48,256]{2,1,0:T(8,128)(2,1)S(1)}, bf16[8,48,256]{2,1,0:T(8,128)(2,1)S(1)}, u32[]{:S(2)}, u32[]{:S(2)}) collective-permute-start(bf16[8,48,256]{2,1,0:T(8,128)(2,1)S(1)} %collective-permute-done.5.refs_2_), channel_id=1, source_target_pairs={{0,4},{4,0},{1,5},{5,1},{2,6},{6,2},{3,7},{7,3},{8,12},{12,8},{9,1... | collective-permute-start | bytes 589832 | tf_op jit(solution)/shard_map/ppermute | solution.py:253
  34.7 0.0 collective-permute-done.2.refs_0_
  34.7 0.3 collective-permute-start.8
  35.0 0.2 shard_map.77
  35.2 0.0 collective-permute-done.9.refs_3_
  35.2 1.9 %shard_map.79.refs_4_ = f32[4,3,1024]{2,1,0:T(4,128)S(1)} custom-call(bf16[3,256,1024]{2,1,0:T(8,128)(2,1)S(1)} %get-tuple-element.14.refs_0_, bf16[1,256,1024]{2,1,0:T(8,128)(2,1)S(1)} %get-tuple-element.15.refs_1_, bf16[8,48,256]{2,1,0:T(8,128)(2,1)S(1)} %all-to-all-done.refs_2_, bf16[8,48,256]{2,1,0:T(8,128)(2,1)S(1)} %collective-permute-done.9.refs_3_), custom_call_target="tpu_custom_call" | custom-call | flops 1610612736 | bytes 2490368 | tf_op jit(solution)/shard_map/pallas_call | solution.py:161
  37.1 1.9 %shard_map.80.refs_4_ = f32[4,3,1024]{2,1,0:T(4,128)S(1)} custom-call(bf16[3,256,1024]{2,1,0:T(8,128)(2,1)S(1)} %get-tuple-element.14.refs_0_, bf16[1,256,1024]{2,1,0:T(8,128)(2,1)S(1)} %get-tuple-element.15.refs_1_, bf16[8,48,256]{2,1,0:T(8,128)(2,1)S(1)} %collective-permute-done.5.refs_2_, bf16[8,48,256]{2,1,0:T(8,128)(2,1)S(1)} %collective-permute-done.7.refs_3_, ...), custom_call_target="tpu_custom_call" | custom-call | flops 1610612736 | bytes 2490368 | tf_op jit(solution)/shard_map/pallas_call | solution.py:161
  39.0 0.0 copy-start.2
  39.0 1.9 %shard_map.81.refs_3_ = f32[4,3,1024]{2,1,0:T(4,128)S(1)} custom-call(bf16[3,256,1024]{2,1,0:T(8,128)(2,1)S(1)} %get-tuple-element.14.refs_0_, bf16[1,256,1024]{2,1,0:T(8,128)(2,1)S(1)} %get-tuple-element.15.refs_1_, bf16[8,48,256]{2,1,0:T(8,128)(2,1)S(1)} %collective-permute-done.6.refs_2_, bf16[8,48,256]{2,1,0:T(8,128)(2,1)S(1)} %collective-permute-done.8.refs_3_, ...), custom_call_target="tpu_custom_call" | custom-call | flops 1610612736 | bytes 2490368 | tf_op jit(solution)/shard_map/pallas_call | solution.py:161
  40.9 0.0 copy-start.1
  41.0 0.3 collective-permute-start.10
  41.3 1.1 %shard_map.82.refs_5_ = f32[4,3,1024]{2,1,0:T(4,128)S(1)} custom-call(bf16[3,256,1024]{2,1,0:T(8,128)(2,1)S(1)} %get-tuple-element.14.refs_0_, bf16[1,256,1024]{2,1,0:T(8,128)(2,1)S(1)} %get-tuple-element.15.refs_1_, bf16[8,48,256]{2,1,0:T(8,128)(2,1)S(1)} %collective-permute-done.4.refs_2_, f32[4,3,1024]{2,1,0:T(4,128)S(1)} %shard_map.81.refs_3_), custom_call_target="tpu_custom_call" | custom-call | flops 805306368 | bytes 2293760 | tf_op jit(solution)/shard_map/pallas_call | solution.py:161
  42.4 0.1 collective-permute-done.10.refs_4_
  42.5 1.7 %shard_map.83 = f32[4,3,4,1024]{3,2,1,0:T(4,128)S(1)} custom-call(s32[4]{0:T(128)S(1)} %and_select_fusion.place_ref, bf16[3,256,1024]{2,1,0:T(8,128)(2,1)S(1)} %get-tuple-element.14.refs_0_, bf16[1,256,1024]{2,1,0:T(8,128)(2,1)S(1)} %get-tuple-element.15.refs_1_, f32[3,1,1024]{2,1,0:T(1,128)S(1)} %get-tuple-element.16.refs_2_, ...), custom_call_target="tpu_custom_call" | custom-call | flops 805306368 | bytes 2293760 | tf_op jit(solution)/shard_map/pallas_call | solution.py:194
  44.2 7.9 %all_to_all.21.dist_ref = f32[4,3,4,1024]{3,2,1,0:T(4,128)S(1)} all-to-all(f32[4,3,4,1024]{3,2,1,0:T(4,128)S(1)} %shard_map.83), channel_id=1, replica_groups=mesh['z'=8,'x'=4,'c'=2,'y'=4] {'y'}, dimensions={0} | all-to-all | bytes 393216 | tf_op jit(solution)/shard_map/all_to_all | solution.py:282
  52.0 0.7 shard_map.84
  52.7 1.8 %collective-permute-start.11 = (f32[32,128]{1,0:T(8,128)S(1)}, f32[32,128]{1,0:T(8,128)S(1)}, u32[]{:S(2)}, u32[]{:S(2)}) collective-permute-start(f32[32,128]{1,0:T(8,128)S(1)} %get-tuple-element.21), channel_id=1, source_target_pairs={{0,4},{4,0},{1,5},{5,1},{2,6},{6,2},{3,7},{7,3},{8,12},{12,8},{9,1... | collective-permute-start | bytes 49160 | tf_op jit(solution)/shard_map/ppermute | solution.py:253
  54.5 0.8 %collective-permute-done.11 = f32[32,128]{1,0:T(8,128)S(1)} collective-permute-done((f32[32,128]{1,0:T(8,128)S(1)}, f32[32,128]{1,0:T(8,128)S(1)}, u32[]{:S(2)}, u32[]{:S(2)}) %collective-permute-start.11) | collective-permute-done | bytes 16416 | tf_op jit(solution)/shard_map/ppermute | solution.py:253
  55.3 12.7 %all_to_all.22 = f32[32,1,128]{2,1,0:T(1,128)S(1)} all-to-all(f32[32,1,128]{2,1,0:T(1,128)S(1)} %bitcast.11), channel_id=1, replica_groups=mesh['z'=8,'x'=4,'c'=2,'y'=4] {'z','x'}, dimensions={0} | all-to-all | bytes 32768 | tf_op jit(solution)/shard_map/all_to_all | solution.py:285
  68.0 0.7 shard_map.85
  (16 shorter events, 0.1 us)
Async XLA Ops:
  0.6 28.6 %copy-start = (bf16[1024,256]{1,0:T(8,128)(2,1)S(1)}, bf16[1024,256]{1,0:T(8,128)(2,1)}, u32[]{:S(2)}) copy-start(bf16[1024,256]{1,0:T(8,128)(2,1)} %points_hbm.1) | copy-start | bytes 1572868
  0.6 13.9 %collective-permute-start = (bf16[1024,256]{1,0:T(8,128)(2,1)}, bf16[1024,256]{1,0:T(8,128)(2,1)S(1)}, u32[]{:S(2)}, u32[]{:S(2)}) collective-permute-start(bf16[1024,256]{1,0:T(8,128)(2,1)} %points_hbm.1), channel_id=1, source_target_pairs={{0,1},{1,2},{2,3},{3,0},{4,5},{5,6},{6,7},{7,4},{8,9},{9,10},{10,1... | collective-permute-start | bytes 1572872 | tf_op jit(solution)/shard_map/ppermute | solution.py:253
  2.8 12.9 %collective-permute-start.1 = (bf16[1024,256]{1,0:T(8,128)(2,1)}, bf16[1024,256]{1,0:T(8,128)(2,1)S(1)}, u32[]{:S(2)}, u32[]{:S(2)}) collective-permute-start(bf16[1024,256]{1,0:T(8,128)(2,1)} %points_hbm.1), channel_id=1, source_target_pairs={{0,3},{1,0},{2,1},{3,2},{4,7},{5,4},{6,5},{7,6},{8,11},{9,8},{10,9... | collective-permute-start | bytes 1572872 | tf_op jit(solution)/shard_map/ppermute | solution.py:253
  6.4 16.6 %all-to-all-start = ((bf16[8,48,256]{2,1,0:T(8,128)(2,1)}), bf16[8,48,256]{2,1,0:T(8,128)(2,1)S(1)}, u32[]{:S(2)}, u32[]{:S(2)}) async-start(bf16[8,48,256]{2,1,0:T(8,128)(2,1)} %shard_map.78), calls=%async_computation | async-start | bytes 393216 | tf_op jit(solution)/shard_map/all_to_all | solution.py:266
  14.6 20.1 %collective-permute-start.2 = (bf16[512,256]{1,0:T(8,128)(2,1)S(1)}, bf16[512,256]{1,0:T(8,128)(2,1)S(1)}, u32[]{:S(2)}, u32[]{:S(2)}) collective-permute-start(bf16[512,256]{1,0:T(8,128)(2,1)S(1)} %slice.8), channel_id=1, source_target_pairs={{0,1},{1,2},{2,3},{3,0},{4,5},{5,6},{6,7},{7,4},{8,9},{9,10},{10,1... | collective-permute-start | bytes 786440 | tf_op jit(solution)/shard_map/ppermute | solution.py:253
  15.8 19.2 %collective-permute-start.3 = (bf16[512,256]{1,0:T(8,128)(2,1)S(1)}, bf16[512,256]{1,0:T(8,128)(2,1)S(1)}, u32[]{:S(2)}, u32[]{:S(2)}) collective-permute-start(bf16[512,256]{1,0:T(8,128)(2,1)S(1)} %slice.9), channel_id=1, source_target_pairs={{0,3},{1,0},{2,1},{3,2},{4,7},{5,4},{6,5},{7,6},{8,11},{9,8},{10,9... | collective-permute-start | bytes 786440 | tf_op jit(solution)/shard_map/ppermute | solution.py:253
  22.9 6.8 %collective-permute-start.5 = (bf16[8,48,256]{2,1,0:T(8,128)(2,1)S(1)}, bf16[8,48,256]{2,1,0:T(8,128)(2,1)S(1)}, u32[]{:S(2)}, u32[]{:S(2)}) collective-permute-start(bf16[8,48,256]{2,1,0:T(8,128)(2,1)S(1)} %all-to-all-done.refs_2_), channel_id=1, source_target_pairs={{0,8},{8,16},{16,24},{24,0},{1,9},{9,17},{17,25},{25,1},{2,10},{10... | collective-permute-start | bytes 589832 | tf_op jit(solution)/shard_map/ppermute | solution.py:253
  24.1 7.3 %collective-permute-start.7 = (bf16[8,48,256]{2,1,0:T(8,128)(2,1)S(1)}, bf16[8,48,256]{2,1,0:T(8,128)(2,1)S(1)}, u32[]{:S(2)}, u32[]{:S(2)}) collective-permute-start(bf16[8,48,256]{2,1,0:T(8,128)(2,1)S(1)} %all-to-all-done.refs_2_), channel_id=1, source_target_pairs={{0,24},{8,0},{16,8},{24,16},{1,25},{9,1},{17,9},{25,17},{2,26},{10... | collective-permute-start | bytes 589832 | tf_op jit(solution)/shard_map/ppermute | solution.py:253
  25.6 9.6 %collective-permute-start.9 = (bf16[8,48,256]{2,1,0:T(8,128)(2,1)S(1)}, bf16[8,48,256]{2,1,0:T(8,128)(2,1)S(1)}, u32[]{:S(2)}, u32[]{:S(2)}) collective-permute-start(bf16[8,48,256]{2,1,0:T(8,128)(2,1)S(1)} %all-to-all-done.refs_2_), channel_id=1, source_target_pairs={{0,4},{4,0},{1,5},{5,1},{2,6},{6,2},{3,7},{7,3},{8,12},{12,8},{9,1... | collective-permute-start | bytes 589832 | tf_op jit(solution)/shard_map/ppermute | solution.py:253
  29.8 11.2 %collective-permute-start.4 = (bf16[8,48,256]{2,1,0:T(8,128)(2,1)S(1)}, bf16[8,48,256]{2,1,0:T(8,128)(2,1)S(1)}, u32[]{:S(2)}, u32[]{:S(2)}) collective-permute-start(bf16[8,48,256]{2,1,0:T(8,128)(2,1)S(1)} %all-to-all-done.refs_2_), channel_id=1, source_target_pairs={{0,16},{8,24},{16,0},{24,8},{1,17},{9,25},{17,1},{25,9},{2,18},{10... | collective-permute-start | bytes 589832 | tf_op jit(solution)/shard_map/ppermute | solution.py:253
  31.4 7.6 %collective-permute-start.6 = (bf16[8,48,256]{2,1,0:T(8,128)(2,1)S(1)}, bf16[8,48,256]{2,1,0:T(8,128)(2,1)S(1)}, u32[]{:S(2)}, u32[]{:S(2)}) collective-permute-start(bf16[8,48,256]{2,1,0:T(8,128)(2,1)S(1)} %collective-permute-done.5.refs_2_), channel_id=1, source_target_pairs={{0,4},{4,0},{1,5},{5,1},{2,6},{6,2},{3,7},{7,3},{8,12},{12,8},{9,1... | collective-permute-start | bytes 589832 | tf_op jit(solution)/shard_map/ppermute | solution.py:253
  34.7 4.3 %collective-permute-start.8 = (bf16[8,48,256]{2,1,0:T(8,128)(2,1)S(1)}, bf16[8,48,256]{2,1,0:T(8,128)(2,1)S(1)}, u32[]{:S(2)}, u32[]{:S(2)}) collective-permute-start(bf16[8,48,256]{2,1,0:T(8,128)(2,1)S(1)} %collective-permute-done.7.refs_3_), channel_id=1, source_target_pairs={{0,4},{4,0},{1,5},{5,1},{2,6},{6,2},{3,7},{7,3},{8,12},{12,8},{9,1... | collective-permute-start | bytes 589832 | tf_op jit(solution)/shard_map/ppermute | solution.py:253
  39.0 2.3 %copy-start.2 = (s32[4]{0:T(128)S(1)}, s32[4]{0:T(128)}, u32[]{:S(2)}) copy-start(s32[4]{0:T(128)} %constant.21.clone) | copy-start | bytes 52
  40.9 1.6 %copy-start.1 = (f32[1024]{0:T(1024)S(1)}, f32[1024]{0:T(1024)}, u32[]{:S(2)}) copy-start(f32[1024]{0:T(1024)} %param.6) | copy-start | bytes 12292
  41.0 1.5 %collective-permute-start.10 = (bf16[8,48,256]{2,1,0:T(8,128)(2,1)S(1)}, bf16[8,48,256]{2,1,0:T(8,128)(2,1)S(1)}, u32[]{:S(2)}, u32[]{:S(2)}) collective-permute-start(bf16[8,48,256]{2,1,0:T(8,128)(2,1)S(1)} %collective-permute-done.4.refs_2_), channel_id=1, source_target_pairs={{0,4},{4,0},{1,5},{5,1},{2,6},{6,2},{3,7},{7,3},{8,12},{12,8},{9,1... | collective-permute-start | bytes 589832 | tf_op jit(solution)/shard_map/ppermute | solution.py:253
  52.7 2.6 %collective-permute-start.11 = (f32[32,128]{1,0:T(8,128)S(1)}, f32[32,128]{1,0:T(8,128)S(1)}, u32[]{:S(2)}, u32[]{:S(2)}) collective-permute-start(f32[32,128]{1,0:T(8,128)S(1)} %get-tuple-element.21), channel_id=1, source_target_pairs={{0,4},{4,0},{1,5},{5,1},{2,6},{6,2},{3,7},{7,3},{8,12},{12,8},{9,1... | collective-permute-start | bytes 49160 | tf_op jit(solution)/shard_map/ppermute | solution.py:253

commit v4 on v3

--- a/solution.py
+++ b/solution.py
@@ -15,25 +15,31 @@
 PARAMS = pltpu.CompilerParams(vmem_limit_bytes=40 * 1024 * 1024)
 
 
-def pick_kernel(picks_hbm, counts_hbm, points_hbm, out_ref, picks_ref, counts_ref, points_ref, select_ref, sems):
+def pick_kernel(picks_hbm, counts_hbm, points_hbm, out_ref, picks_ref, counts_ref, points_ref, sems):
     copies = [
-        pltpu.make_async_copy(points_hbm, points_ref, sems.at[0]),
-        pltpu.make_async_copy(picks_hbm, picks_ref, sems.at[1]),
-        pltpu.make_async_copy(counts_hbm, counts_ref, sems.at[2]),
+        pltpu.make_async_copy(picks_hbm, picks_ref, sems.at[0]),
+        pltpu.make_async_copy(counts_hbm, counts_ref, sems.at[1]),
+        pltpu.make_async_copy(points_hbm, points_ref, sems.at[2]),
     ]
     for copy in copies:
         copy.start()
+    rounds, most = picks_ref.shape
+    rows = points_ref.shape[0]
+    slot = lax.broadcasted_iota(jnp.int32, (1, most), 1)
+    diagonal = lax.broadcasted_iota(jnp.int32, (most, most), 0) == lax.broadcasted_iota(
+        jnp.int32, (most, most), 1
+    )
+    column = lax.broadcasted_iota(jnp.int32, (most, rows), 1)
+    copies[0].wait()
     copies[1].wait()
+    select = []
+    for step in range(rounds):
+        picked = picks_ref[step : step + 1, :]
+        named = jnp.where(slot < counts_ref[step], picked, picked[:, :1])
+        down = jnp.sum(jnp.where(diagonal, named, 0), axis=1, keepdims=True)
+        select.append(jnp.where(column == down, 1.0, 0.0).astype(BF16))
+    select = jnp.concatenate(select, axis=0)
     copies[2].wait()
-    rounds, most = picks_ref.shape
-    column = lax.broadcasted_iota(jnp.int32, (1, points_ref.shape[0]), 1)
-    for step in range(rounds):
-        for slot in range(most):
-            named = jnp.where(slot < counts_ref[step], picks_ref[step, slot], picks_ref[step, 0])
-            row = step * most + slot
-            select_ref[row : row + 1, :] = jnp.where(column == named, 1.0, 0.0).astype(F32)
-    select = select_ref[...].astype(BF16)
-    copies[0].wait()
     cand = jnp.dot(select, points_ref[...], preferred_element_type=F32).astype(BF16)
     for place in range(out_ref.shape[0]):
         out_ref[place] = cand
@@ -48,10 +54,9 @@
         in_specs=[ANY, ANY, ANY],
         out_specs=VMEM,
         scratch_shapes=[
-            pltpu.SMEM(picks.shape, jnp.int32),
+            pltpu.VMEM(picks.shape, jnp.int32),
             pltpu.SMEM(counts.shape, jnp.int32),
             pltpu.VMEM(points.shape, BF16),
-            pltpu.VMEM((slots, rows), F32),
             pltpu.SemaphoreType.DMA((3,)),
         ],
         compiler_params=pltpu.CompilerParams(vmem_limit_bytes=60 * 1024 * 1024),
@@ -187,13 +192,12 @@
                 dist = jnp.maximum(value + length_ref[inner], 0.0)
                 if number == 0:
                     dist = jnp.minimum(dist, init_ref[...])
-                for copy in range(out_ref.shape[0]):
-                    out_ref[copy, step, pl.ds(place, 1), :] = dist
+                out_ref[step, pl.ds(place, 1), :] = dist
 
     slots = sum(cand.shape[0] * cand.shape[1] for cand in cands)
     return pl.pallas_call(
         body,
-        out_shape=jax.ShapeDtypeStruct((count, rounds, count, rows), F32),
+        out_shape=jax.ShapeDtypeStruct((rounds, count, rows), F32),
         in_specs=[SMEM] + [VMEM] * (len(turned) + len(lengths) + len(cands) + 2),
         out_specs=VMEM,
         scratch_shapes=[pltpu.VMEM((rounds, slots // rounds, LANES), F32)],
@@ -202,13 +206,16 @@
     )(places, *turned, *lengths, *cands, low, init_row)
 
 
-def total_kernel(place_ref, dist_ref, own_ref, total_ref):
-    rounds = dist_ref.shape[1]
+def total_kernel(place_ref, *refs):
+    dists, (own_ref, total_ref) = refs[:-2], refs[-2:]
+    rounds = dists[0].shape[0]
     lane = lax.broadcasted_iota(jnp.int32, total_ref.shape, 1)
     total = jnp.zeros(total_ref.shape, F32)
     current = None
     for step in range(rounds):
-        dist = jnp.min(dist_ref[:, step], axis=0)
+        dist = dists[0][step]
+        for dist_ref in dists[1:]:
+            dist = jnp.minimum(dist, dist_ref[step])
         current = dist if step == 0 else jnp.minimum(current, dist)
         total = jnp.where(lane == step, jnp.sum(current), total)
     total_ref[...] = total
@@ -219,17 +226,17 @@
     own_ref[...] = own
 
 
-def totals(places, dist, peers):
+def totals(places, dists, peers):
     return pl.pallas_call(
         total_kernel,
         out_shape=(
-            jax.ShapeDtypeStruct((1, dist.shape[3]), F32),
+            jax.ShapeDtypeStruct((1, dists[0].shape[2]), F32),
             jax.ShapeDtypeStruct((peers, LANES), F32),
         ),
-        in_specs=[SMEM, VMEM],
+        in_specs=[SMEM] + [VMEM] * len(dists),
         out_specs=(VMEM, VMEM),
         compiler_params=PARAMS,
-    )(places, dist)
+    )(places, *dists)
 
 
 def finish(own, shares, rounds, all_rows):
@@ -279,7 +286,7 @@
     low = near(turned, [opposite], low, rounds)
     last = [last]
     dist = last_near(places, turned, last, low, lengths, init_dist[None], rounds)
-    shared = lax.all_to_all(dist, "y", 0, 0, tiled=True)
+    shared = [dist] + [shift(dist, "y", subs, by) for by in (2, 1, 3)]
     own, total = totals(places, shared, lax.axis_size(("z", "x")))
     total = total + shift(total, "c", CORES, 1)
     shares = lax.all_to_all(total, ("z", "x"), 0, 0, tiled=True)

time: 69 us -> 66.4 us (0.962)
  blocking collectives: 20.6 us -> 12.3 us
  starting transfers between devices: 28.4 us -> 32.4 us
  waiting for transfers between devices: 6.4 us -> 8.13 us
    all_to_all x1 -> x0, blocking collectives: 7.87 us -> none  [shards(): shared = lax.all_to_all(dist, 'y', 0, 0, tiled=True)]
    ppermute x12 -> x15, starting transfers between devices: 20.2 us -> 24.2 us  [shift(): lax.ppermute(block, axis, [(i, (i + by) % size) for i in range(size)])]
    ppermute x12 -> x15, waiting for transfers between devices: 0.98 us -> 2.72 us  [shift(): lax.ppermute(block, axis, [(i, (i + by) % size) for i in range(size)])]
  transfers between devices with their start and end apart: 13 -> 16, of which waited for: 3 -> 5; matrix products, arithmetic and copies ran while one was open for 0% -> 0% of each run, Pallas kernels for 14% -> 14%
where the time goes in v4:
time: 66.4 us; the launch traced here: 66.2 us
  starting transfers between devices  32.4 us (49%)
  Pallas kernels  12.5 us (19%)
  blocking collectives  12.3 us (19%)
  waiting for transfers between devices  8.13 us (12%)
  between operations  0.78 us (1%)
    ppermute x15, starting transfers between devices, shift(): lax.ppermute(block, axis, [(i, (i + by) % size) for i in range(size)])  24.2 us
    all_to_all x1, blocking collectives, shards(): shares = lax.all_to_all(total, ('z', 'x'), 0, 0, tiled=True)  12.3 us
    all_to_all x1, starting transfers between devices, shards(): along_z = lax.all_to_all(cand, 'z', 0, 0, tiled=True)  8.2 us
    pallas_call x4, Pallas kernels, near(): pl.pallas_call(body, out_shape=jax.ShapeDtypeStruct((count, rounds, rows)...  6.72 us
    all_to_all x1, waiting for transfers between devices, shards(): along_z = lax.all_to_all(cand, 'z', 0, 0, tiled=True)  5.41 us
    ppermute x15, waiting for transfers between devices, shift(): lax.ppermute(block, axis, [(i, (i + by) % size) for i in range(size)])  2.72 us
    pallas_call x1, Pallas kernels, pick_rows(): pl.pallas_call(pick_kernel, out_shape=jax.ShapeDtypeStruct((copies, slots...  1.98 us
    pallas_call x1, Pallas kernels, last_near(): pl.pallas_call(body, out_shape=jax.ShapeDtypeStruct((rounds, count, rows)...  1.69 us
  transfers between devices with their start and end apart: 16, of which 5 were waited for; matrix products, arithmetic and copies ran while one was open for 0% of the time, Pallas kernels for 14%

profile of v4, /device:TPU:1, one launch (start us, length us, event | category | flops | bytes accessed | tf_op | source)
XLA Modules:
  0.0 66.2 jit_solution(2786369583960167207)
XLA Ops:
  0.6 2.2 %collective-permute-start = (bf16[1024,256]{1,0:T(8,128)(2,1)}, bf16[1024,256]{1,0:T(8,128)(2,1)S(1)}, u32[]{:S(2)}, u32[]{:S(2)}) collective-permute-start(bf16[1024,256]{1,0:T(8,128)(2,1)} %points_hbm.1), channel_id=1, source_target_pairs={{0,1},{1,2},{2,3},{3,0},{4,5},{5,6},{6,7},{7,4},{8,9},{9,10},{10,1... | collective-permute-start | bytes 1572872 | tf_op jit(solution)/shard_map/ppermute | solution.py:260
  2.8 1.5 %collective-permute-start.1 = (bf16[1024,256]{1,0:T(8,128)(2,1)}, bf16[1024,256]{1,0:T(8,128)(2,1)S(1)}, u32[]{:S(2)}, u32[]{:S(2)}) collective-permute-start(bf16[1024,256]{1,0:T(8,128)(2,1)} %points_hbm.1), channel_id=1, source_target_pairs={{0,3},{1,0},{2,1},{3,2},{4,7},{5,4},{6,5},{7,6},{8,11},{9,8},{10,9... | collective-permute-start | bytes 1572872 | tf_op jit(solution)/shard_map/ppermute | solution.py:260
  4.4 2.0 %shard_map.78 = bf16[8,48,256]{2,1,0:T(8,128)(2,1)} custom-call(s32[3,16]{1,0:T(4,128)} %picks_hbm.1, s32[3]{0:T(128)} %bitcast.12, bf16[1024,256]{1,0:T(8,128)(2,1)} %points_hbm.1), custom_call_target="tpu_custom_call" | custom-call | flops 25165824 | bytes 524288 | tf_op jit(solution)/shard_map/pallas_call | solution.py:51
  6.4 8.2 %all-to-all-start = ((bf16[8,48,256]{2,1,0:T(8,128)(2,1)}), bf16[8,48,256]{2,1,0:T(8,128)(2,1)S(1)}, u32[]{:S(2)}, u32[]{:S(2)}) async-start(bf16[8,48,256]{2,1,0:T(8,128)(2,1)} %shard_map.78), calls=%async_computation | async-start | bytes 393216 | tf_op jit(solution)/shard_map/all_to_all | solution.py:273
  14.6 1.2 %collective-permute-start.2 = (bf16[512,256]{1,0:T(8,128)(2,1)S(1)}, bf16[512,256]{1,0:T(8,128)(2,1)S(1)}, u32[]{:S(2)}, u32[]{:S(2)}) collective-permute-start(bf16[512,256]{1,0:T(8,128)(2,1)S(1)} %slice.8), channel_id=1, source_target_pairs={{0,1},{1,2},{2,3},{3,0},{4,5},{5,6},{6,7},{7,4},{8,9},{9,10},{10,1... | collective-permute-start | bytes 786440 | tf_op jit(solution)/shard_map/ppermute | solution.py:260
  15.8 1.7 %collective-permute-start.3 = (bf16[512,256]{1,0:T(8,128)(2,1)S(1)}, bf16[512,256]{1,0:T(8,128)(2,1)S(1)}, u32[]{:S(2)}, u32[]{:S(2)}) collective-permute-start(bf16[512,256]{1,0:T(8,128)(2,1)S(1)} %slice.9), channel_id=1, source_target_pairs={{0,3},{1,0},{2,1},{3,2},{4,7},{5,4},{6,5},{7,6},{8,11},{9,8},{10,9... | collective-permute-start | bytes 786440 | tf_op jit(solution)/shard_map/ppermute | solution.py:260
  17.5 5.4 %all-to-all-done.refs_2_ = bf16[8,48,256]{2,1,0:T(8,128)(2,1)S(1)} async-done(((bf16[8,48,256]{2,1,0:T(8,128)(2,1)}), bf16[8,48,256]{2,1,0:T(8,128)(2,1)S(1)}, u32[]{:S(2)}, u32[]{:S(2)}) %all-to-all-start) | async-done | bytes 196640 | tf_op jit(solution)/shard_map/all_to_all | solution.py:273
  22.9 1.2 %collective-permute-start.5 = (bf16[8,48,256]{2,1,0:T(8,128)(2,1)S(1)}, bf16[8,48,256]{2,1,0:T(8,128)(2,1)S(1)}, u32[]{:S(2)}, u32[]{:S(2)}) collective-permute-start(bf16[8,48,256]{2,1,0:T(8,128)(2,1)S(1)} %all-to-all-done.refs_2_), channel_id=1, source_target_pairs={{0,8},{8,16},{16,24},{24,0},{1,9},{9,17},{17,25},{25,1},{2,10},{10... | collective-permute-start | bytes 589832 | tf_op jit(solution)/shard_map/ppermute | solution.py:260
  24.1 1.5 %collective-permute-start.7 = (bf16[8,48,256]{2,1,0:T(8,128)(2,1)S(1)}, bf16[8,48,256]{2,1,0:T(8,128)(2,1)S(1)}, u32[]{:S(2)}, u32[]{:S(2)}) collective-permute-start(bf16[8,48,256]{2,1,0:T(8,128)(2,1)S(1)} %all-to-all-done.refs_2_), channel_id=1, source_target_pairs={{0,24},{8,0},{16,8},{24,16},{1,25},{9,1},{17,9},{25,17},{2,26},{10... | collective-permute-start | bytes 589832 | tf_op jit(solution)/shard_map/ppermute | solution.py:260
  25.6 3.6 %collective-permute-start.9 = (bf16[8,48,256]{2,1,0:T(8,128)(2,1)S(1)}, bf16[8,48,256]{2,1,0:T(8,128)(2,1)S(1)}, u32[]{:S(2)}, u32[]{:S(2)}) collective-permute-start(bf16[8,48,256]{2,1,0:T(8,128)(2,1)S(1)} %all-to-all-done.refs_2_), channel_id=1, source_target_pairs={{0,4},{4,0},{1,5},{5,1},{2,6},{6,2},{3,7},{7,3},{8,12},{12,8},{9,1... | collective-permute-start | bytes 589832 | tf_op jit(solution)/shard_map/ppermute | solution.py:260
  29.2 0.5 shard_map.76
  29.8 1.6 %collective-permute-start.4 = (bf16[8,48,256]{2,1,0:T(8,128)(2,1)S(1)}, bf16[8,48,256]{2,1,0:T(8,128)(2,1)S(1)}, u32[]{:S(2)}, u32[]{:S(2)}) collective-permute-start(bf16[8,48,256]{2,1,0:T(8,128)(2,1)S(1)} %all-to-all-done.refs_2_), channel_id=1, source_target_pairs={{0,16},{8,24},{16,0},{24,8},{1,17},{9,25},{17,1},{25,9},{2,18},{10... | collective-permute-start | bytes 589832 | tf_op jit(solution)/shard_map/ppermute | solution.py:260
  31.4 3.3 %collective-permute-start.6 = (bf16[8,48,256]{2,1,0:T(8,128)(2,1)S(1)}, bf16[8,48,256]{2,1,0:T(8,128)(2,1)S(1)}, u32[]{:S(2)}, u32[]{:S(2)}) collective-permute-start(bf16[8,48,256]{2,1,0:T(8,128)(2,1)S(1)} %collective-permute-done.5.refs_2_), channel_id=1, source_target_pairs={{0,4},{4,0},{1,5},{5,1},{2,6},{6,2},{3,7},{7,3},{8,12},{12,8},{9,1... | collective-permute-start | bytes 589832 | tf_op jit(solution)/shard_map/ppermute | solution.py:260
  34.7 0.3 collective-permute-start.8
  35.0 0.2 shard_map.77
  35.2 1.9 %shard_map.79.refs_4_ = f32[4,3,1024]{2,1,0:T(4,128)S(1)} custom-call(bf16[3,256,1024]{2,1,0:T(8,128)(2,1)S(1)} %get-tuple-element.14.refs_0_, bf16[1,256,1024]{2,1,0:T(8,128)(2,1)S(1)} %get-tuple-element.15.refs_1_, bf16[8,48,256]{2,1,0:T(8,128)(2,1)S(1)} %all-to-all-done.refs_2_, bf16[8,48,256]{2,1,0:T(8,128)(2,1)S(1)} %collective-permute-done.9.refs_3_), custom_call_target="tpu_custom_call" | custom-call | flops 1610612736 | bytes 2490368 | tf_op jit(solution)/shard_map/pallas_call | solution.py:166
  37.1 1.9 %shard_map.80.refs_4_ = f32[4,3,1024]{2,1,0:T(4,128)S(1)} custom-call(bf16[3,256,1024]{2,1,0:T(8,128)(2,1)S(1)} %get-tuple-element.14.refs_0_, bf16[1,256,1024]{2,1,0:T(8,128)(2,1)S(1)} %get-tuple-element.15.refs_1_, bf16[8,48,256]{2,1,0:T(8,128)(2,1)S(1)} %collective-permute-done.5.refs_2_, bf16[8,48,256]{2,1,0:T(8,128)(2,1)S(1)} %collective-permute-done.7.refs_3_, ...), custom_call_target="tpu_custom_call" | custom-call | flops 1610612736 | bytes 2490368 | tf_op jit(solution)/shard_map/pallas_call | solution.py:166
  39.0 1.9 %shard_map.81.refs_3_ = f32[4,3,1024]{2,1,0:T(4,128)S(1)} custom-call(bf16[3,256,1024]{2,1,0:T(8,128)(2,1)S(1)} %get-tuple-element.14.refs_0_, bf16[1,256,1024]{2,1,0:T(8,128)(2,1)S(1)} %get-tuple-element.15.refs_1_, bf16[8,48,256]{2,1,0:T(8,128)(2,1)S(1)} %collective-permute-done.6.refs_2_, bf16[8,48,256]{2,1,0:T(8,128)(2,1)S(1)} %collective-permute-done.8.refs_3_, ...), custom_call_target="tpu_custom_call" | custom-call | flops 1610612736 | bytes 2490368 | tf_op jit(solution)/shard_map/pallas_call | solution.py:166
  40.9 0.3 collective-permute-start.10
  41.3 1.1 %shard_map.82.refs_5_ = f32[4,3,1024]{2,1,0:T(4,128)S(1)} custom-call(bf16[3,256,1024]{2,1,0:T(8,128)(2,1)S(1)} %get-tuple-element.14.refs_0_, bf16[1,256,1024]{2,1,0:T(8,128)(2,1)S(1)} %get-tuple-element.15.refs_1_, bf16[8,48,256]{2,1,0:T(8,128)(2,1)S(1)} %collective-permute-done.4.refs_2_, f32[4,3,1024]{2,1,0:T(4,128)S(1)} %shard_map.81.refs_3_), custom_call_target="tpu_custom_call" | custom-call | flops 805306368 | bytes 2293760 | tf_op jit(solution)/shard_map/pallas_call | solution.py:166
  42.3 0.1 collective-permute-done.10.refs_4_
  42.5 1.7 %shard_map.83.refs_0_ = f32[3,4,1024]{2,1,0:T(4,128)S(1)} custom-call(s32[4]{0:T(128)S(1)} %and_select_fusion.place_ref, bf16[3,256,1024]{2,1,0:T(8,128)(2,1)S(1)} %get-tuple-element.14.refs_0_, bf16[1,256,1024]{2,1,0:T(8,128)(2,1)S(1)} %get-tuple-element.15.refs_1_, f32[3,1,1024]{2,1,0:T(1,128)S(1)} %get-tuple-element.16.refs_2_, ...), custom_call_target="tpu_custom_call" | custom-call | flops 805306368 | bytes 2293760 | tf_op jit(solution)/shard_map/pallas_call | solution.py:198
  44.1 1.6 %collective-permute-start.11 = (f32[3,4,1024]{2,1,0:T(4,128)S(1)}, f32[3,4,1024]{2,1,0:T(4,128)S(1)}, u32[]{:S(2)}, u32[]{:S(2)}) collective-permute-start(f32[3,4,1024]{2,1,0:T(4,128)S(1)} %shard_map.83.refs_0_), channel_id=1, source_target_pairs={{0,2},{1,3},{2,0},{3,1},{4,6},{5,7},{6,4},{7,5},{8,10},{9,11},{10,... | collective-permute-start | bytes 147464 | tf_op jit(solution)/shard_map/ppermute | solution.py:260
  45.8 0.4 collective-permute-start.12
  46.2 2.3 %collective-permute-start.13 = (f32[3,4,1024]{2,1,0:T(4,128)S(1)}, f32[3,4,1024]{2,1,0:T(4,128)S(1)}, u32[]{:S(2)}, u32[]{:S(2)}) collective-permute-start(f32[3,4,1024]{2,1,0:T(4,128)S(1)} %shard_map.83.refs_0_), channel_id=1, source_target_pairs={{0,3},{1,0},{2,1},{3,2},{4,7},{5,4},{6,5},{7,6},{8,11},{9,8},{10,9... | collective-permute-start | bytes 147464 | tf_op jit(solution)/shard_map/ppermute | solution.py:260
  48.5 0.2 collective-permute-done.11.refs_1_
  48.7 1.5 %collective-permute-done.12.refs_2_ = f32[3,4,1024]{2,1,0:T(4,128)S(1)} collective-permute-done((f32[3,4,1024]{2,1,0:T(4,128)S(1)}, f32[3,4,1024]{2,1,0:T(4,128)S(1)}, u32[]{:S(2)}, u32[]{:S(2)}) %collective-permute-start.12) | collective-permute-done | bytes 49184 | tf_op jit(solution)/shard_map/ppermute | solution.py:260
  50.2 0.7 %shard_map.84 = (f32[1,1024]{1,0:T(1,128)S(1)}, f32[32,128]{1,0:T(8,128)S(1)}) custom-call(s32[4]{0:T(128)S(1)} %and_select_fusion.place_ref, f32[3,4,1024]{2,1,0:T(4,128)S(1)} %shard_map.83.refs_0_, f32[3,4,1024]{2,1,0:T(4,128)S(1)} %collective-permute-done.11.refs_1_, f32[3,4,1024]{2,1,0:T(4,128)S(1)} %collective-permute-done.12.refs_2_, ...), custom_call_target="tpu_custom_call" | custom-call | tf_op jit(solution)/shard_map/pallas_call | solution.py:230
  50.9 1.5 %collective-permute-start.14 = (f32[32,128]{1,0:T(8,128)S(1)}, f32[32,128]{1,0:T(8,128)S(1)}, u32[]{:S(2)}, u32[]{:S(2)}) collective-permute-start(f32[32,128]{1,0:T(8,128)S(1)} %get-tuple-element.21), channel_id=1, source_target_pairs={{0,4},{4,0},{1,5},{5,1},{2,6},{6,2},{3,7},{7,3},{8,12},{12,8},{9,1... | collective-permute-start | bytes 49160 | tf_op jit(solution)/shard_map/ppermute | solution.py:260
  52.4 0.8 %collective-permute-done.14 = f32[32,128]{1,0:T(8,128)S(1)} collective-permute-done((f32[32,128]{1,0:T(8,128)S(1)}, f32[32,128]{1,0:T(8,128)S(1)}, u32[]{:S(2)}, u32[]{:S(2)}) %collective-permute-start.14) | collective-permute-done | bytes 16416 | tf_op jit(solution)/shard_map/ppermute | solution.py:260
  53.2 12.3 %all_to_all.16 = f32[32,1,128]{2,1,0:T(1,128)S(1)} all-to-all(f32[32,1,128]{2,1,0:T(1,128)S(1)} %bitcast.11), channel_id=1, replica_groups=mesh['z'=8,'x'=4,'c'=2,'y'=4] {'z','x'}, dimensions={0} | all-to-all | bytes 32768 | tf_op jit(solution)/shard_map/all_to_all | solution.py:292
  65.5 0.7 %shard_map.85 = (f32[1,1024]{1,0:T(1,128)}, f32[1,1024]{1,0:T(1,128)}, f32[1,3]{1,0:T(1,128)}) custom-call(f32[1,1024]{1,0:T(1,128)S(1)} %get-tuple-element.20.own_ref, f32[32,128]{1,0:T(8,128)S(1)} %bitcast.9), custom_call_target="tpu_custom_call" | custom-call | tf_op jit(solution)/shard_map/pallas_call | solution.py:250
  (21 shorter events, 0.1 us)
Async XLA Ops:
  0.6 28.6 %copy-start = (bf16[1024,256]{1,0:T(8,128)(2,1)S(1)}, bf16[1024,256]{1,0:T(8,128)(2,1)}, u32[]{:S(2)}) copy-start(bf16[1024,256]{1,0:T(8,128)(2,1)} %points_hbm.1) | copy-start | bytes 1572868
  0.6 13.9 %collective-permute-start = (bf16[1024,256]{1,0:T(8,128)(2,1)}, bf16[1024,256]{1,0:T(8,128)(2,1)S(1)}, u32[]{:S(2)}, u32[]{:S(2)}) collective-permute-start(bf16[1024,256]{1,0:T(8,128)(2,1)} %points_hbm.1), channel_id=1, source_target_pairs={{0,1},{1,2},{2,3},{3,0},{4,5},{5,6},{6,7},{7,4},{8,9},{9,10},{10,1... | collective-permute-start | bytes 1572872 | tf_op jit(solution)/shard_map/ppermute | solution.py:260
  2.8 12.9 %collective-permute-start.1 = (bf16[1024,256]{1,0:T(8,128)(2,1)}, bf16[1024,256]{1,0:T(8,128)(2,1)S(1)}, u32[]{:S(2)}, u32[]{:S(2)}) collective-permute-start(bf16[1024,256]{1,0:T(8,128)(2,1)} %points_hbm.1), channel_id=1, source_target_pairs={{0,3},{1,0},{2,1},{3,2},{4,7},{5,4},{6,5},{7,6},{8,11},{9,8},{10,9... | collective-permute-start | bytes 1572872 | tf_op jit(solution)/shard_map/ppermute | solution.py:260
  6.4 16.6 %all-to-all-start = ((bf16[8,48,256]{2,1,0:T(8,128)(2,1)}), bf16[8,48,256]{2,1,0:T(8,128)(2,1)S(1)}, u32[]{:S(2)}, u32[]{:S(2)}) async-start(bf16[8,48,256]{2,1,0:T(8,128)(2,1)} %shard_map.78), calls=%async_computation | async-start | bytes 393216 | tf_op jit(solution)/shard_map/all_to_all | solution.py:273
  14.6 20.1 %collective-permute-start.2 = (bf16[512,256]{1,0:T(8,128)(2,1)S(1)}, bf16[512,256]{1,0:T(8,128)(2,1)S(1)}, u32[]{:S(2)}, u32[]{:S(2)}) collective-permute-start(bf16[512,256]{1,0:T(8,128)(2,1)S(1)} %slice.8), channel_id=1, source_target_pairs={{0,1},{1,2},{2,3},{3,0},{4,5},{5,6},{6,7},{7,4},{8,9},{9,10},{10,1... | collective-permute-start | bytes 786440 | tf_op jit(solution)/shard_map/ppermute | solution.py:260
  15.8 19.2 %collective-permute-start.3 = (bf16[512,256]{1,0:T(8,128)(2,1)S(1)}, bf16[512,256]{1,0:T(8,128)(2,1)S(1)}, u32[]{:S(2)}, u32[]{:S(2)}) collective-permute-start(bf16[512,256]{1,0:T(8,128)(2,1)S(1)} %slice.9), channel_id=1, source_target_pairs={{0,3},{1,0},{2,1},{3,2},{4,7},{5,4},{6,5},{7,6},{8,11},{9,8},{10,9... | collective-permute-start | bytes 786440 | tf_op jit(solution)/shard_map/ppermute | solution.py:260
  22.9 6.8 %collective-permute-start.5 = (bf16[8,48,256]{2,1,0:T(8,128)(2,1)S(1)}, bf16[8,48,256]{2,1,0:T(8,128)(2,1)S(1)}, u32[]{:S(2)}, u32[]{:S(2)}) collective-permute-start(bf16[8,48,256]{2,1,0:T(8,128)(2,1)S(1)} %all-to-all-done.refs_2_), channel_id=1, source_target_pairs={{0,8},{8,16},{16,24},{24,0},{1,9},{9,17},{17,25},{25,1},{2,10},{10... | collective-permute-start | bytes 589832 | tf_op jit(solution)/shard_map/ppermute | solution.py:260
  24.1 7.3 %collective-permute-start.7 = (bf16[8,48,256]{2,1,0:T(8,128)(2,1)S(1)}, bf16[8,48,256]{2,1,0:T(8,128)(2,1)S(1)}, u32[]{:S(2)}, u32[]{:S(2)}) collective-permute-start(bf16[8,48,256]{2,1,0:T(8,128)(2,1)S(1)} %all-to-all-done.refs_2_), channel_id=1, source_target_pairs={{0,24},{8,0},{16,8},{24,16},{1,25},{9,1},{17,9},{25,17},{2,26},{10... | collective-permute-start | bytes 589832 | tf_op jit(solution)/shard_map/ppermute | solution.py:260
  25.6 9.6 %collective-permute-start.9 = (bf16[8,48,256]{2,1,0:T(8,128)(2,1)S(1)}, bf16[8,48,256]{2,1,0:T(8,128)(2,1)S(1)}, u32[]{:S(2)}, u32[]{:S(2)}) collective-permute-start(bf16[8,48,256]{2,1,0:T(8,128)(2,1)S(1)} %all-to-all-done.refs_2_), channel_id=1, source_target_pairs={{0,4},{4,0},{1,5},{5,1},{2,6},{6,2},{3,7},{7,3},{8,12},{12,8},{9,1... | collective-permute-start | bytes 589832 | tf_op jit(solution)/shard_map/ppermute | solution.py:260
  29.8 11.1 %collective-permute-start.4 = (bf16[8,48,256]{2,1,0:T(8,128)(2,1)S(1)}, bf16[8,48,256]{2,1,0:T(8,128)(2,1)S(1)}, u32[]{:S(2)}, u32[]{:S(2)}) collective-permute-start(bf16[8,48,256]{2,1,0:T(8,128)(2,1)S(1)} %all-to-all-done.refs_2_), channel_id=1, source_target_pairs={{0,16},{8,24},{16,0},{24,8},{1,17},{9,25},{17,1},{25,9},{2,18},{10... | collective-permute-start | bytes 589832 | tf_op jit(solution)/shard_map/ppermute | solution.py:260
  31.4 7.6 %collective-permute-start.6 = (bf16[8,48,256]{2,1,0:T(8,128)(2,1)S(1)}, bf16[8,48,256]{2,1,0:T(8,128)(2,1)S(1)}, u32[]{:S(2)}, u32[]{:S(2)}) collective-permute-start(bf16[8,48,256]{2,1,0:T(8,128)(2,1)S(1)} %collective-permute-done.5.refs_2_), channel_id=1, source_target_pairs={{0,4},{4,0},{1,5},{5,1},{2,6},{6,2},{3,7},{7,3},{8,12},{12,8},{9,1... | collective-permute-start | bytes 589832 | tf_op jit(solution)/shard_map/ppermute | solution.py:260
  34.7 4.3 %collective-permute-start.8 = (bf16[8,48,256]{2,1,0:T(8,128)(2,1)S(1)}, bf16[8,48,256]{2,1,0:T(8,128)(2,1)S(1)}, u32[]{:S(2)}, u32[]{:S(2)}) collective-permute-start(bf16[8,48,256]{2,1,0:T(8,128)(2,1)S(1)} %collective-permute-done.7.refs_3_), channel_id=1, source_target_pairs={{0,4},{4,0},{1,5},{5,1},{2,6},{6,2},{3,7},{7,3},{8,12},{12,8},{9,1... | collective-permute-start | bytes 589832 | tf_op jit(solution)/shard_map/ppermute | solution.py:260
  39.0 2.3 %copy-start.2 = (s32[4]{0:T(128)S(1)}, s32[4]{0:T(128)}, u32[]{:S(2)}) copy-start(s32[4]{0:T(128)} %constant.21.clone) | copy-start | bytes 52
  40.9 1.6 %copy-start.1 = (f32[1024]{0:T(1024)S(1)}, f32[1024]{0:T(1024)}, u32[]{:S(2)}) copy-start(f32[1024]{0:T(1024)} %param.6) | copy-start | bytes 12292
  40.9 1.5 %collective-permute-start.10 = (bf16[8,48,256]{2,1,0:T(8,128)(2,1)S(1)}, bf16[8,48,256]{2,1,0:T(8,128)(2,1)S(1)}, u32[]{:S(2)}, u32[]{:S(2)}) collective-permute-start(bf16[8,48,256]{2,1,0:T(8,128)(2,1)S(1)} %collective-permute-done.4.refs_2_), channel_id=1, source_target_pairs={{0,4},{4,0},{1,5},{5,1},{2,6},{6,2},{3,7},{7,3},{8,12},{12,8},{9,1... | collective-permute-start | bytes 589832 | tf_op jit(solution)/shard_map/ppermute | solution.py:260
  44.1 4.5 %collective-permute-start.11 = (f32[3,4,1024]{2,1,0:T(4,128)S(1)}, f32[3,4,1024]{2,1,0:T(4,128)S(1)}, u32[]{:S(2)}, u32[]{:S(2)}) collective-permute-start(f32[3,4,1024]{2,1,0:T(4,128)S(1)} %shard_map.83.refs_0_), channel_id=1, source_target_pairs={{0,2},{1,3},{2,0},{3,1},{4,6},{5,7},{6,4},{7,5},{8,10},{9,11},{10,... | collective-permute-start | bytes 147464 | tf_op jit(solution)/shard_map/ppermute | solution.py:260
  45.8 4.4 %collective-permute-start.12 = (f32[3,4,1024]{2,1,0:T(4,128)S(1)}, f32[3,4,1024]{2,1,0:T(4,128)S(1)}, u32[]{:S(2)}, u32[]{:S(2)}) collective-permute-start(f32[3,4,1024]{2,1,0:T(4,128)S(1)} %shard_map.83.refs_0_), channel_id=1, source_target_pairs={{0,1},{1,2},{2,3},{3,0},{4,5},{5,6},{6,7},{7,4},{8,9},{9,10},{10,1... | collective-permute-start | bytes 147464 | tf_op jit(solution)/shard_map/ppermute | solution.py:260
  46.2 4.0 %collective-permute-start.13 = (f32[3,4,1024]{2,1,0:T(4,128)S(1)}, f32[3,4,1024]{2,1,0:T(4,128)S(1)}, u32[]{:S(2)}, u32[]{:S(2)}) collective-permute-start(f32[3,4,1024]{2,1,0:T(4,128)S(1)} %shard_map.83.refs_0_), channel_id=1, source_target_pairs={{0,3},{1,0},{2,1},{3,2},{4,7},{5,4},{6,5},{7,6},{8,11},{9,8},{10,9... | collective-permute-start | bytes 147464 | tf_op jit(solution)/shard_map/ppermute | solution.py:260
  50.9 2.4 %collective-permute-start.14 = (f32[32,128]{1,0:T(8,128)S(1)}, f32[32,128]{1,0:T(8,128)S(1)}, u32[]{:S(2)}, u32[]{:S(2)}) collective-permute-start(f32[32,128]{1,0:T(8,128)S(1)} %get-tuple-element.21), channel_id=1, source_target_pairs={{0,4},{4,0},{1,5},{5,1},{2,6},{6,2},{3,7},{7,3},{8,12},{12,8},{9,1... | collective-permute-start | bytes 49160 | tf_op jit(solution)/shard_map/ppermute | solution.py:260

commit v5 on v4

--- a/solution.py
+++ b/solution.py
@@ -8,6 +8,7 @@
 CHIPS_Z, CHIPS_X, CORES = 8, 4, 2
 PART = 256
 LANES = 128
+PLACES = (0, 3, 1, 2)
 F32, BF16 = jnp.float32, jnp.bfloat16
 VMEM = pl.BlockSpec(memory_space=pltpu.VMEM)
 ANY = pl.BlockSpec(memory_space=pl.ANY)
@@ -115,12 +116,15 @@
             base += rows
 
 
-def lowest(weights, cands, sq_ref, step, rounds):
+def lowest(weights, cands, sq_ref, step, rounds, skipped=0):
     count = weights.shape[1]
     best = None
     base = 0
-    for cand_ref in cands:
+    for order, cand_ref in enumerate(cands):
         values = half_round(cand_ref, step, rounds)
+        if order < skipped:
+            base += values.shape[0]
+            continue
         for part in range(0, values.shape[0], PART):
             piece = values[part : part + PART]
             size = piece.shape[0]
@@ -146,7 +150,7 @@
     )
 
 
-def near(turned, cands, low, rounds):
+def near(turned, cands, low, rounds, done=0):
     count, rows = sum(block.shape[0] for block in turned), turned[0].shape[2]
 
     def body(*refs):
@@ -155,9 +159,11 @@
         out_ref, sq_ref = refs[-2:]
         squares_of(cand_refs, sq_ref, rounds)
         for place, (ref, number) in enumerate(blocks_of(turned_refs)):
+            known = low is not None and place < low.shape[0]
+            skipped = done if known else 0
             for step in range(rounds):
-                value = lowest(ref[number], cand_refs, sq_ref, step, rounds)
-                if low is not None:
+                value = lowest(ref[number], cand_refs, sq_ref, step, rounds, skipped)
+                if known:
                     value = jnp.minimum(value, refs[0][place, step : step + 1, :])
                 out_ref[place, step : step + 1, :] = value
 
@@ -174,10 +180,10 @@
     )(*turned, *cands, *extra)
 
 
-def last_near(places, turned, cands, low, lengths, init_row, rounds):
+def last_near(turned, cands, low, lengths, init_row, rounds):
     count, rows = sum(block.shape[0] for block in turned), turned[0].shape[2]
 
-    def body(place_ref, *refs):
+    def body(*refs):
         turned_refs, refs = refs[: len(turned)], refs[len(turned) :]
         length_refs, refs = refs[: len(turned)], refs[len(turned) :]
         cand_refs, refs = refs[: len(cands)], refs[len(cands) :]
@@ -185,58 +191,56 @@
         squares_of(cand_refs, sq_ref, rounds)
         blocks = zip(blocks_of(turned_refs), blocks_of(length_refs))
         for number, ((ref, inner), (length_ref, _)) in enumerate(blocks):
-            place = place_ref[number]
             for step in range(rounds):
                 value = lowest(ref[inner], cand_refs, sq_ref, step, rounds)
                 value = jnp.minimum(value, low_ref[number, step : step + 1, :])
                 dist = jnp.maximum(value + length_ref[inner], 0.0)
                 if number == 0:
                     dist = jnp.minimum(dist, init_ref[...])
-                out_ref[step, pl.ds(place, 1), :] = dist
+                out_ref[step, number : number + 1, :] = dist
 
     slots = sum(cand.shape[0] * cand.shape[1] for cand in cands)
     return pl.pallas_call(
         body,
         out_shape=jax.ShapeDtypeStruct((rounds, count, rows), F32),
-        in_specs=[SMEM] + [VMEM] * (len(turned) + len(lengths) + len(cands) + 2),
+        in_specs=[VMEM] * (len(turned) + len(lengths) + len(cands) + 2),
         out_specs=VMEM,
         scratch_shapes=[pltpu.VMEM((rounds, slots // rounds, LANES), F32)],
         compiler_params=PARAMS,
         cost_estimate=near_cost(turned, cands),
-    )(places, *turned, *lengths, *cands, low, init_row)
-
-
-def total_kernel(place_ref, *refs):
-    dists, (own_ref, total_ref) = refs[:-2], refs[-2:]
-    rounds = dists[0].shape[0]
-    lane = lax.broadcasted_iota(jnp.int32, total_ref.shape, 1)
-    total = jnp.zeros(total_ref.shape, F32)
-    current = None
-    for step in range(rounds):
-        dist = dists[0][step]
-        for dist_ref in dists[1:]:
-            dist = jnp.minimum(dist, dist_ref[step])
-        current = dist if step == 0 else jnp.minimum(current, dist)
-        total = jnp.where(lane == step, jnp.sum(current), total)
-    total_ref[...] = total
-    mine = place_ref[0]
-    own = current[0:1]
-    for number in range(1, current.shape[0]):
-        own = jnp.where(mine == number, current[number : number + 1], own)
-    own_ref[...] = own
-
-
-def totals(places, dists, peers):
-    return pl.pallas_call(
-        total_kernel,
+    )(*turned, *lengths, *cands, low, init_row)
+
+
+def totals(dists, shifts, peers):
+    rounds, count, rows = dists[0].shape
+
+    def body(*refs):
+        dist_refs, (own_ref, total_ref) = refs[: len(dists)], refs[len(dists) :]
+        lane = lax.broadcasted_iota(jnp.int32, total_ref.shape, 1)
+        total = jnp.zeros(total_ref.shape, F32)
+        current = [None] * count
+        for step in range(rounds):
+            for number in range(count):
+                for ref, by in zip(dist_refs, (0, *shifts)):
+                    there = PLACES.index((PLACES[number] + by) % count)
+                    dist = ref[step, there : there + 1, :]
+                    best = current[number]
+                    current[number] = dist if best is None else jnp.minimum(best, dist)
+            cost = jnp.sum(sum(current), axis=1, keepdims=True)
+            total = jnp.where(lane == step, cost, total)
+        total_ref[...] = total
+        own_ref[...] = current[0]
+
+    return pl.pallas_call(
+        body,
         out_shape=(
-            jax.ShapeDtypeStruct((1, dists[0].shape[2]), F32),
+            jax.ShapeDtypeStruct((1, rows), F32),
             jax.ShapeDtypeStruct((peers, LANES), F32),
         ),
-        in_specs=[SMEM] + [VMEM] * len(dists),
+        in_specs=[VMEM] * len(dists),
         out_specs=(VMEM, VMEM),
         compiler_params=PARAMS,
-    )(places, *dists)
+    )(*dists)
 
 
 def finish(own, shares, rounds, all_rows):
@@ -264,11 +268,9 @@
     rounds, most = picks.shape
     rows, width = points.shape
     subs = lax.axis_size("y")
-    sub = lax.axis_index("y").astype(jnp.int32)
     half = rows // 2
     behind, ahead = (shift(points, "y", subs, by) for by in (1, 3))
     across = [shift(behind[:half], "y", subs, 1), shift(ahead[half:], "y", subs, 3)]
-    places = (sub + jnp.array([0, 3, 1, 2], jnp.int32)) % subs
     cand = pick_rows(picks, pick_counts.reshape(-1), points, CHIPS_Z)
     along_z = lax.all_to_all(cand, "z", 0, 0, tiled=True)
     from_x = [shift(along_z, "x", CHIPS_X, by) for by in (2, 1, 3)]
@@ -277,7 +279,8 @@
     near_turned, near_lengths = turn([points, behind, ahead], rows)
     far_turned, far_lengths = turn(across, rows)
     turned, lengths = [near_turned, far_turned], [near_lengths, far_lengths]
-    low = near(turned, [along_z, swapped], None, rounds)
+    low = near([near_turned], [along_z], None, rounds)
+    low = near(turned, [along_z, swapped], low, rounds, 1)
     beside = [shift(piece, "c", CORES, 1) for piece in (after, before)]
     low = near(turned, [after, before], low, rounds)
     low = near(turned, beside, low, rounds)
@@ -285,9 +288,9 @@
     last = shift(opposite, "c", CORES, 1)
     low = near(turned, [opposite], low, rounds)
     last = [last]
-    dist = last_near(places, turned, last, low, lengths, init_dist[None], rounds)
+    dist = last_near(turned, last, low, lengths, init_dist[None], rounds)
     shared = [dist] + [shift(dist, "y", subs, by) for by in (2, 1, 3)]
-    own, total = totals(places, shared, lax.axis_size(("z", "x")))
+    own, total = totals(shared, (2, 1, 3), lax.axis_size(("z", "x")))
     total = total + shift(total, "c", CORES, 1)
     shares = lax.all_to_all(total, ("z", "x"), 0, 0, tiled=True)
     all_rows = float(rows * lax.axis_size(("z", "x", "c", "y")))

time: 66.4 us -> 64.7 us (0.974)
  starting transfers between devices: 32.4 us -> 31.5 us
  Pallas kernels: 12.5 us -> 11.7 us
    ppermute x15, starting transfers between devices: 24.2 us -> 23.3 us  [shift(): lax.ppermute(block, axis, [(i, (i + by) % size) for i in range(size)])]
    pallas_call x4 -> x5, Pallas kernels: 6.72 us -> 7.06 us  [near(): pl.pallas_call(body, out_shape=jax.ShapeDtypeStruct((count, rounds, rows)...]
  transfers between devices with their start and end apart: 16 -> 16, of which waited for: 5 -> 5; matrix products, arithmetic and copies ran while one was open for 0% -> 0% of each run, Pallas kernels for 14% -> 15%
where the time goes in v5:
time: 64.7 us; the launch traced here: 64.5 us
  starting transfers between devices  31.5 us (49%)
  blocking collectives  12.3 us (19%)
  Pallas kernels  11.7 us (18%)
  waiting for transfers between devices  8.13 us (13%)
  between operations  0.76 us (1%)
    ppermute x15, starting transfers between devices, shift(): lax.ppermute(block, axis, [(i, (i + by) % size) for i in range(size)])  23.3 us
    all_to_all x1, blocking collectives, shards(): shares = lax.all_to_all(total, ('z', 'x'), 0, 0, tiled=True)  12.3 us
    all_to_all x1, starting transfers between devices, shards(): along_z = lax.all_to_all(cand, 'z', 0, 0, tiled=True)  8.2 us
    pallas_call x5, Pallas kernels, near(): pl.pallas_call(body, out_shape=jax.ShapeDtypeStruct((count, rounds, rows)...  7.06 us
    all_to_all x1, waiting for transfers between devices, shards(): along_z = lax.all_to_all(cand, 'z', 0, 0, tiled=True)  5.42 us
    ppermute x15, waiting for transfers between devices, shift(): lax.ppermute(block, axis, [(i, (i + by) % size) for i in range(size)])  2.71 us
    pallas_call x1, Pallas kernels, pick_rows(): pl.pallas_call(pick_kernel, out_shape=jax.ShapeDtypeStruct((copies, slots...  1.98 us
  transfers between devices with their start and end apart: 16, of which 5 were waited for; matrix products, arithmetic and copies ran while one was open for 0% of the time, Pallas kernels for 15%

profile of v5, /device:TPU:1, one launch (start us, length us, event | category | flops | bytes accessed | tf_op | source)
XLA Modules:
  0.0 64.5 jit_solution(17448220810864985651)
XLA Ops:
  0.6 2.2 %collective-permute-start = (bf16[1024,256]{1,0:T(8,128)(2,1)}, bf16[1024,256]{1,0:T(8,128)(2,1)S(1)}, u32[]{:S(2)}, u32[]{:S(2)}) collective-permute-start(bf16[1024,256]{1,0:T(8,128)(2,1)} %points_hbm.1), channel_id=1, source_target_pairs={{0,1},{1,2},{2,3},{3,0},{4,5},{5,6},{6,7},{7,4},{8,9},{9,10},{10,1... | collective-permute-start | bytes 1572872 | tf_op jit(solution)/shard_map/ppermute | solution.py:264
  2.8 1.5 %collective-permute-start.1 = (bf16[1024,256]{1,0:T(8,128)(2,1)}, bf16[1024,256]{1,0:T(8,128)(2,1)S(1)}, u32[]{:S(2)}, u32[]{:S(2)}) collective-permute-start(bf16[1024,256]{1,0:T(8,128)(2,1)} %points_hbm.1), channel_id=1, source_target_pairs={{0,3},{1,0},{2,1},{3,2},{4,7},{5,4},{6,5},{7,6},{8,11},{9,8},{10,9... | collective-permute-start | bytes 1572872 | tf_op jit(solution)/shard_map/ppermute | solution.py:264
  4.4 2.0 %shard_map.69 = bf16[8,48,256]{2,1,0:T(8,128)(2,1)} custom-call(s32[3,16]{1,0:T(4,128)} %picks_hbm.1, s32[3]{0:T(128)} %bitcast.12, bf16[1024,256]{1,0:T(8,128)(2,1)} %points_hbm.1), custom_call_target="tpu_custom_call" | custom-call | flops 25165824 | bytes 524288 | tf_op jit(solution)/shard_map/pallas_call | solution.py:52
  6.4 8.2 %all-to-all-start = ((bf16[8,48,256]{2,1,0:T(8,128)(2,1)}), bf16[8,48,256]{2,1,0:T(8,128)(2,1)S(1)}, u32[]{:S(2)}, u32[]{:S(2)}) async-start(bf16[8,48,256]{2,1,0:T(8,128)(2,1)} %shard_map.69), calls=%async_computation | async-start | bytes 393216 | tf_op jit(solution)/shard_map/all_to_all | solution.py:275
  14.6 1.2 %collective-permute-start.2 = (bf16[512,256]{1,0:T(8,128)(2,1)S(1)}, bf16[512,256]{1,0:T(8,128)(2,1)S(1)}, u32[]{:S(2)}, u32[]{:S(2)}) collective-permute-start(bf16[512,256]{1,0:T(8,128)(2,1)S(1)} %slice.8), channel_id=1, source_target_pairs={{0,1},{1,2},{2,3},{3,0},{4,5},{5,6},{6,7},{7,4},{8,9},{9,10},{10,1... | collective-permute-start | bytes 786440 | tf_op jit(solution)/shard_map/ppermute | solution.py:264
  15.8 1.7 %collective-permute-start.3 = (bf16[512,256]{1,0:T(8,128)(2,1)S(1)}, bf16[512,256]{1,0:T(8,128)(2,1)S(1)}, u32[]{:S(2)}, u32[]{:S(2)}) collective-permute-start(bf16[512,256]{1,0:T(8,128)(2,1)S(1)} %slice.9), channel_id=1, source_target_pairs={{0,3},{1,0},{2,1},{3,2},{4,7},{5,4},{6,5},{7,6},{8,11},{9,8},{10,9... | collective-permute-start | bytes 786440 | tf_op jit(solution)/shard_map/ppermute | solution.py:264
  17.5 5.4 %all-to-all-done.refs_1_.refs_2_ = bf16[8,48,256]{2,1,0:T(8,128)(2,1)S(1)} async-done(((bf16[8,48,256]{2,1,0:T(8,128)(2,1)}), bf16[8,48,256]{2,1,0:T(8,128)(2,1)S(1)}, u32[]{:S(2)}, u32[]{:S(2)}) %all-to-all-start) | async-done | bytes 196640 | tf_op jit(solution)/shard_map/all_to_all | solution.py:275
  22.9 1.2 %collective-permute-start.5 = (bf16[8,48,256]{2,1,0:T(8,128)(2,1)S(1)}, bf16[8,48,256]{2,1,0:T(8,128)(2,1)S(1)}, u32[]{:S(2)}, u32[]{:S(2)}) collective-permute-start(bf16[8,48,256]{2,1,0:T(8,128)(2,1)S(1)} %all-to-all-done.refs_1_.refs_2_), channel_id=1, source_target_pairs={{0,8},{8,16},{16,24},{24,0},{1,9},{9,17},{17,25},{25,1},{2,10},{10... | collective-permute-start | bytes 589832 | tf_op jit(solution)/shard_map/ppermute | solution.py:264
  24.1 1.5 %collective-permute-start.7 = (bf16[8,48,256]{2,1,0:T(8,128)(2,1)S(1)}, bf16[8,48,256]{2,1,0:T(8,128)(2,1)S(1)}, u32[]{:S(2)}, u32[]{:S(2)}) collective-permute-start(bf16[8,48,256]{2,1,0:T(8,128)(2,1)S(1)} %all-to-all-done.refs_1_.refs_2_), channel_id=1, source_target_pairs={{0,24},{8,0},{16,8},{24,16},{1,25},{9,1},{17,9},{25,17},{2,26},{10... | collective-permute-start | bytes 589832 | tf_op jit(solution)/shard_map/ppermute | solution.py:264
  25.6 3.6 %collective-permute-start.9 = (bf16[8,48,256]{2,1,0:T(8,128)(2,1)S(1)}, bf16[8,48,256]{2,1,0:T(8,128)(2,1)S(1)}, u32[]{:S(2)}, u32[]{:S(2)}) collective-permute-start(bf16[8,48,256]{2,1,0:T(8,128)(2,1)S(1)} %all-to-all-done.refs_1_.refs_2_), channel_id=1, source_target_pairs={{0,4},{4,0},{1,5},{5,1},{2,6},{6,2},{3,7},{7,3},{8,12},{12,8},{9,1... | collective-permute-start | bytes 589832 | tf_op jit(solution)/shard_map/ppermute | solution.py:264
  29.2 0.5 shard_map.67
  29.8 0.8 %shard_map.70.refs_4_ = f32[3,3,1024]{2,1,0:T(4,128)S(1)} custom-call(bf16[3,256,1024]{2,1,0:T(8,128)(2,1)S(1)} %get-tuple-element.14.refs_0_, bf16[8,48,256]{2,1,0:T(8,128)(2,1)S(1)} %all-to-all-done.refs_1_.refs_2_), custom_call_target="tpu_custom_call" | custom-call | flops 603979776 | bytes 1769472 | tf_op jit(solution)/shard_map/pallas_call | solution.py:172
  30.6 1.6 %collective-permute-start.4 = (bf16[8,48,256]{2,1,0:T(8,128)(2,1)S(1)}, bf16[8,48,256]{2,1,0:T(8,128)(2,1)S(1)}, u32[]{:S(2)}, u32[]{:S(2)}) collective-permute-start(bf16[8,48,256]{2,1,0:T(8,128)(2,1)S(1)} %all-to-all-done.refs_1_.refs_2_), channel_id=1, source_target_pairs={{0,16},{8,24},{16,0},{24,8},{1,17},{9,25},{17,1},{25,9},{2,18},{10... | collective-permute-start | bytes 589832 | tf_op jit(solution)/shard_map/ppermute | solution.py:264
  32.2 2.5 %collective-permute-start.6 = (bf16[8,48,256]{2,1,0:T(8,128)(2,1)S(1)}, bf16[8,48,256]{2,1,0:T(8,128)(2,1)S(1)}, u32[]{:S(2)}, u32[]{:S(2)}) collective-permute-start(bf16[8,48,256]{2,1,0:T(8,128)(2,1)S(1)} %collective-permute-done.5.refs_2_), channel_id=1, source_target_pairs={{0,4},{4,0},{1,5},{5,1},{2,6},{6,2},{3,7},{7,3},{8,12},{12,8},{9,1... | collective-permute-start | bytes 589832 | tf_op jit(solution)/shard_map/ppermute | solution.py:264
  34.7 0.3 collective-permute-start.8
  35.0 0.2 shard_map.68
  35.2 1.3 %shard_map.71.refs_4_ = f32[4,3,1024]{2,1,0:T(4,128)S(1)} custom-call(bf16[3,256,1024]{2,1,0:T(8,128)(2,1)S(1)} %get-tuple-element.14.refs_0_, bf16[1,256,1024]{2,1,0:T(8,128)(2,1)S(1)} %get-tuple-element.15.refs_1_, bf16[8,48,256]{2,1,0:T(8,128)(2,1)S(1)} %all-to-all-done.refs_1_.refs_2_, bf16[8,48,256]{2,1,0:T(8,128)(2,1)S(1)} %collective-permute-done.9.refs_3_, ...), custom_call_target="tpu_custom_call" | custom-call | flops 1610612736 | bytes 2490368 | tf_op jit(solution)/shard_map/pallas_call | solution.py:172
  36.5 1.9 %shard_map.72.refs_4_ = f32[4,3,1024]{2,1,0:T(4,128)S(1)} custom-call(bf16[3,256,1024]{2,1,0:T(8,128)(2,1)S(1)} %get-tuple-element.14.refs_0_, bf16[1,256,1024]{2,1,0:T(8,128)(2,1)S(1)} %get-tuple-element.15.refs_1_, bf16[8,48,256]{2,1,0:T(8,128)(2,1)S(1)} %collective-permute-done.5.refs_2_, bf16[8,48,256]{2,1,0:T(8,128)(2,1)S(1)} %collective-permute-done.7.refs_3_, ...), custom_call_target="tpu_custom_call" | custom-call | flops 1610612736 | bytes 2490368 | tf_op jit(solution)/shard_map/pallas_call | solution.py:172
  38.5 1.9 %shard_map.73.refs_3_ = f32[4,3,1024]{2,1,0:T(4,128)S(1)} custom-call(bf16[3,256,1024]{2,1,0:T(8,128)(2,1)S(1)} %get-tuple-element.14.refs_0_, bf16[1,256,1024]{2,1,0:T(8,128)(2,1)S(1)} %get-tuple-element.15.refs_1_, bf16[8,48,256]{2,1,0:T(8,128)(2,1)S(1)} %collective-permute-done.6.refs_2_, bf16[8,48,256]{2,1,0:T(8,128)(2,1)S(1)} %collective-permute-done.8.refs_3_, ...), custom_call_target="tpu_custom_call" | custom-call | flops 1610612736 | bytes 2490368 | tf_op jit(solution)/shard_map/pallas_call | solution.py:172
  40.4 0.3 collective-permute-start.10
  40.7 1.1 %shard_map.74.refs_5_ = f32[4,3,1024]{2,1,0:T(4,128)S(1)} custom-call(bf16[3,256,1024]{2,1,0:T(8,128)(2,1)S(1)} %get-tuple-element.14.refs_0_, bf16[1,256,1024]{2,1,0:T(8,128)(2,1)S(1)} %get-tuple-element.15.refs_1_, bf16[8,48,256]{2,1,0:T(8,128)(2,1)S(1)} %collective-permute-done.4.refs_2_, f32[4,3,1024]{2,1,0:T(4,128)S(1)} %shard_map.73.refs_3_), custom_call_target="tpu_custom_call" | custom-call | flops 805306368 | bytes 2293760 | tf_op jit(solution)/shard_map/pallas_call | solution.py:172
  41.8 0.1 collective-permute-done.10.refs_4_
  42.0 1.1 %shard_map.75.refs_0_ = f32[3,4,1024]{2,1,0:T(4,128)S(1)} custom-call(bf16[3,256,1024]{2,1,0:T(8,128)(2,1)S(1)} %get-tuple-element.14.refs_0_, bf16[1,256,1024]{2,1,0:T(8,128)(2,1)S(1)} %get-tuple-element.15.refs_1_, f32[3,1,1024]{2,1,0:T(1,128)S(1)} %get-tuple-element.16.refs_2_, f32[1,1,1024]{2,1,0:T(1,128)S(1)} %get-tuple-element.17.refs_3_, ...), custom_call_target="tpu_custom_call" | custom-call | flops 805306368 | bytes 2293760 | tf_op jit(solution)/shard_map/pallas_call | solution.py:203
  43.1 1.6 %collective-permute-start.11 = (f32[3,4,1024]{2,1,0:T(4,128)S(1)}, f32[3,4,1024]{2,1,0:T(4,128)S(1)}, u32[]{:S(2)}, u32[]{:S(2)}) collective-permute-start(f32[3,4,1024]{2,1,0:T(4,128)S(1)} %shard_map.75.refs_0_), channel_id=1, source_target_pairs={{0,2},{1,3},{2,0},{3,1},{4,6},{5,7},{6,4},{7,5},{8,10},{9,11},{10,... | collective-permute-start | bytes 147464 | tf_op jit(solution)/shard_map/ppermute | solution.py:264
  44.7 0.4 collective-permute-start.12
  45.1 2.3 %collective-permute-start.13 = (f32[3,4,1024]{2,1,0:T(4,128)S(1)}, f32[3,4,1024]{2,1,0:T(4,128)S(1)}, u32[]{:S(2)}, u32[]{:S(2)}) collective-permute-start(f32[3,4,1024]{2,1,0:T(4,128)S(1)} %shard_map.75.refs_0_), channel_id=1, source_target_pairs={{0,3},{1,0},{2,1},{3,2},{4,7},{5,4},{6,5},{7,6},{8,11},{9,8},{10,9... | collective-permute-start | bytes 147464 | tf_op jit(solution)/shard_map/ppermute | solution.py:264
  47.4 0.2 collective-permute-done.11.refs_1_
  47.6 1.5 %collective-permute-done.12.refs_2_ = f32[3,4,1024]{2,1,0:T(4,128)S(1)} collective-permute-done((f32[3,4,1024]{2,1,0:T(4,128)S(1)}, f32[3,4,1024]{2,1,0:T(4,128)S(1)}, u32[]{:S(2)}, u32[]{:S(2)}) %collective-permute-start.12) | collective-permute-done | bytes 49184 | tf_op jit(solution)/shard_map/ppermute | solution.py:264
  49.2 1.4 %collective-permute-start.14 = (f32[32,128]{1,0:T(8,128)S(1)}, f32[32,128]{1,0:T(8,128)S(1)}, u32[]{:S(2)}, u32[]{:S(2)}) collective-permute-start(f32[32,128]{1,0:T(8,128)S(1)} %get-tuple-element.21), channel_id=1, source_target_pairs={{0,4},{4,0},{1,5},{5,1},{2,6},{6,2},{3,7},{7,3},{8,12},{12,8},{9,1... | collective-permute-start | bytes 49160 | tf_op jit(solution)/shard_map/ppermute | solution.py:264
  50.7 0.8 %collective-permute-done.14 = f32[32,128]{1,0:T(8,128)S(1)} collective-permute-done((f32[32,128]{1,0:T(8,128)S(1)}, f32[32,128]{1,0:T(8,128)S(1)}, u32[]{:S(2)}, u32[]{:S(2)}) %collective-permute-start.14) | collective-permute-done | bytes 16416 | tf_op jit(solution)/shard_map/ppermute | solution.py:264
  51.5 12.3 %all_to_all.16 = f32[32,1,128]{2,1,0:T(1,128)S(1)} all-to-all(f32[32,1,128]{2,1,0:T(1,128)S(1)} %bitcast.11), channel_id=1, replica_groups=mesh['z'=8,'x'=4,'c'=2,'y'=4] {'z','x'}, dimensions={0} | all-to-all | bytes 32768 | tf_op jit(solution)/shard_map/all_to_all | solution.py:295
  63.8 0.7 %shard_map.77 = (f32[1,1024]{1,0:T(1,128)}, f32[1,1024]{1,0:T(1,128)}, f32[1,3]{1,0:T(1,128)}) custom-call(f32[1,1024]{1,0:T(1,128)S(1)} %get-tuple-element.20.own_ref, f32[32,128]{1,0:T(8,128)S(1)} %bitcast.9), custom_call_target="tpu_custom_call" | custom-call | tf_op jit(solution)/shard_map/pallas_call | solution.py:254
  (19 shorter events, 0.2 us)
Async XLA Ops:
  0.6 28.6 %copy-start = (bf16[1024,256]{1,0:T(8,128)(2,1)S(1)}, bf16[1024,256]{1,0:T(8,128)(2,1)}, u32[]{:S(2)}) copy-start(bf16[1024,256]{1,0:T(8,128)(2,1)} %points_hbm.1) | copy-start | bytes 1572868
  0.6 13.9 %collective-permute-start = (bf16[1024,256]{1,0:T(8,128)(2,1)}, bf16[1024,256]{1,0:T(8,128)(2,1)S(1)}, u32[]{:S(2)}, u32[]{:S(2)}) collective-permute-start(bf16[1024,256]{1,0:T(8,128)(2,1)} %points_hbm.1), channel_id=1, source_target_pairs={{0,1},{1,2},{2,3},{3,0},{4,5},{5,6},{6,7},{7,4},{8,9},{9,10},{10,1... | collective-permute-start | bytes 1572872 | tf_op jit(solution)/shard_map/ppermute | solution.py:264
  2.8 12.9 %collective-permute-start.1 = (bf16[1024,256]{1,0:T(8,128)(2,1)}, bf16[1024,256]{1,0:T(8,128)(2,1)S(1)}, u32[]{:S(2)}, u32[]{:S(2)}) collective-permute-start(bf16[1024,256]{1,0:T(8,128)(2,1)} %points_hbm.1), channel_id=1, source_target_pairs={{0,3},{1,0},{2,1},{3,2},{4,7},{5,4},{6,5},{7,6},{8,11},{9,8},{10,9... | collective-permute-start | bytes 1572872 | tf_op jit(solution)/shard_map/ppermute | solution.py:264
  6.4 16.6 %all-to-all-start = ((bf16[8,48,256]{2,1,0:T(8,128)(2,1)}), bf16[8,48,256]{2,1,0:T(8,128)(2,1)S(1)}, u32[]{:S(2)}, u32[]{:S(2)}) async-start(bf16[8,48,256]{2,1,0:T(8,128)(2,1)} %shard_map.69), calls=%async_computation | async-start | bytes 393216 | tf_op jit(solution)/shard_map/all_to_all | solution.py:275
  14.6 20.1 %collective-permute-start.2 = (bf16[512,256]{1,0:T(8,128)(2,1)S(1)}, bf16[512,256]{1,0:T(8,128)(2,1)S(1)}, u32[]{:S(2)}, u32[]{:S(2)}) collective-permute-start(bf16[512,256]{1,0:T(8,128)(2,1)S(1)} %slice.8), channel_id=1, source_target_pairs={{0,1},{1,2},{2,3},{3,0},{4,5},{5,6},{6,7},{7,4},{8,9},{9,10},{10,1... | collective-permute-start | bytes 786440 | tf_op jit(solution)/shard_map/ppermute | solution.py:264
  15.8 19.2 %collective-permute-start.3 = (bf16[512,256]{1,0:T(8,128)(2,1)S(1)}, bf16[512,256]{1,0:T(8,128)(2,1)S(1)}, u32[]{:S(2)}, u32[]{:S(2)}) collective-permute-start(bf16[512,256]{1,0:T(8,128)(2,1)S(1)} %slice.9), channel_id=1, source_target_pairs={{0,3},{1,0},{2,1},{3,2},{4,7},{5,4},{6,5},{7,6},{8,11},{9,8},{10,9... | collective-permute-start | bytes 786440 | tf_op jit(solution)/shard_map/ppermute | solution.py:264
  22.9 7.7 %collective-permute-start.5 = (bf16[8,48,256]{2,1,0:T(8,128)(2,1)S(1)}, bf16[8,48,256]{2,1,0:T(8,128)(2,1)S(1)}, u32[]{:S(2)}, u32[]{:S(2)}) collective-permute-start(bf16[8,48,256]{2,1,0:T(8,128)(2,1)S(1)} %all-to-all-done.refs_1_.refs_2_), channel_id=1, source_target_pairs={{0,8},{8,16},{16,24},{24,0},{1,9},{9,17},{17,25},{25,1},{2,10},{10... | collective-permute-start | bytes 589832 | tf_op jit(solution)/shard_map/ppermute | solution.py:264
  24.1 8.1 %collective-permute-start.7 = (bf16[8,48,256]{2,1,0:T(8,128)(2,1)S(1)}, bf16[8,48,256]{2,1,0:T(8,128)(2,1)S(1)}, u32[]{:S(2)}, u32[]{:S(2)}) collective-permute-start(bf16[8,48,256]{2,1,0:T(8,128)(2,1)S(1)} %all-to-all-done.refs_1_.refs_2_), channel_id=1, source_target_pairs={{0,24},{8,0},{16,8},{24,16},{1,25},{9,1},{17,9},{25,17},{2,26},{10... | collective-permute-start | bytes 589832 | tf_op jit(solution)/shard_map/ppermute | solution.py:264
  25.6 9.6 %collective-permute-start.9 = (bf16[8,48,256]{2,1,0:T(8,128)(2,1)S(1)}, bf16[8,48,256]{2,1,0:T(8,128)(2,1)S(1)}, u32[]{:S(2)}, u32[]{:S(2)}) collective-permute-start(bf16[8,48,256]{2,1,0:T(8,128)(2,1)S(1)} %all-to-all-done.refs_1_.refs_2_), channel_id=1, source_target_pairs={{0,4},{4,0},{1,5},{5,1},{2,6},{6,2},{3,7},{7,3},{8,12},{12,8},{9,1... | collective-permute-start | bytes 589832 | tf_op jit(solution)/shard_map/ppermute | solution.py:264
  30.6 9.8 %collective-permute-start.4 = (bf16[8,48,256]{2,1,0:T(8,128)(2,1)S(1)}, bf16[8,48,256]{2,1,0:T(8,128)(2,1)S(1)}, u32[]{:S(2)}, u32[]{:S(2)}) collective-permute-start(bf16[8,48,256]{2,1,0:T(8,128)(2,1)S(1)} %all-to-all-done.refs_1_.refs_2_), channel_id=1, source_target_pairs={{0,16},{8,24},{16,0},{24,8},{1,17},{9,25},{17,1},{25,9},{2,18},{10... | collective-permute-start | bytes 589832 | tf_op jit(solution)/shard_map/ppermute | solution.py:264
  32.2 6.2 %collective-permute-start.6 = (bf16[8,48,256]{2,1,0:T(8,128)(2,1)S(1)}, bf16[8,48,256]{2,1,0:T(8,128)(2,1)S(1)}, u32[]{:S(2)}, u32[]{:S(2)}) collective-permute-start(bf16[8,48,256]{2,1,0:T(8,128)(2,1)S(1)} %collective-permute-done.5.refs_2_), channel_id=1, source_target_pairs={{0,4},{4,0},{1,5},{5,1},{2,6},{6,2},{3,7},{7,3},{8,12},{12,8},{9,1... | collective-permute-start | bytes 589832 | tf_op jit(solution)/shard_map/ppermute | solution.py:264
  34.7 3.8 %collective-permute-start.8 = (bf16[8,48,256]{2,1,0:T(8,128)(2,1)S(1)}, bf16[8,48,256]{2,1,0:T(8,128)(2,1)S(1)}, u32[]{:S(2)}, u32[]{:S(2)}) collective-permute-start(bf16[8,48,256]{2,1,0:T(8,128)(2,1)S(1)} %collective-permute-done.7.refs_3_), channel_id=1, source_target_pairs={{0,4},{4,0},{1,5},{5,1},{2,6},{6,2},{3,7},{7,3},{8,12},{12,8},{9,1... | collective-permute-start | bytes 589832 | tf_op jit(solution)/shard_map/ppermute | solution.py:264
  40.4 1.6 %copy-start.1 = (f32[1024]{0:T(1024)S(1)}, f32[1024]{0:T(1024)}, u32[]{:S(2)}) copy-start(f32[1024]{0:T(1024)} %param.5) | copy-start | bytes 12292
  40.4 1.5 %collective-permute-start.10 = (bf16[8,48,256]{2,1,0:T(8,128)(2,1)S(1)}, bf16[8,48,256]{2,1,0:T(8,128)(2,1)S(1)}, u32[]{:S(2)}, u32[]{:S(2)}) collective-permute-start(bf16[8,48,256]{2,1,0:T(8,128)(2,1)S(1)} %collective-permute-done.4.refs_2_), channel_id=1, source_target_pairs={{0,4},{4,0},{1,5},{5,1},{2,6},{6,2},{3,7},{7,3},{8,12},{12,8},{9,1... | collective-permute-start | bytes 589832 | tf_op jit(solution)/shard_map/ppermute | solution.py:264
  43.1 4.5 %collective-permute-start.11 = (f32[3,4,1024]{2,1,0:T(4,128)S(1)}, f32[3,4,1024]{2,1,0:T(4,128)S(1)}, u32[]{:S(2)}, u32[]{:S(2)}) collective-permute-start(f32[3,4,1024]{2,1,0:T(4,128)S(1)} %shard_map.75.refs_0_), channel_id=1, source_target_pairs={{0,2},{1,3},{2,0},{3,1},{4,6},{5,7},{6,4},{7,5},{8,10},{9,11},{10,... | collective-permute-start | bytes 147464 | tf_op jit(solution)/shard_map/ppermute | solution.py:264
  44.7 4.4 %collective-permute-start.12 = (f32[3,4,1024]{2,1,0:T(4,128)S(1)}, f32[3,4,1024]{2,1,0:T(4,128)S(1)}, u32[]{:S(2)}, u32[]{:S(2)}) collective-permute-start(f32[3,4,1024]{2,1,0:T(4,128)S(1)} %shard_map.75.refs_0_), channel_id=1, source_target_pairs={{0,1},{1,2},{2,3},{3,0},{4,5},{5,6},{6,7},{7,4},{8,9},{9,10},{10,1... | collective-permute-start | bytes 147464 | tf_op jit(solution)/shard_map/ppermute | solution.py:264
  45.1 4.0 %collective-permute-start.13 = (f32[3,4,1024]{2,1,0:T(4,128)S(1)}, f32[3,4,1024]{2,1,0:T(4,128)S(1)}, u32[]{:S(2)}, u32[]{:S(2)}) collective-permute-start(f32[3,4,1024]{2,1,0:T(4,128)S(1)} %shard_map.75.refs_0_), channel_id=1, source_target_pairs={{0,3},{1,0},{2,1},{3,2},{4,7},{5,4},{6,5},{7,6},{8,11},{9,8},{10,9... | collective-permute-start | bytes 147464 | tf_op jit(solution)/shard_map/ppermute | solution.py:264
  49.2 2.3 %collective-permute-start.14 = (f32[32,128]{1,0:T(8,128)S(1)}, f32[32,128]{1,0:T(8,128)S(1)}, u32[]{:S(2)}, u32[]{:S(2)}) collective-permute-start(f32[32,128]{1,0:T(8,128)S(1)} %get-tuple-element.21), channel_id=1, source_target_pairs={{0,4},{4,0},{1,5},{5,1},{2,6},{6,2},{3,7},{7,3},{8,12},{12,8},{9,1... | collective-permute-start | bytes 49160 | tf_op jit(solution)/shard_map/ppermute | solution.py:264

commit v6 on v5

--- a/solution.py
+++ b/solution.py
@@ -226,7 +226,8 @@
                     dist = ref[step, there : there + 1, :]
                     best = current[number]
                     current[number] = dist if best is None else jnp.minimum(best, dist)
-            cost = jnp.sum(sum(current), axis=1, keepdims=True)
+            pairs = (current[0] + current[3]) + (current[1] + current[2])
+            cost = jnp.sum(pairs, axis=1, keepdims=True)
             total = jnp.where(lane == step, cost, total)
         total_ref[...] = total
         own_ref[...] = current[0]
@@ -275,19 +276,17 @@
     along_z = lax.all_to_all(cand, "z", 0, 0, tiled=True)
     from_x = [shift(along_z, "x", CHIPS_X, by) for by in (2, 1, 3)]
     opposite, after, before = from_x
-    swapped = shift(along_z, "c", CORES, 1)
     near_turned, near_lengths = turn([points, behind, ahead], rows)
     far_turned, far_lengths = turn(across, rows)
     turned, lengths = [near_turned, far_turned], [near_lengths, far_lengths]
     low = near([near_turned], [along_z], None, rounds)
-    low = near(turned, [along_z, swapped], low, rounds, 1)
-    beside = [shift(piece, "c", CORES, 1) for piece in (after, before)]
-    low = near(turned, [after, before], low, rounds)
+    also = along_z
+    beside = [shift(piece, "c", CORES, 1) for piece in (also, after, before)]
+    low = near(turned, [along_z, after, before], low, rounds, 1)
     low = near(turned, beside, low, rounds)
     opposite, low = lax.optimization_barrier((opposite, low))
-    last = shift(opposite, "c", CORES, 1)
+    last = [shift(opposite, "c", CORES, 1)]
     low = near(turned, [opposite], low, rounds)
-    last = [last]
     dist = last_near(turned, last, low, lengths, init_dist[None], rounds)
     shared = [dist] + [shift(dist, "y", subs, by) for by in (2, 1, 3)]
     own, total = totals(shared, (2, 1, 3), lax.axis_size(("z", "x")))

time: 64.7 us -> 64.4 us (level)
    pallas_call x5 -> x4, Pallas kernels: 7.06 us -> 6.82 us  [near(): pl.pallas_call(body, out_shape=jax.ShapeDtypeStruct((count, rounds, rows)...]
where the time goes in v6:
time: 64.4 us; the launch traced here: 64.2 us
  starting transfers between devices  31.6 us (49%)
  blocking collectives  12.3 us (19%)
  Pallas kernels  11.4 us (18%)
  waiting for transfers between devices  8.14 us (13%)
  between operations  0.76 us (1%)
    ppermute x15, starting transfers between devices, shift(): lax.ppermute(block, axis, [(i, (i + by) % size) for i in range(size)])  23.4 us
    all_to_all x1, blocking collectives, shards(): shares = lax.all_to_all(total, ('z', 'x'), 0, 0, tiled=True)  12.3 us
    all_to_all x1, starting transfers between devices, shards(): along_z = lax.all_to_all(cand, 'z', 0, 0, tiled=True)  8.2 us
    pallas_call x4, Pallas kernels, near(): pl.pallas_call(body, out_shape=jax.ShapeDtypeStruct((count, rounds, rows)...  6.82 us
    all_to_all x1, waiting for transfers between devices, shards(): along_z = lax.all_to_all(cand, 'z', 0, 0, tiled=True)  5.42 us
    ppermute x15, waiting for transfers between devices, shift(): lax.ppermute(block, axis, [(i, (i + by) % size) for i in range(size)])  2.72 us
    pallas_call x1, Pallas kernels, pick_rows(): pl.pallas_call(pick_kernel, out_shape=jax.ShapeDtypeStruct((copies, slots...  1.98 us
  transfers between devices with their start and end apart: 16, of which 5 were waited for; matrix products, arithmetic and copies ran while one was open for 0% of the time, Pallas kernels for 15%

profile of v6, /device:TPU:1, one launch (start us, length us, event | category | flops | bytes accessed | tf_op | source)
XLA Modules:
  0.0 64.2 jit_solution(9155676264369905868)
XLA Ops:
  0.6 2.2 %collective-permute-start = (bf16[1024,256]{1,0:T(8,128)(2,1)}, bf16[1024,256]{1,0:T(8,128)(2,1)S(1)}, u32[]{:S(2)}, u32[]{:S(2)}) collective-permute-start(bf16[1024,256]{1,0:T(8,128)(2,1)} %points_hbm.1), channel_id=1, source_target_pairs={{0,1},{1,2},{2,3},{3,0},{4,5},{5,6},{6,7},{7,4},{8,9},{9,10},{10,1... | collective-permute-start | bytes 1572872 | tf_op jit(solution)/shard_map/ppermute | solution.py:265
  2.8 1.5 %collective-permute-start.1 = (bf16[1024,256]{1,0:T(8,128)(2,1)}, bf16[1024,256]{1,0:T(8,128)(2,1)S(1)}, u32[]{:S(2)}, u32[]{:S(2)}) collective-permute-start(bf16[1024,256]{1,0:T(8,128)(2,1)} %points_hbm.1), channel_id=1, source_target_pairs={{0,3},{1,0},{2,1},{3,2},{4,7},{5,4},{6,5},{7,6},{8,11},{9,8},{10,9... | collective-permute-start | bytes 1572872 | tf_op jit(solution)/shard_map/ppermute | solution.py:265
  4.4 2.0 %shard_map.69 = bf16[8,48,256]{2,1,0:T(8,128)(2,1)} custom-call(s32[3,16]{1,0:T(4,128)} %picks_hbm.1, s32[3]{0:T(128)} %bitcast.12, bf16[1024,256]{1,0:T(8,128)(2,1)} %points_hbm.1), custom_call_target="tpu_custom_call" | custom-call | flops 25165824 | bytes 524288 | tf_op jit(solution)/shard_map/pallas_call | solution.py:52
  6.4 8.2 %all-to-all-start = ((bf16[8,48,256]{2,1,0:T(8,128)(2,1)}), bf16[8,48,256]{2,1,0:T(8,128)(2,1)S(1)}, u32[]{:S(2)}, u32[]{:S(2)}) async-start(bf16[8,48,256]{2,1,0:T(8,128)(2,1)} %shard_map.69), calls=%async_computation | async-start | bytes 393216 | tf_op jit(solution)/shard_map/all_to_all | solution.py:276
  14.6 1.2 %collective-permute-start.2 = (bf16[512,256]{1,0:T(8,128)(2,1)S(1)}, bf16[512,256]{1,0:T(8,128)(2,1)S(1)}, u32[]{:S(2)}, u32[]{:S(2)}) collective-permute-start(bf16[512,256]{1,0:T(8,128)(2,1)S(1)} %slice.8), channel_id=1, source_target_pairs={{0,1},{1,2},{2,3},{3,0},{4,5},{5,6},{6,7},{7,4},{8,9},{9,10},{10,1... | collective-permute-start | bytes 786440 | tf_op jit(solution)/shard_map/ppermute | solution.py:265
  15.8 1.7 %collective-permute-start.3 = (bf16[512,256]{1,0:T(8,128)(2,1)S(1)}, bf16[512,256]{1,0:T(8,128)(2,1)S(1)}, u32[]{:S(2)}, u32[]{:S(2)}) collective-permute-start(bf16[512,256]{1,0:T(8,128)(2,1)S(1)} %slice.9), channel_id=1, source_target_pairs={{0,3},{1,0},{2,1},{3,2},{4,7},{5,4},{6,5},{7,6},{8,11},{9,8},{10,9... | collective-permute-start | bytes 786440 | tf_op jit(solution)/shard_map/ppermute | solution.py:265
  17.5 5.4 %all-to-all-done.refs_1_.refs_2_ = bf16[8,48,256]{2,1,0:T(8,128)(2,1)S(1)} async-done(((bf16[8,48,256]{2,1,0:T(8,128)(2,1)}), bf16[8,48,256]{2,1,0:T(8,128)(2,1)S(1)}, u32[]{:S(2)}, u32[]{:S(2)}) %all-to-all-start) | async-done | bytes 196640 | tf_op jit(solution)/shard_map/all_to_all | solution.py:276
  22.9 1.2 %collective-permute-start.6 = (bf16[8,48,256]{2,1,0:T(8,128)(2,1)S(1)}, bf16[8,48,256]{2,1,0:T(8,128)(2,1)S(1)}, u32[]{:S(2)}, u32[]{:S(2)}) collective-permute-start(bf16[8,48,256]{2,1,0:T(8,128)(2,1)S(1)} %all-to-all-done.refs_1_.refs_2_), channel_id=1, source_target_pairs={{0,8},{8,16},{16,24},{24,0},{1,9},{9,17},{17,25},{25,1},{2,10},{10... | collective-permute-start | bytes 589832 | tf_op jit(solution)/shard_map/ppermute | solution.py:265
  24.1 1.5 %collective-permute-start.8 = (bf16[8,48,256]{2,1,0:T(8,128)(2,1)S(1)}, bf16[8,48,256]{2,1,0:T(8,128)(2,1)S(1)}, u32[]{:S(2)}, u32[]{:S(2)}) collective-permute-start(bf16[8,48,256]{2,1,0:T(8,128)(2,1)S(1)} %all-to-all-done.refs_1_.refs_2_), channel_id=1, source_target_pairs={{0,24},{8,0},{16,8},{24,16},{1,25},{9,1},{17,9},{25,17},{2,26},{10... | collective-permute-start | bytes 589832 | tf_op jit(solution)/shard_map/ppermute | solution.py:265
  25.6 3.6 %collective-permute-start.5 = (bf16[8,48,256]{2,1,0:T(8,128)(2,1)S(1)}, bf16[8,48,256]{2,1,0:T(8,128)(2,1)S(1)}, u32[]{:S(2)}, u32[]{:S(2)}) collective-permute-start(bf16[8,48,256]{2,1,0:T(8,128)(2,1)S(1)} %all-to-all-done.refs_1_.refs_2_), channel_id=1, source_target_pairs={{0,4},{4,0},{1,5},{5,1},{2,6},{6,2},{3,7},{7,3},{8,12},{12,8},{9,1... | collective-permute-start | bytes 589832 | tf_op jit(solution)/shard_map/ppermute | solution.py:265
  29.2 0.5 shard_map.67
  29.8 0.8 %shard_map.70.refs_5_ = f32[3,3,1024]{2,1,0:T(4,128)S(1)} custom-call(bf16[3,256,1024]{2,1,0:T(8,128)(2,1)S(1)} %get-tuple-element.14.refs_0_, bf16[8,48,256]{2,1,0:T(8,128)(2,1)S(1)} %all-to-all-done.refs_1_.refs_2_), custom_call_target="tpu_custom_call" | custom-call | flops 603979776 | bytes 1769472 | tf_op jit(solution)/shard_map/pallas_call | solution.py:172
  30.6 1.6 %collective-permute-start.4 = (bf16[8,48,256]{2,1,0:T(8,128)(2,1)S(1)}, bf16[8,48,256]{2,1,0:T(8,128)(2,1)S(1)}, u32[]{:S(2)}, u32[]{:S(2)}) collective-permute-start(bf16[8,48,256]{2,1,0:T(8,128)(2,1)S(1)} %all-to-all-done.refs_1_.refs_2_), channel_id=1, source_target_pairs={{0,16},{8,24},{16,0},{24,8},{1,17},{9,25},{17,1},{25,9},{2,18},{10... | collective-permute-start | bytes 589832 | tf_op jit(solution)/shard_map/ppermute | solution.py:265
  32.2 2.5 %collective-permute-start.7 = (bf16[8,48,256]{2,1,0:T(8,128)(2,1)S(1)}, bf16[8,48,256]{2,1,0:T(8,128)(2,1)S(1)}, u32[]{:S(2)}, u32[]{:S(2)}) collective-permute-start(bf16[8,48,256]{2,1,0:T(8,128)(2,1)S(1)} %collective-permute-done.6.refs_3_), channel_id=1, source_target_pairs={{0,4},{4,0},{1,5},{5,1},{2,6},{6,2},{3,7},{7,3},{8,12},{12,8},{9,1... | collective-permute-start | bytes 589832 | tf_op jit(solution)/shard_map/ppermute | solution.py:265
  34.7 0.3 collective-permute-start.9
  35.0 0.2 shard_map.68
  35.2 2.1 %shard_map.71.refs_5_ = f32[4,3,1024]{2,1,0:T(4,128)S(1)} custom-call(bf16[3,256,1024]{2,1,0:T(8,128)(2,1)S(1)} %get-tuple-element.14.refs_0_, bf16[1,256,1024]{2,1,0:T(8,128)(2,1)S(1)} %get-tuple-element.15.refs_1_, bf16[8,48,256]{2,1,0:T(8,128)(2,1)S(1)} %all-to-all-done.refs_1_.refs_2_, bf16[8,48,256]{2,1,0:T(8,128)(2,1)S(1)} %collective-permute-done.6.refs_3_, ...), custom_call_target="tpu_custom_call" | custom-call | flops 2415919104 | bytes 2686976 | tf_op jit(solution)/shard_map/pallas_call | solution.py:172
  37.4 2.8 %shard_map.72.refs_3_ = f32[4,3,1024]{2,1,0:T(4,128)S(1)} custom-call(bf16[3,256,1024]{2,1,0:T(8,128)(2,1)S(1)} %get-tuple-element.14.refs_0_, bf16[1,256,1024]{2,1,0:T(8,128)(2,1)S(1)} %get-tuple-element.15.refs_1_, bf16[8,48,256]{2,1,0:T(8,128)(2,1)S(1)} %collective-permute-done.5.refs_2_, bf16[8,48,256]{2,1,0:T(8,128)(2,1)S(1)} %collective-permute-done.7.refs_3_, ...), custom_call_target="tpu_custom_call" | custom-call | flops 2415919104 | bytes 2686976 | tf_op jit(solution)/shard_map/pallas_call | solution.py:172
  40.2 0.3 collective-permute-start.10
  40.5 1.1 %shard_map.73.refs_5_ = f32[4,3,1024]{2,1,0:T(4,128)S(1)} custom-call(bf16[3,256,1024]{2,1,0:T(8,128)(2,1)S(1)} %get-tuple-element.14.refs_0_, bf16[1,256,1024]{2,1,0:T(8,128)(2,1)S(1)} %get-tuple-element.15.refs_1_, bf16[8,48,256]{2,1,0:T(8,128)(2,1)S(1)} %collective-permute-done.4.refs_2_, f32[4,3,1024]{2,1,0:T(4,128)S(1)} %shard_map.72.refs_3_), custom_call_target="tpu_custom_call" | custom-call | flops 805306368 | bytes 2293760 | tf_op jit(solution)/shard_map/pallas_call | solution.py:172
  41.6 0.1 collective-permute-done.10.refs_4_
  41.7 1.1 %shard_map.74.refs_0_ = f32[3,4,1024]{2,1,0:T(4,128)S(1)} custom-call(bf16[3,256,1024]{2,1,0:T(8,128)(2,1)S(1)} %get-tuple-element.14.refs_0_, bf16[1,256,1024]{2,1,0:T(8,128)(2,1)S(1)} %get-tuple-element.15.refs_1_, f32[3,1,1024]{2,1,0:T(1,128)S(1)} %get-tuple-element.16.refs_2_, f32[1,1,1024]{2,1,0:T(1,128)S(1)} %get-tuple-element.17.refs_3_, ...), custom_call_target="tpu_custom_call" | custom-call | flops 805306368 | bytes 2293760 | tf_op jit(solution)/shard_map/pallas_call | solution.py:203
  42.8 1.6 %collective-permute-start.11 = (f32[3,4,1024]{2,1,0:T(4,128)S(1)}, f32[3,4,1024]{2,1,0:T(4,128)S(1)}, u32[]{:S(2)}, u32[]{:S(2)}) collective-permute-start(f32[3,4,1024]{2,1,0:T(4,128)S(1)} %shard_map.74.refs_0_), channel_id=1, source_target_pairs={{0,2},{1,3},{2,0},{3,1},{4,6},{5,7},{6,4},{7,5},{8,10},{9,11},{10,... | collective-permute-start | bytes 147464 | tf_op jit(solution)/shard_map/ppermute | solution.py:265
  44.4 0.4 collective-permute-start.12
  44.8 2.3 %collective-permute-start.13 = (f32[3,4,1024]{2,1,0:T(4,128)S(1)}, f32[3,4,1024]{2,1,0:T(4,128)S(1)}, u32[]{:S(2)}, u32[]{:S(2)}) collective-permute-start(f32[3,4,1024]{2,1,0:T(4,128)S(1)} %shard_map.74.refs_0_), channel_id=1, source_target_pairs={{0,3},{1,0},{2,1},{3,2},{4,7},{5,4},{6,5},{7,6},{8,11},{9,8},{10,9... | collective-permute-start | bytes 147464 | tf_op jit(solution)/shard_map/ppermute | solution.py:265
  47.1 0.2 collective-permute-done.11.refs_1_
  47.3 1.5 %collective-permute-done.12.refs_2_ = f32[3,4,1024]{2,1,0:T(4,128)S(1)} collective-permute-done((f32[3,4,1024]{2,1,0:T(4,128)S(1)}, f32[3,4,1024]{2,1,0:T(4,128)S(1)}, u32[]{:S(2)}, u32[]{:S(2)}) %collective-permute-start.12) | collective-permute-done | bytes 49184 | tf_op jit(solution)/shard_map/ppermute | solution.py:265
  48.8 0.1 shard_map.75
  48.9 1.5 %collective-permute-start.14 = (f32[32,128]{1,0:T(8,128)S(1)}, f32[32,128]{1,0:T(8,128)S(1)}, u32[]{:S(2)}, u32[]{:S(2)}) collective-permute-start(f32[32,128]{1,0:T(8,128)S(1)} %get-tuple-element.21), channel_id=1, source_target_pairs={{0,4},{4,0},{1,5},{5,1},{2,6},{6,2},{3,7},{7,3},{8,12},{12,8},{9,1... | collective-permute-start | bytes 49160 | tf_op jit(solution)/shard_map/ppermute | solution.py:265
  50.4 0.8 %collective-permute-done.14 = f32[32,128]{1,0:T(8,128)S(1)} collective-permute-done((f32[32,128]{1,0:T(8,128)S(1)}, f32[32,128]{1,0:T(8,128)S(1)}, u32[]{:S(2)}, u32[]{:S(2)}) %collective-permute-start.14) | collective-permute-done | bytes 16416 | tf_op jit(solution)/shard_map/ppermute | solution.py:265
  51.2 12.3 %all_to_all.16 = f32[32,1,128]{2,1,0:T(1,128)S(1)} all-to-all(f32[32,1,128]{2,1,0:T(1,128)S(1)} %bitcast.11), channel_id=1, replica_groups=mesh['z'=8,'x'=4,'c'=2,'y'=4] {'z','x'}, dimensions={0} | all-to-all | bytes 32768 | tf_op jit(solution)/shard_map/all_to_all | solution.py:294
  63.5 0.7 %shard_map.76 = (f32[1,1024]{1,0:T(1,128)}, f32[1,1024]{1,0:T(1,128)}, f32[1,3]{1,0:T(1,128)}) custom-call(f32[1,1024]{1,0:T(1,128)S(1)} %get-tuple-element.20.own_ref, f32[32,128]{1,0:T(8,128)S(1)} %bitcast.9), custom_call_target="tpu_custom_call" | custom-call | tf_op jit(solution)/shard_map/pallas_call | solution.py:255
  (18 shorter events, 0.1 us)
Async XLA Ops:
  0.6 28.6 %copy-start = (bf16[1024,256]{1,0:T(8,128)(2,1)S(1)}, bf16[1024,256]{1,0:T(8,128)(2,1)}, u32[]{:S(2)}) copy-start(bf16[1024,256]{1,0:T(8,128)(2,1)} %points_hbm.1) | copy-start | bytes 1572868
  0.6 13.9 %collective-permute-start = (bf16[1024,256]{1,0:T(8,128)(2,1)}, bf16[1024,256]{1,0:T(8,128)(2,1)S(1)}, u32[]{:S(2)}, u32[]{:S(2)}) collective-permute-start(bf16[1024,256]{1,0:T(8,128)(2,1)} %points_hbm.1), channel_id=1, source_target_pairs={{0,1},{1,2},{2,3},{3,0},{4,5},{5,6},{6,7},{7,4},{8,9},{9,10},{10,1... | collective-permute-start | bytes 1572872 | tf_op jit(solution)/shard_map/ppermute | solution.py:265
  2.8 12.9 %collective-permute-start.1 = (bf16[1024,256]{1,0:T(8,128)(2,1)}, bf16[1024,256]{1,0:T(8,128)(2,1)S(1)}, u32[]{:S(2)}, u32[]{:S(2)}) collective-permute-start(bf16[1024,256]{1,0:T(8,128)(2,1)} %points_hbm.1), channel_id=1, source_target_pairs={{0,3},{1,0},{2,1},{3,2},{4,7},{5,4},{6,5},{7,6},{8,11},{9,8},{10,9... | collective-permute-start | bytes 1572872 | tf_op jit(solution)/shard_map/ppermute | solution.py:265
  6.4 16.6 %all-to-all-start = ((bf16[8,48,256]{2,1,0:T(8,128)(2,1)}), bf16[8,48,256]{2,1,0:T(8,128)(2,1)S(1)}, u32[]{:S(2)}, u32[]{:S(2)}) async-start(bf16[8,48,256]{2,1,0:T(8,128)(2,1)} %shard_map.69), calls=%async_computation | async-start | bytes 393216 | tf_op jit(solution)/shard_map/all_to_all | solution.py:276
  14.6 20.1 %collective-permute-start.2 = (bf16[512,256]{1,0:T(8,128)(2,1)S(1)}, bf16[512,256]{1,0:T(8,128)(2,1)S(1)}, u32[]{:S(2)}, u32[]{:S(2)}) collective-permute-start(bf16[512,256]{1,0:T(8,128)(2,1)S(1)} %slice.8), channel_id=1, source_target_pairs={{0,1},{1,2},{2,3},{3,0},{4,5},{5,6},{6,7},{7,4},{8,9},{9,10},{10,1... | collective-permute-start | bytes 786440 | tf_op jit(solution)/shard_map/ppermute | solution.py:265
  15.8 19.2 %collective-permute-start.3 = (bf16[512,256]{1,0:T(8,128)(2,1)S(1)}, bf16[512,256]{1,0:T(8,128)(2,1)S(1)}, u32[]{:S(2)}, u32[]{:S(2)}) collective-permute-start(bf16[512,256]{1,0:T(8,128)(2,1)S(1)} %slice.9), channel_id=1, source_target_pairs={{0,3},{1,0},{2,1},{3,2},{4,7},{5,4},{6,5},{7,6},{8,11},{9,8},{10,9... | collective-permute-start | bytes 786440 | tf_op jit(solution)/shard_map/ppermute | solution.py:265
  22.9 7.7 %collective-permute-start.6 = (bf16[8,48,256]{2,1,0:T(8,128)(2,1)S(1)}, bf16[8,48,256]{2,1,0:T(8,128)(2,1)S(1)}, u32[]{:S(2)}, u32[]{:S(2)}) collective-permute-start(bf16[8,48,256]{2,1,0:T(8,128)(2,1)S(1)} %all-to-all-done.refs_1_.refs_2_), channel_id=1, source_target_pairs={{0,8},{8,16},{16,24},{24,0},{1,9},{9,17},{17,25},{25,1},{2,10},{10... | collective-permute-start | bytes 589832 | tf_op jit(solution)/shard_map/ppermute | solution.py:265
  24.1 8.1 %collective-permute-start.8 = (bf16[8,48,256]{2,1,0:T(8,128)(2,1)S(1)}, bf16[8,48,256]{2,1,0:T(8,128)(2,1)S(1)}, u32[]{:S(2)}, u32[]{:S(2)}) collective-permute-start(bf16[8,48,256]{2,1,0:T(8,128)(2,1)S(1)} %all-to-all-done.refs_1_.refs_2_), channel_id=1, source_target_pairs={{0,24},{8,0},{16,8},{24,16},{1,25},{9,1},{17,9},{25,17},{2,26},{10... | collective-permute-start | bytes 589832 | tf_op jit(solution)/shard_map/ppermute | solution.py:265
  25.6 11.7 %collective-permute-start.5 = (bf16[8,48,256]{2,1,0:T(8,128)(2,1)S(1)}, bf16[8,48,256]{2,1,0:T(8,128)(2,1)S(1)}, u32[]{:S(2)}, u32[]{:S(2)}) collective-permute-start(bf16[8,48,256]{2,1,0:T(8,128)(2,1)S(1)} %all-to-all-done.refs_1_.refs_2_), channel_id=1, source_target_pairs={{0,4},{4,0},{1,5},{5,1},{2,6},{6,2},{3,7},{7,3},{8,12},{12,8},{9,1... | collective-permute-start | bytes 589832 | tf_op jit(solution)/shard_map/ppermute | solution.py:265
  30.6 9.6 %collective-permute-start.4 = (bf16[8,48,256]{2,1,0:T(8,128)(2,1)S(1)}, bf16[8,48,256]{2,1,0:T(8,128)(2,1)S(1)}, u32[]{:S(2)}, u32[]{:S(2)}) collective-permute-start(bf16[8,48,256]{2,1,0:T(8,128)(2,1)S(1)} %all-to-all-done.refs_1_.refs_2_), channel_id=1, source_target_pairs={{0,16},{8,24},{16,0},{24,8},{1,17},{9,25},{17,1},{25,9},{2,18},{10... | collective-permute-start | bytes 589832 | tf_op jit(solution)/shard_map/ppermute | solution.py:265
  32.2 5.1 %collective-permute-start.7 = (bf16[8,48,256]{2,1,0:T(8,128)(2,1)S(1)}, bf16[8,48,256]{2,1,0:T(8,128)(2,1)S(1)}, u32[]{:S(2)}, u32[]{:S(2)}) collective-permute-start(bf16[8,48,256]{2,1,0:T(8,128)(2,1)S(1)} %collective-permute-done.6.refs_3_), channel_id=1, source_target_pairs={{0,4},{4,0},{1,5},{5,1},{2,6},{6,2},{3,7},{7,3},{8,12},{12,8},{9,1... | collective-permute-start | bytes 589832 | tf_op jit(solution)/shard_map/ppermute | solution.py:265
  34.7 2.7 %collective-permute-start.9 = (bf16[8,48,256]{2,1,0:T(8,128)(2,1)S(1)}, bf16[8,48,256]{2,1,0:T(8,128)(2,1)S(1)}, u32[]{:S(2)}, u32[]{:S(2)}) collective-permute-start(bf16[8,48,256]{2,1,0:T(8,128)(2,1)S(1)} %collective-permute-done.8.refs_4_), channel_id=1, source_target_pairs={{0,4},{4,0},{1,5},{5,1},{2,6},{6,2},{3,7},{7,3},{8,12},{12,8},{9,1... | collective-permute-start | bytes 589832 | tf_op jit(solution)/shard_map/ppermute | solution.py:265
  40.1 1.6 %copy-start.1 = (f32[1024]{0:T(1024)S(1)}, f32[1024]{0:T(1024)}, u32[]{:S(2)}) copy-start(f32[1024]{0:T(1024)} %param.5) | copy-start | bytes 12292
  40.2 1.5 %collective-permute-start.10 = (bf16[8,48,256]{2,1,0:T(8,128)(2,1)S(1)}, bf16[8,48,256]{2,1,0:T(8,128)(2,1)S(1)}, u32[]{:S(2)}, u32[]{:S(2)}) collective-permute-start(bf16[8,48,256]{2,1,0:T(8,128)(2,1)S(1)} %collective-permute-done.4.refs_2_), channel_id=1, source_target_pairs={{0,4},{4,0},{1,5},{5,1},{2,6},{6,2},{3,7},{7,3},{8,12},{12,8},{9,1... | collective-permute-start | bytes 589832 | tf_op jit(solution)/shard_map/ppermute | solution.py:265
  42.8 4.5 %collective-permute-start.11 = (f32[3,4,1024]{2,1,0:T(4,128)S(1)}, f32[3,4,1024]{2,1,0:T(4,128)S(1)}, u32[]{:S(2)}, u32[]{:S(2)}) collective-permute-start(f32[3,4,1024]{2,1,0:T(4,128)S(1)} %shard_map.74.refs_0_), channel_id=1, source_target_pairs={{0,2},{1,3},{2,0},{3,1},{4,6},{5,7},{6,4},{7,5},{8,10},{9,11},{10,... | collective-permute-start | bytes 147464 | tf_op jit(solution)/shard_map/ppermute | solution.py:265
  44.4 4.4 %collective-permute-start.12 = (f32[3,4,1024]{2,1,0:T(4,128)S(1)}, f32[3,4,1024]{2,1,0:T(4,128)S(1)}, u32[]{:S(2)}, u32[]{:S(2)}) collective-permute-start(f32[3,4,1024]{2,1,0:T(4,128)S(1)} %shard_map.74.refs_0_), channel_id=1, source_target_pairs={{0,1},{1,2},{2,3},{3,0},{4,5},{5,6},{6,7},{7,4},{8,9},{9,10},{10,1... | collective-permute-start | bytes 147464 | tf_op jit(solution)/shard_map/ppermute | solution.py:265
  44.8 4.0 %collective-permute-start.13 = (f32[3,4,1024]{2,1,0:T(4,128)S(1)}, f32[3,4,1024]{2,1,0:T(4,128)S(1)}, u32[]{:S(2)}, u32[]{:S(2)}) collective-permute-start(f32[3,4,1024]{2,1,0:T(4,128)S(1)} %shard_map.74.refs_0_), channel_id=1, source_target_pairs={{0,3},{1,0},{2,1},{3,2},{4,7},{5,4},{6,5},{7,6},{8,11},{9,8},{10,9... | collective-permute-start | bytes 147464 | tf_op jit(solution)/shard_map/ppermute | solution.py:265
  48.9 2.3 %collective-permute-start.14 = (f32[32,128]{1,0:T(8,128)S(1)}, f32[32,128]{1,0:T(8,128)S(1)}, u32[]{:S(2)}, u32[]{:S(2)}) collective-permute-start(f32[32,128]{1,0:T(8,128)S(1)} %get-tuple-element.21), channel_id=1, source_target_pairs={{0,4},{4,0},{1,5},{5,1},{2,6},{6,2},{3,7},{7,3},{8,12},{12,8},{9,1... | collective-permute-start | bytes 49160 | tf_op jit(solution)/shard_map/ppermute | solution.py:265

commit v7 on v6

--- a/solution.py
+++ b/solution.py
@@ -8,6 +8,7 @@
 CHIPS_Z, CHIPS_X, CORES = 8, 4, 2
 PART = 256
 LANES = 128
+COLUMNS = 512
 PLACES = (0, 3, 1, 2)
 F32, BF16 = jnp.float32, jnp.bfloat16
 VMEM = pl.BlockSpec(memory_space=pltpu.VMEM)
@@ -117,24 +118,27 @@
 
 
 def lowest(weights, cands, sq_ref, step, rounds, skipped=0):
-    count = weights.shape[1]
-    best = None
-    base = 0
-    for order, cand_ref in enumerate(cands):
-        values = half_round(cand_ref, step, rounds)
-        if order < skipped:
-            base += values.shape[0]
-            continue
-        for part in range(0, values.shape[0], PART):
-            piece = values[part : part + PART]
-            size = piece.shape[0]
-            inner = jnp.dot(piece, weights, preferred_element_type=F32)
-            squares = sq_ref[step, base : base + size, :]
-            dist = inner + jnp.concatenate([squares] * (count // LANES), axis=1)
-            low = jnp.min(dist.reshape(size // 8, 8, count), axis=0)
-            best = low if best is None else jnp.minimum(best, low)
-            base += size
-    return jnp.min(best, axis=0, keepdims=True)
+    found = []
+    for column in range(0, weights.shape[1], COLUMNS):
+        tile = weights[:, column : column + COLUMNS]
+        best = None
+        base = 0
+        for order, cand_ref in enumerate(cands):
+            values = half_round(cand_ref, step, rounds)
+            if order < skipped:
+                base += values.shape[0]
+                continue
+            for part in range(0, values.shape[0], PART):
+                piece = values[part : part + PART]
+                size = piece.shape[0]
+                inner = jnp.dot(piece, tile, preferred_element_type=F32)
+                squares = sq_ref[step, base : base + size, :]
+                dist = inner + jnp.concatenate([squares] * (COLUMNS // LANES), axis=1)
+                low = jnp.min(dist.reshape(size // 8, 8, COLUMNS), axis=0)
+                best = low if best is None else jnp.minimum(best, low)
+                base += size
+        found.append(jnp.min(best, axis=0, keepdims=True))
+    return jnp.concatenate(found, axis=1)
 
 
 def blocks_of(turned):
@@ -281,7 +285,7 @@
     turned, lengths = [near_turned, far_turned], [near_lengths, far_lengths]
     low = near([near_turned], [along_z], None, rounds)
     also = along_z
-    beside = [shift(piece, "c", CORES, 1) for piece in (also, after, before)]
+    beside = [shift(piece, "c", CORES, 1) for piece in (after, before, also)]
     low = near(turned, [along_z, after, before], low, rounds, 1)
     low = near(turned, beside, low, rounds)
     opposite, low = lax.optimization_barrier((opposite, low))

time: 64.4 us -> 64.5 us (level)
  no operation moved by 1% of the time
where the time goes in v7:
time: 64.5 us; the launch traced here: 64.2 us
  starting transfers between devices  31.6 us (49%)
  blocking collectives  12.3 us (19%)
  Pallas kernels  11.5 us (18%)
  waiting for transfers between devices  8.13 us (13%)
  between operations  0.76 us (1%)
    ppermute x15, starting transfers between devices, shift(): lax.ppermute(block, axis, [(i, (i + by) % size) for i in range(size)])  23.4 us
    all_to_all x1, blocking collectives, shards(): shares = lax.all_to_all(total, ('z', 'x'), 0, 0, tiled=True)  12.3 us
    all_to_all x1, starting transfers between devices, shards(): along_z = lax.all_to_all(cand, 'z', 0, 0, tiled=True)  8.2 us
    pallas_call x4, Pallas kernels, near(): pl.pallas_call(body, out_shape=jax.ShapeDtypeStruct((count, rounds, rows)...  6.85 us
    all_to_all x1, waiting for transfers between devices, shards(): along_z = lax.all_to_all(cand, 'z', 0, 0, tiled=True)  5.42 us
    ppermute x15, waiting for transfers between devices, shift(): lax.ppermute(block, axis, [(i, (i + by) % size) for i in range(size)])  2.71 us
    pallas_call x1, Pallas kernels, pick_rows(): pl.pallas_call(pick_kernel, out_shape=jax.ShapeDtypeStruct((copies, slots...  1.98 us
  transfers between devices with their start and end apart: 16, of which 5 were waited for; matrix products, arithmetic and copies ran while one was open for 0% of the time, Pallas kernels for 15%

profile of v7, /device:TPU:1, one launch (start us, length us, event | category | flops | bytes accessed | tf_op | source)
XLA Modules:
  0.0 64.2 jit_solution(810034478207050919)
XLA Ops:
  0.6 2.2 %collective-permute-start = (bf16[1024,256]{1,0:T(8,128)(2,1)}, bf16[1024,256]{1,0:T(8,128)(2,1)S(1)}, u32[]{:S(2)}, u32[]{:S(2)}) collective-permute-start(bf16[1024,256]{1,0:T(8,128)(2,1)} %points_hbm.1), channel_id=1, source_target_pairs={{0,1},{1,2},{2,3},{3,0},{4,5},{5,6},{6,7},{7,4},{8,9},{9,10},{10,1... | collective-permute-start | bytes 1572872 | tf_op jit(solution)/shard_map/ppermute | solution.py:269
  2.8 1.5 %collective-permute-start.1 = (bf16[1024,256]{1,0:T(8,128)(2,1)}, bf16[1024,256]{1,0:T(8,128)(2,1)S(1)}, u32[]{:S(2)}, u32[]{:S(2)}) collective-permute-start(bf16[1024,256]{1,0:T(8,128)(2,1)} %points_hbm.1), channel_id=1, source_target_pairs={{0,3},{1,0},{2,1},{3,2},{4,7},{5,4},{6,5},{7,6},{8,11},{9,8},{10,9... | collective-permute-start | bytes 1572872 | tf_op jit(solution)/shard_map/ppermute | solution.py:269
  4.4 2.0 %shard_map.69 = bf16[8,48,256]{2,1,0:T(8,128)(2,1)} custom-call(s32[3,16]{1,0:T(4,128)} %picks_hbm.1, s32[3]{0:T(128)} %bitcast.12, bf16[1024,256]{1,0:T(8,128)(2,1)} %points_hbm.1), custom_call_target="tpu_custom_call" | custom-call | flops 25165824 | bytes 524288 | tf_op jit(solution)/shard_map/pallas_call | solution.py:53
  6.4 8.2 %all-to-all-start = ((bf16[8,48,256]{2,1,0:T(8,128)(2,1)}), bf16[8,48,256]{2,1,0:T(8,128)(2,1)S(1)}, u32[]{:S(2)}, u32[]{:S(2)}) async-start(bf16[8,48,256]{2,1,0:T(8,128)(2,1)} %shard_map.69), calls=%async_computation | async-start | bytes 393216 | tf_op jit(solution)/shard_map/all_to_all | solution.py:280
  14.6 1.2 %collective-permute-start.2 = (bf16[512,256]{1,0:T(8,128)(2,1)S(1)}, bf16[512,256]{1,0:T(8,128)(2,1)S(1)}, u32[]{:S(2)}, u32[]{:S(2)}) collective-permute-start(bf16[512,256]{1,0:T(8,128)(2,1)S(1)} %slice.8), channel_id=1, source_target_pairs={{0,1},{1,2},{2,3},{3,0},{4,5},{5,6},{6,7},{7,4},{8,9},{9,10},{10,1... | collective-permute-start | bytes 786440 | tf_op jit(solution)/shard_map/ppermute | solution.py:269
  15.8 1.7 %collective-permute-start.3 = (bf16[512,256]{1,0:T(8,128)(2,1)S(1)}, bf16[512,256]{1,0:T(8,128)(2,1)S(1)}, u32[]{:S(2)}, u32[]{:S(2)}) collective-permute-start(bf16[512,256]{1,0:T(8,128)(2,1)S(1)} %slice.9), channel_id=1, source_target_pairs={{0,3},{1,0},{2,1},{3,2},{4,7},{5,4},{6,5},{7,6},{8,11},{9,8},{10,9... | collective-permute-start | bytes 786440 | tf_op jit(solution)/shard_map/ppermute | solution.py:269
  17.5 5.4 %all-to-all-done.refs_1_.refs_2_ = bf16[8,48,256]{2,1,0:T(8,128)(2,1)S(1)} async-done(((bf16[8,48,256]{2,1,0:T(8,128)(2,1)}), bf16[8,48,256]{2,1,0:T(8,128)(2,1)S(1)}, u32[]{:S(2)}, u32[]{:S(2)}) %all-to-all-start) | async-done | bytes 196640 | tf_op jit(solution)/shard_map/all_to_all | solution.py:280
  22.9 1.2 %collective-permute-start.5 = (bf16[8,48,256]{2,1,0:T(8,128)(2,1)S(1)}, bf16[8,48,256]{2,1,0:T(8,128)(2,1)S(1)}, u32[]{:S(2)}, u32[]{:S(2)}) collective-permute-start(bf16[8,48,256]{2,1,0:T(8,128)(2,1)S(1)} %all-to-all-done.refs_1_.refs_2_), channel_id=1, source_target_pairs={{0,8},{8,16},{16,24},{24,0},{1,9},{9,17},{17,25},{25,1},{2,10},{10... | collective-permute-start | bytes 589832 | tf_op jit(solution)/shard_map/ppermute | solution.py:269
  24.1 1.5 %collective-permute-start.7 = (bf16[8,48,256]{2,1,0:T(8,128)(2,1)S(1)}, bf16[8,48,256]{2,1,0:T(8,128)(2,1)S(1)}, u32[]{:S(2)}, u32[]{:S(2)}) collective-permute-start(bf16[8,48,256]{2,1,0:T(8,128)(2,1)S(1)} %all-to-all-done.refs_1_.refs_2_), channel_id=1, source_target_pairs={{0,24},{8,0},{16,8},{24,16},{1,25},{9,1},{17,9},{25,17},{2,26},{10... | collective-permute-start | bytes 589832 | tf_op jit(solution)/shard_map/ppermute | solution.py:269
  25.6 3.6 %collective-permute-start.9 = (bf16[8,48,256]{2,1,0:T(8,128)(2,1)S(1)}, bf16[8,48,256]{2,1,0:T(8,128)(2,1)S(1)}, u32[]{:S(2)}, u32[]{:S(2)}) collective-permute-start(bf16[8,48,256]{2,1,0:T(8,128)(2,1)S(1)} %all-to-all-done.refs_1_.refs_2_), channel_id=1, source_target_pairs={{0,4},{4,0},{1,5},{5,1},{2,6},{6,2},{3,7},{7,3},{8,12},{12,8},{9,1... | collective-permute-start | bytes 589832 | tf_op jit(solution)/shard_map/ppermute | solution.py:269
  29.2 0.5 shard_map.67
  29.8 0.8 %shard_map.70.refs_5_ = f32[3,3,1024]{2,1,0:T(4,128)S(1)} custom-call(bf16[3,256,1024]{2,1,0:T(8,128)(2,1)S(1)} %get-tuple-element.14.refs_0_, bf16[8,48,256]{2,1,0:T(8,128)(2,1)S(1)} %all-to-all-done.refs_1_.refs_2_), custom_call_target="tpu_custom_call" | custom-call | flops 603979776 | bytes 1769472 | tf_op jit(solution)/shard_map/pallas_call | solution.py:176
  30.6 1.6 %collective-permute-start.4 = (bf16[8,48,256]{2,1,0:T(8,128)(2,1)S(1)}, bf16[8,48,256]{2,1,0:T(8,128)(2,1)S(1)}, u32[]{:S(2)}, u32[]{:S(2)}) collective-permute-start(bf16[8,48,256]{2,1,0:T(8,128)(2,1)S(1)} %all-to-all-done.refs_1_.refs_2_), channel_id=1, source_target_pairs={{0,16},{8,24},{16,0},{24,8},{1,17},{9,25},{17,1},{25,9},{2,18},{10... | collective-permute-start | bytes 589832 | tf_op jit(solution)/shard_map/ppermute | solution.py:269
  32.2 2.5 %collective-permute-start.6 = (bf16[8,48,256]{2,1,0:T(8,128)(2,1)S(1)}, bf16[8,48,256]{2,1,0:T(8,128)(2,1)S(1)}, u32[]{:S(2)}, u32[]{:S(2)}) collective-permute-start(bf16[8,48,256]{2,1,0:T(8,128)(2,1)S(1)} %collective-permute-done.5.refs_3_), channel_id=1, source_target_pairs={{0,4},{4,0},{1,5},{5,1},{2,6},{6,2},{3,7},{7,3},{8,12},{12,8},{9,1... | collective-permute-start | bytes 589832 | tf_op jit(solution)/shard_map/ppermute | solution.py:269
  34.7 0.3 collective-permute-start.8
  35.0 0.2 shard_map.68
  35.2 2.2 %shard_map.71.refs_5_ = f32[4,3,1024]{2,1,0:T(4,128)S(1)} custom-call(bf16[3,256,1024]{2,1,0:T(8,128)(2,1)S(1)} %get-tuple-element.14.refs_0_, bf16[1,256,1024]{2,1,0:T(8,128)(2,1)S(1)} %get-tuple-element.15.refs_1_, bf16[8,48,256]{2,1,0:T(8,128)(2,1)S(1)} %all-to-all-done.refs_1_.refs_2_, bf16[8,48,256]{2,1,0:T(8,128)(2,1)S(1)} %collective-permute-done.5.refs_3_, ...), custom_call_target="tpu_custom_call" | custom-call | flops 2415919104 | bytes 2686976 | tf_op jit(solution)/shard_map/pallas_call | solution.py:176
  37.4 2.8 %shard_map.72.refs_3_ = f32[4,3,1024]{2,1,0:T(4,128)S(1)} custom-call(bf16[3,256,1024]{2,1,0:T(8,128)(2,1)S(1)} %get-tuple-element.14.refs_0_, bf16[1,256,1024]{2,1,0:T(8,128)(2,1)S(1)} %get-tuple-element.15.refs_1_, bf16[8,48,256]{2,1,0:T(8,128)(2,1)S(1)} %collective-permute-done.6.refs_2_, bf16[8,48,256]{2,1,0:T(8,128)(2,1)S(1)} %collective-permute-done.8.refs_3_, ...), custom_call_target="tpu_custom_call" | custom-call | flops 2415919104 | bytes 2686976 | tf_op jit(solution)/shard_map/pallas_call | solution.py:176
  40.2 0.3 collective-permute-start.10
  40.5 1.1 %shard_map.73.refs_5_ = f32[4,3,1024]{2,1,0:T(4,128)S(1)} custom-call(bf16[3,256,1024]{2,1,0:T(8,128)(2,1)S(1)} %get-tuple-element.14.refs_0_, bf16[1,256,1024]{2,1,0:T(8,128)(2,1)S(1)} %get-tuple-element.15.refs_1_, bf16[8,48,256]{2,1,0:T(8,128)(2,1)S(1)} %collective-permute-done.4.refs_2_, f32[4,3,1024]{2,1,0:T(4,128)S(1)} %shard_map.72.refs_3_), custom_call_target="tpu_custom_call" | custom-call | flops 805306368 | bytes 2293760 | tf_op jit(solution)/shard_map/pallas_call | solution.py:176
  41.6 0.1 collective-permute-done.10.refs_4_
  41.7 1.1 %shard_map.74.refs_0_ = f32[3,4,1024]{2,1,0:T(4,128)S(1)} custom-call(bf16[3,256,1024]{2,1,0:T(8,128)(2,1)S(1)} %get-tuple-element.14.refs_0_, bf16[1,256,1024]{2,1,0:T(8,128)(2,1)S(1)} %get-tuple-element.15.refs_1_, f32[3,1,1024]{2,1,0:T(1,128)S(1)} %get-tuple-element.16.refs_2_, f32[1,1,1024]{2,1,0:T(1,128)S(1)} %get-tuple-element.17.refs_3_, ...), custom_call_target="tpu_custom_call" | custom-call | flops 805306368 | bytes 2293760 | tf_op jit(solution)/shard_map/pallas_call | solution.py:207
  42.8 1.6 %collective-permute-start.11 = (f32[3,4,1024]{2,1,0:T(4,128)S(1)}, f32[3,4,1024]{2,1,0:T(4,128)S(1)}, u32[]{:S(2)}, u32[]{:S(2)}) collective-permute-start(f32[3,4,1024]{2,1,0:T(4,128)S(1)} %shard_map.74.refs_0_), channel_id=1, source_target_pairs={{0,2},{1,3},{2,0},{3,1},{4,6},{5,7},{6,4},{7,5},{8,10},{9,11},{10,... | collective-permute-start | bytes 147464 | tf_op jit(solution)/shard_map/ppermute | solution.py:269
  44.5 0.4 collective-permute-start.12
  44.9 2.3 %collective-permute-start.13 = (f32[3,4,1024]{2,1,0:T(4,128)S(1)}, f32[3,4,1024]{2,1,0:T(4,128)S(1)}, u32[]{:S(2)}, u32[]{:S(2)}) collective-permute-start(f32[3,4,1024]{2,1,0:T(4,128)S(1)} %shard_map.74.refs_0_), channel_id=1, source_target_pairs={{0,3},{1,0},{2,1},{3,2},{4,7},{5,4},{6,5},{7,6},{8,11},{9,8},{10,9... | collective-permute-start | bytes 147464 | tf_op jit(solution)/shard_map/ppermute | solution.py:269
  47.2 0.2 collective-permute-done.11.refs_1_
  47.4 1.5 %collective-permute-done.12.refs_2_ = f32[3,4,1024]{2,1,0:T(4,128)S(1)} collective-permute-done((f32[3,4,1024]{2,1,0:T(4,128)S(1)}, f32[3,4,1024]{2,1,0:T(4,128)S(1)}, u32[]{:S(2)}, u32[]{:S(2)}) %collective-permute-start.12) | collective-permute-done | bytes 49184 | tf_op jit(solution)/shard_map/ppermute | solution.py:269
  48.9 0.1 shard_map.75
  49.0 1.4 %collective-permute-start.14 = (f32[32,128]{1,0:T(8,128)S(1)}, f32[32,128]{1,0:T(8,128)S(1)}, u32[]{:S(2)}, u32[]{:S(2)}) collective-permute-start(f32[32,128]{1,0:T(8,128)S(1)} %get-tuple-element.21), channel_id=1, source_target_pairs={{0,4},{4,0},{1,5},{5,1},{2,6},{6,2},{3,7},{7,3},{8,12},{12,8},{9,1... | collective-permute-start | bytes 49160 | tf_op jit(solution)/shard_map/ppermute | solution.py:269
  50.4 0.8 %collective-permute-done.14 = f32[32,128]{1,0:T(8,128)S(1)} collective-permute-done((f32[32,128]{1,0:T(8,128)S(1)}, f32[32,128]{1,0:T(8,128)S(1)}, u32[]{:S(2)}, u32[]{:S(2)}) %collective-permute-start.14) | collective-permute-done | bytes 16416 | tf_op jit(solution)/shard_map/ppermute | solution.py:269
  51.3 12.3 %all_to_all.16 = f32[32,1,128]{2,1,0:T(1,128)S(1)} all-to-all(f32[32,1,128]{2,1,0:T(1,128)S(1)} %bitcast.11), channel_id=1, replica_groups=mesh['z'=8,'x'=4,'c'=2,'y'=4] {'z','x'}, dimensions={0} | all-to-all | bytes 32768 | tf_op jit(solution)/shard_map/all_to_all | solution.py:298
  63.5 0.7 %shard_map.76 = (f32[1,1024]{1,0:T(1,128)}, f32[1,1024]{1,0:T(1,128)}, f32[1,3]{1,0:T(1,128)}) custom-call(f32[1,1024]{1,0:T(1,128)S(1)} %get-tuple-element.20.own_ref, f32[32,128]{1,0:T(8,128)S(1)} %bitcast.9), custom_call_target="tpu_custom_call" | custom-call | tf_op jit(solution)/shard_map/pallas_call | solution.py:259
  (18 shorter events, 0.1 us)
Async XLA Ops:
  0.6 28.6 %copy-start = (bf16[1024,256]{1,0:T(8,128)(2,1)S(1)}, bf16[1024,256]{1,0:T(8,128)(2,1)}, u32[]{:S(2)}) copy-start(bf16[1024,256]{1,0:T(8,128)(2,1)} %points_hbm.1) | copy-start | bytes 1572868
  0.6 13.9 %collective-permute-start = (bf16[1024,256]{1,0:T(8,128)(2,1)}, bf16[1024,256]{1,0:T(8,128)(2,1)S(1)}, u32[]{:S(2)}, u32[]{:S(2)}) collective-permute-start(bf16[1024,256]{1,0:T(8,128)(2,1)} %points_hbm.1), channel_id=1, source_target_pairs={{0,1},{1,2},{2,3},{3,0},{4,5},{5,6},{6,7},{7,4},{8,9},{9,10},{10,1... | collective-permute-start | bytes 1572872 | tf_op jit(solution)/shard_map/ppermute | solution.py:269
  2.8 12.9 %collective-permute-start.1 = (bf16[1024,256]{1,0:T(8,128)(2,1)}, bf16[1024,256]{1,0:T(8,128)(2,1)S(1)}, u32[]{:S(2)}, u32[]{:S(2)}) collective-permute-start(bf16[1024,256]{1,0:T(8,128)(2,1)} %points_hbm.1), channel_id=1, source_target_pairs={{0,3},{1,0},{2,1},{3,2},{4,7},{5,4},{6,5},{7,6},{8,11},{9,8},{10,9... | collective-permute-start | bytes 1572872 | tf_op jit(solution)/shard_map/ppermute | solution.py:269
  6.4 16.6 %all-to-all-start = ((bf16[8,48,256]{2,1,0:T(8,128)(2,1)}), bf16[8,48,256]{2,1,0:T(8,128)(2,1)S(1)}, u32[]{:S(2)}, u32[]{:S(2)}) async-start(bf16[8,48,256]{2,1,0:T(8,128)(2,1)} %shard_map.69), calls=%async_computation | async-start | bytes 393216 | tf_op jit(solution)/shard_map/all_to_all | solution.py:280
  14.6 20.1 %collective-permute-start.2 = (bf16[512,256]{1,0:T(8,128)(2,1)S(1)}, bf16[512,256]{1,0:T(8,128)(2,1)S(1)}, u32[]{:S(2)}, u32[]{:S(2)}) collective-permute-start(bf16[512,256]{1,0:T(8,128)(2,1)S(1)} %slice.8), channel_id=1, source_target_pairs={{0,1},{1,2},{2,3},{3,0},{4,5},{5,6},{6,7},{7,4},{8,9},{9,10},{10,1... | collective-permute-start | bytes 786440 | tf_op jit(solution)/shard_map/ppermute | solution.py:269
  15.8 19.2 %collective-permute-start.3 = (bf16[512,256]{1,0:T(8,128)(2,1)S(1)}, bf16[512,256]{1,0:T(8,128)(2,1)S(1)}, u32[]{:S(2)}, u32[]{:S(2)}) collective-permute-start(bf16[512,256]{1,0:T(8,128)(2,1)S(1)} %slice.9), channel_id=1, source_target_pairs={{0,3},{1,0},{2,1},{3,2},{4,7},{5,4},{6,5},{7,6},{8,11},{9,8},{10,9... | collective-permute-start | bytes 786440 | tf_op jit(solution)/shard_map/ppermute | solution.py:269
  22.9 7.7 %collective-permute-start.5 = (bf16[8,48,256]{2,1,0:T(8,128)(2,1)S(1)}, bf16[8,48,256]{2,1,0:T(8,128)(2,1)S(1)}, u32[]{:S(2)}, u32[]{:S(2)}) collective-permute-start(bf16[8,48,256]{2,1,0:T(8,128)(2,1)S(1)} %all-to-all-done.refs_1_.refs_2_), channel_id=1, source_target_pairs={{0,8},{8,16},{16,24},{24,0},{1,9},{9,17},{17,25},{25,1},{2,10},{10... | collective-permute-start | bytes 589832 | tf_op jit(solution)/shard_map/ppermute | solution.py:269
  24.1 8.1 %collective-permute-start.7 = (bf16[8,48,256]{2,1,0:T(8,128)(2,1)S(1)}, bf16[8,48,256]{2,1,0:T(8,128)(2,1)S(1)}, u32[]{:S(2)}, u32[]{:S(2)}) collective-permute-start(bf16[8,48,256]{2,1,0:T(8,128)(2,1)S(1)} %all-to-all-done.refs_1_.refs_2_), channel_id=1, source_target_pairs={{0,24},{8,0},{16,8},{24,16},{1,25},{9,1},{17,9},{25,17},{2,26},{10... | collective-permute-start | bytes 589832 | tf_op jit(solution)/shard_map/ppermute | solution.py:269
  25.6 11.7 %collective-permute-start.9 = (bf16[8,48,256]{2,1,0:T(8,128)(2,1)S(1)}, bf16[8,48,256]{2,1,0:T(8,128)(2,1)S(1)}, u32[]{:S(2)}, u32[]{:S(2)}) collective-permute-start(bf16[8,48,256]{2,1,0:T(8,128)(2,1)S(1)} %all-to-all-done.refs_1_.refs_2_), channel_id=1, source_target_pairs={{0,4},{4,0},{1,5},{5,1},{2,6},{6,2},{3,7},{7,3},{8,12},{12,8},{9,1... | collective-permute-start | bytes 589832 | tf_op jit(solution)/shard_map/ppermute | solution.py:269
  30.6 9.6 %collective-permute-start.4 = (bf16[8,48,256]{2,1,0:T(8,128)(2,1)S(1)}, bf16[8,48,256]{2,1,0:T(8,128)(2,1)S(1)}, u32[]{:S(2)}, u32[]{:S(2)}) collective-permute-start(bf16[8,48,256]{2,1,0:T(8,128)(2,1)S(1)} %all-to-all-done.refs_1_.refs_2_), channel_id=1, source_target_pairs={{0,16},{8,24},{16,0},{24,8},{1,17},{9,25},{17,1},{25,9},{2,18},{10... | collective-permute-start | bytes 589832 | tf_op jit(solution)/shard_map/ppermute | solution.py:269
  32.2 5.1 %collective-permute-start.6 = (bf16[8,48,256]{2,1,0:T(8,128)(2,1)S(1)}, bf16[8,48,256]{2,1,0:T(8,128)(2,1)S(1)}, u32[]{:S(2)}, u32[]{:S(2)}) collective-permute-start(bf16[8,48,256]{2,1,0:T(8,128)(2,1)S(1)} %collective-permute-done.5.refs_3_), channel_id=1, source_target_pairs={{0,4},{4,0},{1,5},{5,1},{2,6},{6,2},{3,7},{7,3},{8,12},{12,8},{9,1... | collective-permute-start | bytes 589832 | tf_op jit(solution)/shard_map/ppermute | solution.py:269
  34.7 2.7 %collective-permute-start.8 = (bf16[8,48,256]{2,1,0:T(8,128)(2,1)S(1)}, bf16[8,48,256]{2,1,0:T(8,128)(2,1)S(1)}, u32[]{:S(2)}, u32[]{:S(2)}) collective-permute-start(bf16[8,48,256]{2,1,0:T(8,128)(2,1)S(1)} %collective-permute-done.7.refs_4_), channel_id=1, source_target_pairs={{0,4},{4,0},{1,5},{5,1},{2,6},{6,2},{3,7},{7,3},{8,12},{12,8},{9,1... | collective-permute-start | bytes 589832 | tf_op jit(solution)/shard_map/ppermute | solution.py:269
  40.2 1.6 %copy-start.1 = (f32[1024]{0:T(1024)S(1)}, f32[1024]{0:T(1024)}, u32[]{:S(2)}) copy-start(f32[1024]{0:T(1024)} %param.5) | copy-start | bytes 12292
  40.2 1.5 %collective-permute-start.10 = (bf16[8,48,256]{2,1,0:T(8,128)(2,1)S(1)}, bf16[8,48,256]{2,1,0:T(8,128)(2,1)S(1)}, u32[]{:S(2)}, u32[]{:S(2)}) collective-permute-start(bf16[8,48,256]{2,1,0:T(8,128)(2,1)S(1)} %collective-permute-done.4.refs_2_), channel_id=1, source_target_pairs={{0,4},{4,0},{1,5},{5,1},{2,6},{6,2},{3,7},{7,3},{8,12},{12,8},{9,1... | collective-permute-start | bytes 589832 | tf_op jit(solution)/shard_map/ppermute | solution.py:269
  42.8 4.5 %collective-permute-start.11 = (f32[3,4,1024]{2,1,0:T(4,128)S(1)}, f32[3,4,1024]{2,1,0:T(4,128)S(1)}, u32[]{:S(2)}, u32[]{:S(2)}) collective-permute-start(f32[3,4,1024]{2,1,0:T(4,128)S(1)} %shard_map.74.refs_0_), channel_id=1, source_target_pairs={{0,2},{1,3},{2,0},{3,1},{4,6},{5,7},{6,4},{7,5},{8,10},{9,11},{10,... | collective-permute-start | bytes 147464 | tf_op jit(solution)/shard_map/ppermute | solution.py:269
  44.5 4.4 %collective-permute-start.12 = (f32[3,4,1024]{2,1,0:T(4,128)S(1)}, f32[3,4,1024]{2,1,0:T(4,128)S(1)}, u32[]{:S(2)}, u32[]{:S(2)}) collective-permute-start(f32[3,4,1024]{2,1,0:T(4,128)S(1)} %shard_map.74.refs_0_), channel_id=1, source_target_pairs={{0,1},{1,2},{2,3},{3,0},{4,5},{5,6},{6,7},{7,4},{8,9},{9,10},{10,1... | collective-permute-start | bytes 147464 | tf_op jit(solution)/shard_map/ppermute | solution.py:269
  44.9 4.0 %collective-permute-start.13 = (f32[3,4,1024]{2,1,0:T(4,128)S(1)}, f32[3,4,1024]{2,1,0:T(4,128)S(1)}, u32[]{:S(2)}, u32[]{:S(2)}) collective-permute-start(f32[3,4,1024]{2,1,0:T(4,128)S(1)} %shard_map.74.refs_0_), channel_id=1, source_target_pairs={{0,3},{1,0},{2,1},{3,2},{4,7},{5,4},{6,5},{7,6},{8,11},{9,8},{10,9... | collective-permute-start | bytes 147464 | tf_op jit(solution)/shard_map/ppermute | solution.py:269
  49.0 2.3 %collective-permute-start.14 = (f32[32,128]{1,0:T(8,128)S(1)}, f32[32,128]{1,0:T(8,128)S(1)}, u32[]{:S(2)}, u32[]{:S(2)}) collective-permute-start(f32[32,128]{1,0:T(8,128)S(1)} %get-tuple-element.21), channel_id=1, source_target_pairs={{0,4},{4,0},{1,5},{5,1},{2,6},{6,2},{3,7},{7,3},{8,12},{12,8},{9,1... | collective-permute-start | bytes 49160 | tf_op jit(solution)/shard_map/ppermute | solution.py:269
